TPU v7x, 32 devices: a whole 2x2x4 slice. The times are simulated.
32 devices in a mesh: section: 2 (over x), fsdp: 16 (over z, y, core).
Axes of the slice: x: 2, y: 2, z: 4, core: 2. Of those that a mesh axis runs over, the one named last changes fastest.
Arguments:
- section_input: bfloat16 [2, 4096, 4096], P('section', 'fsdp'), may hold values from -6 to 6
- segment_ids: int32 [2, 4096], P('section', 'fsdp'), may hold values from 0 to 2, never falling along the last dimension, each value on 1 to 3072 neighbouring positions
- query_weight: bfloat16 [2, 4096, 2048], P('section', 'fsdp'), as said below
- keyval_weight: bfloat16 [2, 4096, 512], P('section', 'fsdp'), as said below
- out_weight: bfloat16 [2, 2048, 4096], P('section', None, 'fsdp'), may hold values from -0.125 to 0.125
Outputs:
- passed: bfloat16 [2, 4096, 4096], P('section', 'fsdp')
Inputs may be any that keep to these rules, and one draw needn't show every extreme that they name: `query_weight`: query projection weights. `keyval_weight`: key and value projection weights.
All inputs are finite; a program needn't handle non-finite values.
Results may differ from a plain program's by a relative error of at most 0.012.
The roundings to bfloat16 on the way count: a program that leaves them out, or rounds other values in their place, can miss the bound.
Values may be sent and summed in bfloat16 or wider, within the bound.
No kernel may reach another device: no remote copies, remote signals or barrier semaphores. Data moves between devices by JAX's collectives and lax.ppermute only.
A program may use at most 192 MiB of HBM per device.

v0:
```python
import jax
import jax.numpy as jnp
from jax import lax
from jax.experimental import pallas as pl
from jax.experimental.pallas import tpu as pltpu
from jax.sharding import PartitionSpec as P

QUERY_HEADS = 32
KEY_HEADS = 4
HEAD_SIZE = 64
LOOKBACK_SPAN = 2048
GROUP = QUERY_HEADS // KEY_HEADS
GROUP_WIDTH = GROUP * HEAD_SIZE
TILE = 256
MASKED = -1e30


def normed(values):
    widened = values.astype(jnp.float32)
    scaled = widened * lax.rsqrt(jnp.mean(widened * widened, axis=-1, keepdims=True) + 1e-05)
    return scaled.astype(jnp.bfloat16)


def swap_cores(value):
    count = lax.axis_size("fsdp")
    return lax.ppermute(value, "fsdp", [(i, i ^ 1) for i in range(count)])


def gathered(value):
    count = lax.axis_size("fsdp")
    groups = [list(range(core, count, 2)) for core in range(2)]
    return lax.all_gather(value, "fsdp", axis=0, tiled=False, axis_index_groups=groups)


def swap_chips(value):
    count = lax.axis_size("fsdp")
    return lax.ppermute(value, "fsdp", [(i, i ^ 2) for i in range(count)])


def two_chips_on(value):
    count = lax.axis_size("fsdp")
    return lax.ppermute(value, "fsdp", [(i, i + 4) for i in range(count - 4)])


def to_next_section(value):
    count = lax.axis_size("section")
    return lax.ppermute(value, "section", [(i, (i + 1) % count) for i in range(count)])


def out_kernel(rows_ref, weight_ref, add_ref, out_ref):
    total = add_ref[...].astype(jnp.float32) + jnp.dot(
        rows_ref[...], weight_ref[0], preferred_element_type=jnp.float32
    )
    out_ref[...] = total.astype(out_ref.dtype)


def out_columns(rows, weights, add):
    chips, depth, columns = weights.shape
    count = rows.shape[0]
    return pl.pallas_call(
        out_kernel,
        grid=(chips,),
        in_specs=[
            pl.BlockSpec((count, depth), lambda i: (0, 0)),
            pl.BlockSpec((1, depth, columns), lambda i: (i, 0, 0)),
            pl.BlockSpec((count, columns), lambda i: (0, i)),
        ],
        out_specs=pl.BlockSpec((count, columns), lambda i: (0, i)),
        out_shape=jax.ShapeDtypeStruct(add.shape, add.dtype),
        compiler_params=pltpu.CompilerParams(vmem_limit_bytes=40 * 1024 * 1024),
        cost_estimate=pl.CostEstimate(
            flops=2 * count * depth * chips * columns, bytes_accessed=12 * 1024 * 1024, transcendentals=0
        ),
    )(rows, weights, add)


def attention_kernel(lo_ref, q_ref, kt_ref, v_ref, out_ref, score_ref):
    tile = pl.program_id(0)
    start = pl.multiple_of(tile * TILE, TILE)
    span = LOOKBACK_SPAN + TILE
    lo = lo_ref[...] - start
    lane = lax.broadcasted_iota(jnp.int32, (TILE, 128), 1)
    row = lax.broadcasted_iota(jnp.int32, (TILE, 128), 0)
    blocks = span // TILE

    def scores_of(pair, parity):
        q = q_ref[:, pair * 128:(pair + 1) * 128]
        peak = jnp.full((TILE, 128), MASKED, jnp.float32)
        for block in range(blocks):
            first = pl.multiple_of(start + block * TILE, TILE)
            found = jnp.dot(q, kt_ref[parity, :, pl.ds(first, TILE)], preferred_element_type=jnp.float32)
            for part in range(TILE // 128):
                at = block * TILE + part * 128
                visible = lane + at >= lo
                if at >= LOOKBACK_SPAN:
                    visible = visible & (lane + (at - LOOKBACK_SPAN) <= row)
                kept = jnp.where(visible, found[:, part * 128:(part + 1) * 128], MASKED)
                peak = jnp.maximum(peak, kept)
                score_ref[parity, :, at:at + 128] = kept
        return jnp.max(peak, axis=1, keepdims=True)

    def mixed_of(parity, peak):
        total = jnp.zeros((TILE, 128), jnp.float32)
        mixed = jnp.zeros((TILE, 128), jnp.float32)
        for block in range(blocks):
            first = pl.multiple_of(start + block * TILE, TILE)
            weights = jnp.exp(score_ref[parity, :, block * TILE:(block + 1) * TILE] - peak)
            for part in range(TILE // 128):
                total = total + weights[:, part * 128:(part + 1) * 128]
            mixed = mixed + jnp.dot(
                weights.astype(jnp.bfloat16), v_ref[parity, pl.ds(first, TILE), :],
                preferred_element_type=jnp.float32,
            )
        return mixed * (1.0 / jnp.sum(total, axis=1, keepdims=True))

    pairs = q_ref.shape[1] // 128
    for pair in range(pairs):
        peaks = [scores_of(pair, parity) for parity in range(2)]
        parts = [mixed_of(parity, peaks[parity]) for parity in range(2)]
        out_ref[:, pair * 128:(pair + 1) * 128] = (parts[0] + parts[1]).astype(out_ref.dtype)


def attention(lo, queries, keys_t, values):
    rows = queries.shape[0]
    window = keys_t.shape[2]
    span = LOOKBACK_SPAN + TILE
    flops = 4 * rows * span * GROUP * 128
    return pl.pallas_call(
        attention_kernel,
        grid=(rows // TILE,),
        in_specs=[
            pl.BlockSpec((TILE, 128), lambda t: (t, 0)),
            pl.BlockSpec((TILE, GROUP_WIDTH), lambda t: (t, 0)),
            pl.BlockSpec((2, 128, window), lambda t: (0, 0, 0)),
            pl.BlockSpec((2, window, 128), lambda t: (0, 0, 0)),
        ],
        out_specs=pl.BlockSpec((TILE, GROUP_WIDTH), lambda t: (t, 0)),
        out_shape=jax.ShapeDtypeStruct((rows, GROUP_WIDTH), jnp.bfloat16),
        scratch_shapes=[pltpu.VMEM((2, TILE, span), jnp.float32)],
        compiler_params=pltpu.CompilerParams(vmem_limit_bytes=40 * 1024 * 1024),
        cost_estimate=pl.CostEstimate(flops=flops, bytes_accessed=4 * 1024 * 1024, transcendentals=rows * span * GROUP),
    )(lo, queries, keys_t, values)


def body(section_input, segment_ids, query_weight, keyval_weight, out_weight):
    hidden, segments = section_input[0], segment_ids[0]
    rows, width = hidden.shape
    device = lax.axis_index("fsdp")
    chips = lax.axis_size("fsdp") // 2
    chip, core = device // 2, device % 2

    def in_order(own, other, axis=0):
        first = jnp.where(core == 0, own, other)
        return jnp.concatenate([first, jnp.where(core == 0, other, own)], axis=axis)

    def own_features(value):
        parts = value.reshape(rows, chips, 2, -1)
        kept = lax.dynamic_index_in_dim(parts, core, 2, keepdims=False).reshape(rows, -1)
        sent = lax.dynamic_index_in_dim(parts, 1 - core, 2, keepdims=False).reshape(rows, -1)
        return in_order(kept, swap_cores(sent))

    weights = gathered(jnp.concatenate([keyval_weight[0], query_weight[0]], axis=1))
    weights = weights.reshape(chips * rows, -1)
    out_shard = to_next_section(out_weight[0])
    chip_rows = own_features(normed(hidden))
    hidden_before = own_features(to_next_section(hidden))
    key_width = keyval_weight.shape[2]

    def projected(first, count):
        return jnp.dot(chip_rows, weights[:, first:first + count], preferred_element_type=jnp.float32)

    def of_core(value, which):
        parts = value.reshape(2 * rows, -1, 2, HEAD_SIZE)
        return lax.dynamic_index_in_dim(parts, which, 2, keepdims=False).reshape(2 * rows, -1)

    partial = projected(0, key_width)
    marks = jnp.zeros((8, rows), jnp.float32).at[0].set((segments + 1).astype(jnp.float32))
    received = swap_cores(jnp.concatenate([of_core(partial, 1 - core), marks], axis=0))
    keyvals = (of_core(partial, core) + received[: 2 * rows]).astype(jnp.bfloat16)
    chip_marks = in_order(marks[:1], received[2 * rows:2 * rows + 1]).astype(jnp.bfloat16)
    chip_marks = jnp.concatenate([chip_marks, jnp.zeros((14, rows), jnp.bfloat16)], axis=0)
    parcel = jnp.concatenate([keyvals, chip_marks], axis=0)
    back_two = two_chips_on(parcel)
    back_four = two_chips_on(back_two)
    even = chip % 2 == 0
    swapped = swap_chips(jnp.concatenate([jnp.where(even, parcel, back_four), back_two], axis=0))
    length = parcel.shape[0]
    crossed = [swapped[:length], swapped[length:]]
    parcels = [
        back_four, jnp.where(even, crossed[0], crossed[1]), back_two, jnp.where(even, crossed[1], crossed[0]), parcel
    ]
    window = jnp.concatenate([item[: 2 * rows] for item in parcels], axis=0)
    window_marks = jnp.concatenate([item[2 * rows:2 * rows + 2].reshape(-1) for item in parcels]).astype(jnp.int32)
    own_marks = window_marks[-2 * rows:]
    earlier = jnp.sum((window_marks[None, :] < own_marks[:, None]).astype(jnp.int32), axis=1)
    lowest = jnp.maximum(earlier, jnp.arange(1, 2 * rows + 1, dtype=jnp.int32))
    lowest = jnp.broadcast_to(lowest[:, None], (2 * rows, 128))

    out_weights = gathered(out_shard)
    attended_rows = []
    for g in range(2):
        partial = projected(key_width + 2 * g * GROUP_WIDTH, 2 * GROUP_WIDTH)
        kept = lax.dynamic_slice(partial, (0, core * GROUP_WIDTH), (2 * rows, GROUP_WIDTH))
        sent = lax.dynamic_slice(partial, (0, (1 - core) * GROUP_WIDTH), (2 * rows, GROUP_WIDTH))
        queries = (kept + swap_cores(sent)).astype(jnp.bfloat16) * jnp.bfloat16(HEAD_SIZE ** -0.5)
        keys = window[:, g * HEAD_SIZE:(g + 1) * HEAD_SIZE]
        values = window[:, (2 + g) * HEAD_SIZE:(3 + g) * HEAD_SIZE]
        blank = jnp.zeros_like(keys)
        keys_t = jnp.stack(
            [jnp.concatenate([keys, blank], axis=1).T, jnp.concatenate([blank, keys], axis=1).T]
        )
        wide = jnp.stack(
            [jnp.concatenate([values, blank], axis=1), jnp.concatenate([blank, values], axis=1)]
        )
        attended = to_next_section(attention(lowest, queries, keys_t, wide))
        attended_rows.append(in_order(attended, swap_cores(attended), axis=1))
    attended_rows = jnp.concatenate(attended_rows, axis=1)

    made = out_columns(attended_rows, out_weights, hidden_before)
    kept = lax.dynamic_slice(made, (core * rows, 0), (rows, width // 2)).reshape(rows, chips, 1, -1)
    sent = lax.dynamic_slice(made, ((1 - core) * rows, 0), (rows, width // 2))
    other = swap_cores(sent).reshape(rows, chips, 1, -1)
    return in_order(kept, other, axis=2).reshape(1, rows, width)


def solution(mesh):
    return jax.shard_map(
        body,
        mesh=mesh,
        in_specs=(
            P("section", "fsdp", None),
            P("section", "fsdp"),
            P("section", "fsdp", None),
            P("section", "fsdp", None),
            P("section", None, "fsdp"),
        ),
        out_specs=P("section", "fsdp", None),
        check_vma=False,
    )
```

profile of v0, /device:TPU:0, one launch (start us, length us, event | category | flops | bytes accessed | tf_op | source)
XLA Modules:
  0.0 336.2 jit_solution(15000819432787138707)
XLA Ops:
  9.2 3.0 collective-permute-start.11
  12.8 5.2 %reshape.191 = f32[256,8,2,256]{3,2,1,0:T(2,128)} reshape(bf16[1,256,4096]{2,1,0:T(8,128)(2,1)S(1)} %copy-done.4) | data formatting | bytes 6291456 | tf_op jit(solution)/shard_map/convert_element_type | solution.py:19
  17.9 2.9 fusion.4
  22.4 14.1 %collective-permute-done.11 = bf16[2048,256]{1,0:T(8,128)(2,1)} collective-permute-done((bf16[2048,256]{1,0:T(8,128)(2,1)}, bf16[2048,256]{1,0:T(8,128)(2,1)}, u32[]{:S(2)}, u32[]{:S(2)}) %collective-permute-start.11) | collective-permute-done | bytes 1048608 | tf_op jit(solution)/shard_map/ppermute | solution.py:47
  37.9 3.0 broadcast_select_fusion.5
  41.0 39.6 %collective-permute-done.12 = bf16[256,4096]{1,0:T(8,128)(2,1)} collective-permute-done((bf16[256,4096]{1,0:T(8,128)(2,1)S(1)}, bf16[256,4096]{1,0:T(8,128)(2,1)}, u32[]{:S(2)}, u32[]{:S(2)}) %collective-permute-start.12) | collective-permute-done | bytes 2097184 | tf_op jit(solution)/shard_map/ppermute | solution.py:47
  80.6 3.5 %reshape.187 = bf16[256,8,2,256]{3,2,1,0:T(2,128)(2,1)S(1)} reshape(bf16[256,4096]{1,0:T(8,128)(2,1)} %collective-permute-done.12) | data formatting | bytes 4194304 | tf_op jit(solution)/shard_map/reshape | solution.py:157
  84.1 13.6 %dynamic-slice_reduce_fusion.1 = (bf16[256,8,256]{2,1,0:T(8,128)(2,1)}, bf16[256,8,256]{2,1,0:T(8,128)(2,1)S(1)}) fusion(bf16[256,8,2,256]{3,2,1,0:T(2,128)(2,1)S(1)} %reshape.187, s32[]{:T(128)S(6)} %select_n.144, s32[]{:T(128)S(6)} %select_n.145), kind=kLoop, calls=%fused_computation.15 | loop fusion | bytes 4194312 | tf_op jit(solution)/shard_map/jit(dynamic_index_in_dim)/dynamic_slice | solution.py:158
  101.7 61.4 %all-gather.5.cloned.1.call-done = bf16[2048,2560]{1,0:T(8,128)(2,1)} async-done(((bf16[256,2560]{1,0:T(8,128)(2,1)}), bf16[2048,2560]{1,0:T(8,128)(2,1)}) %all-gather.5.cloned.1.call-update) | async-done | bytes 10485776 | tf_op jit(solution)/shard_map/all_gather | solution.py:32
  163.1 2.9 fusion.5
  167.9 4.5 %fusion = f32[512,1024]{1,0:T(8,128)S(1)} fusion(bf16[2048,2560]{1,0:T(8,128)(2,1)} %all-gather.5.cloned.1.call-done, bf16[256,2048]{1,0:T(8,128)(2,1)S(1)} %copy-done.11, bf16[256,2048]{1,0:T(8,128)(2,1)S(1)} %copy-done.9), kind=kOutput, calls=%fused_computation.1 | convolution fusion | flops 2151677952 | bytes 8388608 | tf_op jit(solution)/shard_map/dot_general | solution.py:170
  176.5 4.6 %fusion.2 = f32[512,1024]{1,0:T(8,128)S(1)} fusion(bf16[2048,2560]{1,0:T(8,128)(2,1)} %all-gather.5.cloned.1.call-done, bf16[256,2048]{1,0:T(8,128)(2,1)S(1)} %copy-done.12, bf16[256,2048]{1,0:T(8,128)(2,1)S(1)} %copy-done.9), kind=kOutput, calls=%fused_computation.3 | convolution fusion | flops 2151677952 | bytes 8388608 | tf_op jit(solution)/shard_map/dot_general | solution.py:170
  181.3 7.5 %collective-permute-done.2 = bf16[528,256]{1,0:T(8,128)(2,1)S(1)} collective-permute-done((bf16[528,256]{1,0:T(8,128)(2,1)S(1)}, bf16[528,256]{1,0:T(8,128)(2,1)S(1)}, u32[]{:S(2)}, u32[]{:S(2)}) %collective-permute-start.2) | collective-permute-done | bytes 270368 | tf_op jit(solution)/shard_map/ppermute | solution.py:42
  188.8 9.9 %collective-permute-start.3 = (bf16[528,256]{1,0:T(8,128)(2,1)S(1)}, bf16[528,256]{1,0:T(8,128)(2,1)S(1)}, u32[]{:S(2)}, u32[]{:S(2)}) collective-permute-start(bf16[528,256]{1,0:T(8,128)(2,1)S(1)} %collective-permute-done.2), channel_id=1, source_target_pairs={{0,4},{1,5},{2,6},{3,7},{4,8},{5,9},{6,10},{7,11},{8,12},{9,13},{1... | collective-permute-start | bytes 811016 | tf_op jit(solution)/shard_map/ppermute | solution.py:42
  199.1 11.2 %collective-permute-done.3 = bf16[528,256]{1,0:T(8,128)(2,1)S(1)} collective-permute-done((bf16[528,256]{1,0:T(8,128)(2,1)S(1)}, bf16[528,256]{1,0:T(8,128)(2,1)S(1)}, u32[]{:S(2)}, u32[]{:S(2)}) %collective-permute-start.3) | collective-permute-done | bytes 270368 | tf_op jit(solution)/shard_map/ppermute | solution.py:42
  213.5 9.1 %collective-permute-done.4 = bf16[1056,256]{1,0:T(8,128)(2,1)} collective-permute-done((bf16[1056,256]{1,0:T(8,128)(2,1)}, bf16[1056,256]{1,0:T(8,128)(2,1)}, u32[]{:S(2)}, u32[]{:S(2)}) %collective-permute-start.4) | collective-permute-done | bytes 540704 | tf_op jit(solution)/shard_map/ppermute | solution.py:37
  234.2 16.0 %shard_map.56 = bf16[512,512]{1,0:T(8,128)(2,1)} custom-call(s32[512,128]{1,0:T(8,128)S(1)} %broadcast_in_dim.5.lo_ref, bf16[512,512]{1,0:T(8,128)(2,1)S(1)} %fusion.9.q_ref, bf16[2,128,2560]{2,1,0:T(8,128)(2,1)S(1)} %copy.30.kt_ref, bf16[2,2560,128]{2,1,0:T(8,128)(2,1)S(1)} %pad_maximum_fusion.8.v_ref), custom_call_target="tpu_custom_call" | custom-call | flops 4831838208 | bytes 4194304 | tf_op jit(solution)/shard_map/pallas_call | solution.py:128
  255.5 15.1 %shard_map.55 = bf16[512,512]{1,0:T(8,128)(2,1)S(1)} custom-call(s32[512,128]{1,0:T(8,128)S(1)} %broadcast_in_dim.5.lo_ref, bf16[512,512]{1,0:T(8,128)(2,1)S(1)} %fusion.8.q_ref, bf16[2,128,2560]{2,1,0:T(8,128)(2,1)S(1)} %copy.29.kt_ref, bf16[2,2560,128]{2,1,0:T(8,128)(2,1)S(1)} %pad_maximum_fusion.6.v_ref), custom_call_target="tpu_custom_call" | custom-call | flops 4831838208 | bytes 4194304 | tf_op jit(solution)/shard_map/pallas_call | solution.py:128
  272.7 8.0 %collective-permute-done.6 = bf16[512,512]{1,0:T(8,128)(2,1)S(1)} collective-permute-done((bf16[512,512]{1,0:T(8,128)(2,1)S(1)}, bf16[512,512]{1,0:T(8,128)(2,1)S(1)}, u32[]{:S(2)}, u32[]{:S(2)}) %collective-permute-start.6) | collective-permute-done | bytes 524320 | tf_op jit(solution)/shard_map/ppermute | solution.py:47
  285.3 20.3 %all-gather.7.cloned.1.call-done = bf16[16384,256]{1,0:T(8,128)(2,1)} async-done(((bf16[2048,256]{1,0:T(8,128)(2,1)}), bf16[16384,256]{1,0:T(8,128)(2,1)}) %all-gather.7.cloned.1.call-update) | async-done | bytes 8388624 | tf_op jit(solution)/shard_map/all_gather | solution.py:32
  308.7 9.1 %shard_map.57 = bf16[512,2048]{1,0:T(8,128)(2,1)S(1)} custom-call(bf16[512,2048]{1,0:T(8,128)(2,1)S(1)} %copy-done.1, bf16[8,2048,256]{2,1,0:T(8,128)(2,1)} %bitcast.93, bf16[512,2048]{1,0:T(8,128)(2,1)S(1)} %copy-done), custom_call_target="tpu_custom_call" | custom-call | flops 4294967296 | bytes 12582912 | tf_op jit(solution)/shard_map/pallas_call | solution.py:60
  318.9 2.8 collective-permute-done.14
  323.1 3.2 copy.33
  326.3 2.8 reshape.190
  (131 shorter events, 48.4 us)
Async XLA Ops:
  6.5 5.6 %copy-start.4 = (bf16[1,256,4096]{2,1,0:T(8,128)(2,1)S(1)}, bf16[1,256,4096]{2,1,0:T(8,128)(2,1)}, u32[]{:S(2)}) copy-start(bf16[1,256,4096]{2,1,0:T(8,128)(2,1)} %param.7) | copy-start | bytes 6291460
  6.5 156.6 %all-gather.5.cloned.1.call-start = ((), (), s32[]{:S(2)}) async-start(), calls=%async_computation | async-start | bytes 11796480 | tf_op jit(solution)/shard_map/all_gather | solution.py:32
  9.1 296.4 %all-gather.7.cloned.1.call-start = ((), (), s32[]{:S(2)}) async-start(), calls=%async_computation.1 | async-start | bytes 9437184 | tf_op jit(solution)/shard_map/all_gather | solution.py:32
  9.2 27.3 %collective-permute-start.11 = (bf16[2048,256]{1,0:T(8,128)(2,1)}, bf16[2048,256]{1,0:T(8,128)(2,1)}, u32[]{:S(2)}, u32[]{:S(2)}) collective-permute-start(bf16[2048,256]{1,0:T(8,128)(2,1)} %bitcast.18), channel_id=1, source_target_pairs={{0,16},{16,0},{1,17},{17,1},{2,18},{18,2},{3,19},{19,3},{4,20},{20... | collective-permute-start | bytes 3145736 | tf_op jit(solution)/shard_map/ppermute | solution.py:47
  12.2 68.4 %collective-permute-start.12 = (bf16[256,4096]{1,0:T(8,128)(2,1)S(1)}, bf16[256,4096]{1,0:T(8,128)(2,1)}, u32[]{:S(2)}, u32[]{:S(2)}) collective-permute-start(bf16[256,4096]{1,0:T(8,128)(2,1)S(1)} %bitcast.72), channel_id=1, source_target_pairs={{0,16},{16,0},{1,17},{17,1},{2,18},{18,2},{3,19},{19,3},{4,20},{20... | collective-permute-start | bytes 6291464 | tf_op jit(solution)/shard_map/ppermute | solution.py:47
  22.3 15.6 %copy-start.15 = (s32[1,256]{1,0:T(1,128)S(1)}, s32[1,256]{1,0:T(1,128)}, u32[]{:S(2)}) copy-start(s32[1,256]{1,0:T(1,128)} %param.8) | copy-start | bytes 3076
  22.4 15.6 %collective-permute-start = (bf16[256,2048]{1,0:T(8,128)(2,1)}, bf16[256,2048]{1,0:T(8,128)(2,1)}, u32[]{:S(2)}, u32[]{:S(2)}) collective-permute-start(bf16[256,2048]{1,0:T(8,128)(2,1)} %bitcast.35), channel_id=1, source_target_pairs={{0,1},{1,0},{2,3},{3,2},{4,5},{5,4},{6,7},{7,6},{8,9},{9,8},{10,11... | collective-permute-start | bytes 3145736 | tf_op jit(solution)/shard_map/ppermute | solution.py:26
  97.7 65.4 %copy-start.8 = (bf16[256,2048]{1,0:T(8,128)(2,1)S(1)}, bf16[256,2048]{1,0:T(8,128)(2,1)}, u32[]{:S(2)}) copy-start(bf16[256,2048]{1,0:T(8,128)(2,1)} %get-tuple-element.23) | copy-start | bytes 3145732
  97.7 65.4 %copy-start.10 = (bf16[256,2048]{1,0:T(8,128)(2,1)S(1)}, bf16[256,2048]{1,0:T(8,128)(2,1)}, u32[]{:S(2)}) copy-start(bf16[256,2048]{1,0:T(8,128)(2,1)} %get-tuple-element.24) | copy-start | bytes 3145732
  101.7 169.6 %collective-permute-start.13 = (bf16[256,2048]{1,0:T(8,128)(2,1)}, bf16[256,2048]{1,0:T(8,128)(2,1)}, u32[]{:S(2)}, u32[]{:S(2)}) collective-permute-start(bf16[256,2048]{1,0:T(8,128)(2,1)} %bitcast.49), channel_id=1, source_target_pairs={{0,1},{1,0},{2,3},{3,2},{4,5},{5,4},{6,7},{7,6},{8,9},{9,8},{10,11... | collective-permute-start | bytes 3145736 | tf_op jit(solution)/shard_map/ppermute | solution.py:26
  167.2 5.5 %collective-permute-start.1 = (f32[520,256]{1,0:T(8,128)}, f32[520,256]{1,0:T(8,128)}, u32[]{:S(2)}, u32[]{:S(2)}) collective-permute-start(f32[520,256]{1,0:T(8,128)} %select_maximum_fusion), channel_id=1, source_target_pairs={{0,1},{1,0},{2,3},{3,2},{4,5},{5,4},{6,7},{7,6},{8,9},{9,8},{10,11... | collective-permute-start | bytes 1597448 | tf_op jit(solution)/shard_map/ppermute | solution.py:26
  172.5 4.0 %copy-start.12 = (bf16[256,2048]{1,0:T(8,128)(2,1)S(1)}, bf16[256,2048]{1,0:T(8,128)(2,1)}, u32[]{:S(2)}) copy-start(bf16[256,2048]{1,0:T(8,128)(2,1)} %get-tuple-element.24) | copy-start | bytes 3145732
  172.6 26.2 %collective-permute-start.8 = (f32[512,512]{1,0:T(8,128)S(1)}, f32[512,512]{1,0:T(8,128)S(1)}, u32[]{:S(2)}, u32[]{:S(2)}) collective-permute-start(f32[512,512]{1,0:T(8,128)S(1)} %constant_dynamic-slice_fusion.1), channel_id=1, source_target_pairs={{0,1},{1,0},{2,3},{3,2},{4,5},{5,4},{6,7},{7,6},{8,9},{9,8},{10,11... | collective-permute-start | bytes 3145736 | tf_op jit(solution)/shard_map/ppermute | solution.py:26
  174.8 14.0 %collective-permute-start.2 = (bf16[528,256]{1,0:T(8,128)(2,1)S(1)}, bf16[528,256]{1,0:T(8,128)(2,1)S(1)}, u32[]{:S(2)}, u32[]{:S(2)}) collective-permute-start(bf16[528,256]{1,0:T(8,128)(2,1)S(1)} %maximum_maximum_fusion), channel_id=1, source_target_pairs={{0,4},{1,5},{2,6},{3,7},{4,8},{5,9},{6,10},{7,11},{8,12},{9,13},{1... | collective-permute-start | bytes 811016 | tf_op jit(solution)/shard_map/ppermute | solution.py:42
  181.2 31.2 %collective-permute-start.5 = (f32[512,512]{1,0:T(8,128)S(1)}, f32[512,512]{1,0:T(8,128)S(1)}, u32[]{:S(2)}, u32[]{:S(2)}) collective-permute-start(f32[512,512]{1,0:T(8,128)S(1)} %constant_dynamic-slice_fusion.2), channel_id=1, source_target_pairs={{0,1},{1,0},{2,3},{3,2},{4,5},{5,4},{6,7},{7,6},{8,9},{9,8},{10,11... | collective-permute-start | bytes 3145736 | tf_op jit(solution)/shard_map/ppermute | solution.py:26
  188.8 21.4 %collective-permute-start.3 = (bf16[528,256]{1,0:T(8,128)(2,1)S(1)}, bf16[528,256]{1,0:T(8,128)(2,1)S(1)}, u32[]{:S(2)}, u32[]{:S(2)}) collective-permute-start(bf16[528,256]{1,0:T(8,128)(2,1)S(1)} %collective-permute-done.2), channel_id=1, source_target_pairs={{0,4},{1,5},{2,6},{3,7},{4,8},{5,9},{6,10},{7,11},{8,12},{9,13},{1... | collective-permute-start | bytes 811016 | tf_op jit(solution)/shard_map/ppermute | solution.py:42
  211.3 11.3 %collective-permute-start.4 = (bf16[1056,256]{1,0:T(8,128)(2,1)}, bf16[1056,256]{1,0:T(8,128)(2,1)}, u32[]{:S(2)}, u32[]{:S(2)}) collective-permute-start(bf16[1056,256]{1,0:T(8,128)(2,1)} %pad_maximum_fusion.12), channel_id=1, source_target_pairs={{0,2},{1,3},{2,0},{3,1},{4,6},{5,7},{6,4},{7,5},{8,10},{9,11},{10,... | collective-permute-start | bytes 1622024 | tf_op jit(solution)/shard_map/ppermute | solution.py:37
  234.2 17.7 %copy-start.6 = (bf16[2560,64]{1,0:T(8,128)(2,1)S(1)}, bf16[2560,64]{1,0:T(8,128)(2,1)}, u32[]{:S(2)}) copy-start(bf16[2560,64]{1,0:T(8,128)(2,1)} %get-tuple-element.30) | copy-start | bytes 983044
  250.2 21.1 %collective-permute-start.9 = (bf16[512,512]{1,0:T(8,128)(2,1)}, bf16[512,512]{1,0:T(8,128)(2,1)}, u32[]{:S(2)}, u32[]{:S(2)}) collective-permute-start(bf16[512,512]{1,0:T(8,128)(2,1)} %shard_map.56), channel_id=1, source_target_pairs={{0,16},{16,0},{1,17},{17,1},{2,18},{18,2},{3,19},{19,3},{4,20},{20... | collective-permute-start | bytes 1572872 | tf_op jit(solution)/shard_map/ppermute | solution.py:47
  255.5 15.9 %copy-start.5 = (bf16[32,8,8,256]{3,1,2,0:T(8,128)(2,1)S(1)}, bf16[32,8,8,256]{3,1,2,0:T(8,128)(2,1)}, u32[]{:S(2)}) copy-start(bf16[32,8,8,256]{3,1,2,0:T(8,128)(2,1)} %copy.45) | copy-start | bytes 3145732
  270.6 10.1 %collective-permute-start.6 = (bf16[512,512]{1,0:T(8,128)(2,1)S(1)}, bf16[512,512]{1,0:T(8,128)(2,1)S(1)}, u32[]{:S(2)}, u32[]{:S(2)}) collective-permute-start(bf16[512,512]{1,0:T(8,128)(2,1)S(1)} %shard_map.55), channel_id=1, source_target_pairs={{0,16},{16,0},{1,17},{17,1},{2,18},{18,2},{3,19},{19,3},{4,20},{20... | collective-permute-start | bytes 1572872 | tf_op jit(solution)/shard_map/ppermute | solution.py:47
  271.3 11.0 %collective-permute-start.10 = (bf16[512,512]{1,0:T(8,128)(2,1)}, bf16[512,512]{1,0:T(8,128)(2,1)S(1)}, u32[]{:S(2)}, u32[]{:S(2)}) collective-permute-start(bf16[512,512]{1,0:T(8,128)(2,1)} %collective-permute-done.9), channel_id=1, source_target_pairs={{0,1},{1,0},{2,3},{3,2},{4,5},{5,4},{6,7},{7,6},{8,9},{9,8},{10,11... | collective-permute-start | bytes 1572872 | tf_op jit(solution)/shard_map/ppermute | solution.py:26
  280.7 2.8 collective-permute-start.7
  318.9 2.9 collective-permute-start.14
  (11 other events, 20.8 us)
Sparse Core Ops, SparseCore 0:
  9.5 153.5 all-gather.4
  165.2 140.2 all-gather.6
where the time goes:
time: 340 us; the launch traced here: 336 us
  waiting for transfers between devices  174 us (51%)
  local copies, waits for them, and re-layouts  51.3 us (15%)
  Pallas kernels  40.2 us (12%)
  other arithmetic  25.8 us (8%)
  starting transfers between devices  18.5 us (5%)
  between operations  14.2 us (4%)
  matrix products  12 us (4%)
    all_gather x2, waiting for transfers between devices, gathered(): lax.all_gather(value, 'fsdp', axis=0, tiled=False, axis_index_groups=groups)  81.7 us
    ppermute x4, waiting for transfers between devices, to_next_section(): lax.ppermute(value, 'section', [(i, (i + 1) % count) for i in range(count)])  61.8 us
    pallas_call x2, Pallas kernels, attention(): pl.pallas_call(attention_kernel, grid=(rows // TILE,), in_specs=[pl.Block...  31.1 us
    ppermute x2, waiting for transfers between devices, two_chips_on(): return lax.ppermute(value, 'fsdp', [(i, i + 4) for i in range(count - 4)])  18.7 us
    unnamed x56, local copies, waits for them, and re-layouts  14.1 us
    dynamic_slice x2, local copies, waits for them, and re-layouts, own_features(): lax.dynamic_index_in_dim(parts, core, 2, keepdims=False).reshape(rows, -1)  13.7 us
    dot_general x3, matrix products, projected(): jnp.dot(chip_rows, weights[:, first:first + count], preferred_element_typ...  12 us
    ppermute x2, starting transfers between devices, two_chips_on(): return lax.ppermute(value, 'fsdp', [(i, i + 4) for i in range(count - 4)])  11.6 us
  transfers between devices with their start and end apart: 17, of which 9 were waited for; matrix products, arithmetic and copies ran while one was open for 22% of the time, Pallas kernels for 9%

commit v1 on v0

v1 whole, which is shorter than its diff:
```python
import functools

import jax
import jax.numpy as jnp
from jax import lax
from jax.experimental import pallas as pl
from jax.experimental.pallas import tpu as pltpu
from jax.sharding import PartitionSpec as P

QUERY_HEADS = 32
KEY_HEADS = 4
HEAD_SIZE = 64
LOOKBACK_SPAN = 2048
GROUP = QUERY_HEADS // KEY_HEADS
GROUP_WIDTH = GROUP * HEAD_SIZE
TILE = 256
MASKED = -1e30
MARK_ROWS = 16


def ring_order(chips):
    return list(range(0, chips, 2)) + list(range(chips - 1, 0, -2))


def swap_cores(value):
    count = lax.axis_size("fsdp")
    return lax.ppermute(value, "fsdp", [(i, i ^ 1) for i in range(count)])


def swap_chips(value):
    count = lax.axis_size("fsdp")
    return lax.ppermute(value, "fsdp", [(i, i ^ 2) for i in range(count)])


def two_chips_on(value):
    count = lax.axis_size("fsdp")
    return lax.ppermute(value, "fsdp", [(i, i + 4) for i in range(count - 4)])


def to_next_section(value):
    count = lax.axis_size("section")
    return lax.ppermute(value, "section", [(i, (i + 1) % count) for i in range(count)])


def along_ring(value, step):
    chips = lax.axis_size("fsdp") // 2
    order = ring_order(chips)
    pairs = []
    for place in range(chips):
        target = order[(place + step) % chips]
        pairs += [(2 * order[place] + core, 2 * target + core) for core in range(2)]
    return lax.ppermute(value, "fsdp", pairs)


def run(kernel, outs, scalars, arrays, waits=(), aliases=None, scratch=()):
    whole = pl.BlockSpec(memory_space=pltpu.VMEM)
    taken = 1 + len(arrays)

    def only(*refs):
        kernel(*refs[:taken], *refs[taken + len(waits):])

    return pl.pallas_call(
        only,
        in_specs=[pl.BlockSpec(memory_space=pltpu.SMEM)] + [whole] * len(arrays)
        + [pl.BlockSpec(memory_space=pl.ANY)] * len(waits),
        out_specs=[whole] * len(outs),
        out_shape=[jax.ShapeDtypeStruct(shape, dtype) for shape, dtype in outs],
        scratch_shapes=list(scratch),
        input_output_aliases=aliases or {},
        compiler_params=pltpu.CompilerParams(vmem_limit_bytes=40 * 1024 * 1024),
        cost_estimate=pl.CostEstimate(flops=1000000, bytes_accessed=100000, transcendentals=0),
    )(scalars, *arrays, *waits)


def tied_kernel(*refs):
    pass


def after(value, *others):
    anywhere = pl.BlockSpec(memory_space=pl.ANY)
    return pl.pallas_call(
        tied_kernel,
        in_specs=[anywhere] * (1 + len(others)),
        out_specs=anywhere,
        out_shape=jax.ShapeDtypeStruct(value.shape, value.dtype),
        input_output_aliases={0: 0},
        cost_estimate=pl.CostEstimate(flops=0, bytes_accessed=0, transcendentals=0),
    )(value, *others)


class Ring:
    def __init__(self, shard, longer):
        self.chips, self.longer, self.step = lax.axis_size("fsdp") // 2, longer, 0
        self.moving, self.found = {1: shard, -1: shard}, {0: shard}
        self.last = shard

    def advance(self, *waits):
        self.step += 1
        for way in (1, -1):
            if 2 * self.step < self.chips or way == self.longer:
                value = after(self.moving[way], *waits) if waits else self.moving[way]
                self.moving[way] = self.last = along_ring(value, way)
                self.found[-way * self.step % self.chips] = self.last


def block(index, size):
    return pl.ds(pl.multiple_of(index * size, size), size)


def split_kernel(norm, scal_ref, rows_ref, kept_ref, sent_ref):
    core = scal_ref[0]
    count, width = rows_ref.shape
    size, some = 256, 64
    for first in range(0, count, some):
        at = slice(first, first + some)
        if norm:
            values = rows_ref[at, :].astype(jnp.float32)
            scale = lax.rsqrt(jnp.mean(values * values, axis=1, keepdims=True) + 1e-05)
        for j in range(width // (2 * size)):
            for out_ref, which in ((kept_ref, core), (sent_ref, 1 - core)):
                part = rows_ref[at, block(2 * j + which, size)]
                if norm:
                    part = (part.astype(jnp.float32) * scale).astype(jnp.bfloat16)
                out_ref[at, j * size:(j + 1) * size] = part


def keyval_kernel(distances, scal_ref, segs_ref, own_ref, other_ref, *refs):
    weights, (kept_ref, sent_ref) = refs[: len(distances)], refs[len(distances):]
    core = scal_ref[0]
    rows = own_ref.shape[0]
    lane = lax.broadcasted_iota(jnp.int32, (rows, 128), 1)
    for rows_ref, which in ((own_ref, core), (other_ref, 1 - core)):
        total = None
        for distance, weight_ref in zip(distances, weights):
            found = jnp.dot(
                rows_ref[:, block(scal_ref[2 + distance], weight_ref.shape[0])], weight_ref[...],
                preferred_element_type=jnp.float32,
            )
            total = found if total is None else total + found
        for part in range(2):
            low = total[:, part * 256:part * 256 + 128]
            high = total[:, part * 256 + 128:part * 256 + 256]
            zero = jnp.where(lane < HEAD_SIZE, low, pltpu.roll(high, HEAD_SIZE, 1))
            one = jnp.where(lane < HEAD_SIZE, pltpu.roll(low, HEAD_SIZE, 1), high)
            at = slice(part * 128, part * 128 + 128)
            kept_ref[block(which, rows), at] = jnp.where(core == 0, zero, one)
            sent_ref[block(which, rows), at] = jnp.where(core == 0, one, zero)
    marks = (segs_ref[...] + 1).astype(jnp.float32)
    sent_ref[2 * rows:, :] = jnp.broadcast_to(marks, (8, marks.shape[1]))


def parcel_kernel(scal_ref, segs_ref, kept_ref, received_ref, out_ref):
    core = scal_ref[0]
    count = kept_ref.shape[0]
    out_ref[:count, :] = (kept_ref[...] + received_ref[:count, :]).astype(out_ref.dtype)
    own = (segs_ref[...] + 1).astype(jnp.float32)
    other = received_ref[count:count + 1, :]
    first, second = jnp.where(core == 0, own, other), jnp.where(core == 0, other, own)
    row = lax.broadcasted_iota(jnp.int32, (MARK_ROWS, own.shape[1]), 0)
    marks = jnp.where(row == 0, first, jnp.where(row == 1, second, 0.0))
    out_ref[count:, :] = marks.astype(out_ref.dtype)


def window_kernel(scal_ref, four_ref, two_ref, own_ref, crossed_ref, kt_ref, v_ref, lo_ref):
    odd = scal_ref[1]
    length = own_ref.shape[0]
    count = length - MARK_ROWS
    half = count // 2
    second = pl.multiple_of(odd * length, MARK_ROWS)
    fourth = pl.multiple_of((1 - odd) * length, MARK_ROWS)
    places = [(four_ref, 0), (crossed_ref, second), (two_ref, 0), (crossed_ref, fourth), (own_ref, 0)]
    lane = lax.broadcasted_iota(jnp.int32, (count, 128), 1)
    blank = jnp.zeros((HEAD_SIZE, count), jnp.bfloat16)
    marks = []
    for i, (ref, first) in enumerate(places):
        at = slice(i * count, (i + 1) * count)
        keys = ref[pl.ds(first, count), 0:128].astype(jnp.float32).T.astype(jnp.bfloat16)
        values = ref[pl.ds(first, count), 128:256].astype(jnp.float32)
        turned = pltpu.roll(values, HEAD_SIZE, 1)
        for g in range(2):
            head = keys[g * HEAD_SIZE:(g + 1) * HEAD_SIZE]
            kt_ref[g, 0, :HEAD_SIZE, at] = head
            kt_ref[g, 0, HEAD_SIZE:, at] = blank
            kt_ref[g, 1, :HEAD_SIZE, at] = blank
            kt_ref[g, 1, HEAD_SIZE:, at] = head
            low, high = (values, turned) if g == 0 else (turned, values)
            v_ref[g, 0, at, :] = jnp.where(lane < HEAD_SIZE, low, 0.0).astype(jnp.bfloat16)
            v_ref[g, 1, at, :] = jnp.where(lane < HEAD_SIZE, 0.0, high).astype(jnp.bfloat16)
        found = ref[pl.ds(first + count, MARK_ROWS), :].astype(jnp.float32)
        marks += [found[0:1, :], found[1:2, :]]
    across = lax.broadcasted_iota(jnp.int32, (half, half), 1)
    down = lax.broadcasted_iota(jnp.int32, (half, half), 0)
    for part in range(2):
        mine = jnp.sum(jnp.where(across == down, marks[-2 + part], 0.0), axis=1, keepdims=True)
        earlier = jnp.zeros((half, half), jnp.float32)
        for row in marks:
            earlier = earlier + jnp.where(row < mine, 1.0, 0.0)
        earlier = jnp.sum(earlier, axis=1, keepdims=True).astype(jnp.int32)
        place = lax.broadcasted_iota(jnp.int32, (half, 128), 0) + (part * half + 1)
        lo_ref[part * half:(part + 1) * half, :] = jnp.maximum(earlier, place)


def query_kernel(distances, more, scal_ref, own_ref, other_ref, *refs):
    weights, refs = refs[: len(distances)], refs[len(distances):]
    core = scal_ref[0]
    rows = own_ref.shape[0]
    outs = refs[-2:]
    for rows_ref, which in ((own_ref, core), (other_ref, 1 - core)):
        at = block(which, rows)
        for i, column in enumerate((core, 1 - core)):
            total = refs[i][at, :] if more else None
            for distance, weight_ref in zip(distances, weights):
                found = jnp.dot(
                    rows_ref[:, block(scal_ref[2 + distance], weight_ref.shape[0])],
                    weight_ref[:, block(column, GROUP_WIDTH)],
                    preferred_element_type=jnp.float32,
                )
                total = found if total is None else total + found
            outs[i][at, :] = total


def attention_kernel(lo_ref, kept_ref, received_ref, kt_ref, v_ref, out_ref, query_ref, score_ref):
    tile = pl.program_id(0)
    start = pl.multiple_of(tile * TILE, TILE)
    span = LOOKBACK_SPAN + TILE
    lo = lo_ref[...] - start
    lane = lax.broadcasted_iota(jnp.int32, (TILE, 128), 1)
    row = lax.broadcasted_iota(jnp.int32, (TILE, 128), 0)
    blocks = span // TILE
    queries = (kept_ref[...] + received_ref[...]).astype(jnp.bfloat16)
    query_ref[...] = queries * jnp.bfloat16(HEAD_SIZE ** -0.5)

    def scores_of(pair, parity):
        q = query_ref[:, pair * 128:(pair + 1) * 128]
        peak = jnp.full((TILE, 128), MASKED, jnp.float32)
        for i in range(blocks):
            first = pl.multiple_of(start + i * TILE, TILE)
            found = jnp.dot(q, kt_ref[parity, :, pl.ds(first, TILE)], preferred_element_type=jnp.float32)
            for part in range(TILE // 128):
                at = i * TILE + part * 128
                visible = lane + at >= lo
                if at >= LOOKBACK_SPAN:
                    visible = visible & (lane + (at - LOOKBACK_SPAN) <= row)
                kept = jnp.where(visible, found[:, part * 128:(part + 1) * 128], MASKED)
                peak = jnp.maximum(peak, kept)
                score_ref[parity, :, at:at + 128] = kept
        return jnp.max(peak, axis=1, keepdims=True)

    def mixed_of(parity, peak):
        total = jnp.zeros((TILE, 128), jnp.float32)
        mixed = jnp.zeros((TILE, 128), jnp.float32)
        for i in range(blocks):
            first = pl.multiple_of(start + i * TILE, TILE)
            weights = jnp.exp(score_ref[parity, :, i * TILE:(i + 1) * TILE] - peak)
            for part in range(TILE // 128):
                total = total + weights[:, part * 128:(part + 1) * 128]
            mixed = mixed + jnp.dot(
                weights.astype(jnp.bfloat16), v_ref[parity, pl.ds(first, TILE), :],
                preferred_element_type=jnp.float32,
            )
        return mixed * (1.0 / jnp.sum(total, axis=1, keepdims=True))

    for pair in range(GROUP // 2):
        peaks = [scores_of(pair, parity) for parity in range(2)]
        parts = [mixed_of(parity, peaks[parity]) for parity in range(2)]
        out_ref[:, pair * 128:(pair + 1) * 128] = (parts[0] + parts[1]).astype(out_ref.dtype)


def attention(lo, kept, received, keys_t, values, waits):
    rows = kept.shape[0]
    window = keys_t.shape[2]
    span = LOOKBACK_SPAN + TILE

    def only(*refs):
        attention_kernel(*refs[:5], *refs[5 + len(waits):])

    return pl.pallas_call(
        only,
        grid=(rows // TILE,),
        in_specs=[
            pl.BlockSpec((TILE, 128), lambda t: (t, 0)),
            pl.BlockSpec((TILE, GROUP_WIDTH), lambda t: (t, 0)),
            pl.BlockSpec((TILE, GROUP_WIDTH), lambda t: (t, 0)),
            pl.BlockSpec((2, 128, window), lambda t: (0, 0, 0)),
            pl.BlockSpec((2, window, 128), lambda t: (0, 0, 0)),
        ] + [pl.BlockSpec(memory_space=pl.ANY)] * len(waits),
        out_specs=pl.BlockSpec((TILE, GROUP_WIDTH), lambda t: (t, 0)),
        out_shape=jax.ShapeDtypeStruct((rows, GROUP_WIDTH), jnp.bfloat16),
        scratch_shapes=[
            pltpu.VMEM((TILE, GROUP_WIDTH), jnp.bfloat16), pltpu.VMEM((2, TILE, span), jnp.float32)
        ],
        compiler_params=pltpu.CompilerParams(vmem_limit_bytes=40 * 1024 * 1024),
        cost_estimate=pl.CostEstimate(flops=1000000, bytes_accessed=100000, transcendentals=0),
    )(lo, kept, received, keys_t, values, *waits)


def out_kernel(distances, mode, scal_ref, *refs):
    attended, refs = refs[:4], refs[4:]
    adds, refs = refs[:2], refs[2:]
    weights, refs = refs[: 2 * len(distances)], refs[2 * len(distances):]
    outs = refs[-2:]
    core = scal_ref[0]
    rows = adds[0].shape[0]
    depth = attended[0].shape[1]
    if mode != "alone":
        for i in range(2):
            outs[i][...] = refs[i][...] if mode == "more" else jnp.zeros_like(outs[i])
    for i, which in enumerate((core, 1 - core)):
        for j, distance in enumerate(distances):
            columns = weights[2 * j].shape[1]
            at = block(scal_ref[2 + distance], columns)
            total = adds[i][:, at].astype(jnp.float32)
            for g in range(2):
                for side, column in enumerate((core, 1 - core)):
                    total = total + jnp.dot(
                        attended[2 * g + side][block(which, rows), :],
                        weights[2 * j + g][block(column, depth), :],
                        preferred_element_type=jnp.float32,
                    )
            if mode == "alone":
                outs[i][...] = total.astype(outs[i].dtype)
            else:
                outs[i][:, at] = total.astype(outs[i].dtype)


def join_kernel(last, scal_ref, own_ref, other_ref, own_last_ref, other_last_ref, out_ref):
    core = scal_ref[0]
    size = own_last_ref.shape[1]
    for j in range(own_ref.shape[1] // size):
        at = slice(j * size, (j + 1) * size)
        out_ref[:, block(2 * j + core, size)] = own_ref[:, at]
        out_ref[:, block(2 * j + 1 - core, size)] = other_ref[:, at]
    j = scal_ref[2 + last]
    out_ref[:, block(2 * j + core, size)] = own_last_ref[...]
    out_ref[:, block(2 * j + 1 - core, size)] = other_last_ref[...]


def body(section_input, segment_ids, query_weight, keyval_weight, out_weight):
    hidden = section_input[0]
    rows, width = hidden.shape
    device = lax.axis_index("fsdp")
    chips = lax.axis_size("fsdp") // 2
    chip, core = device // 2, device % 2
    order = jnp.array(ring_order(chips), jnp.int32)
    place = jnp.argmax(order == chip).astype(jnp.int32)
    sources = order[(place + jnp.arange(chips, dtype=jnp.int32)) % chips]
    scalars = jnp.concatenate([jnp.stack([core, chip % 2]).astype(jnp.int32), sources])

    per_half = query_weight.shape[2] // 2
    keyval = Ring(keyval_weight[0], 1)
    query = [Ring(query_weight[0][:, g * per_half:(g + 1) * per_half], 1 - 2 * g) for g in range(2)]
    keyval.advance()
    query[0].advance()
    query[1].advance()
    out_shard = to_next_section(out_weight[0])

    half = ((rows, width // 2), jnp.bfloat16)
    own_rows, sent = run(functools.partial(split_kernel, True), [half, half], scalars, [hidden])
    other_rows = swap_cores(sent)

    keyval.advance()
    keyval.advance()
    query[0].advance()
    query[1].advance(query[0].found[chips - 1])
    keyval.advance(query[1].found[1])
    distances = list(range(chips))
    kept, sent = run(
        functools.partial(keyval_kernel, distances),
        [((2 * rows, 256), jnp.float32), ((2 * rows + 8, 256), jnp.float32)],
        scalars, [segment_ids, own_rows, other_rows] + [keyval.found[d] for d in distances],
    )
    parcel, = run(
        parcel_kernel, [((2 * rows + MARK_ROWS, 256), jnp.bfloat16)], scalars,
        [segment_ids, kept, swap_cores(sent)],
    )
    back_two = two_chips_on(parcel)

    query[0].advance(keyval.last)
    query[1].advance(query[0].found[2])
    near = [0, 1, chips - 1, 2, chips - 2]
    far = [d for d in distances if d not in near]
    partial_sum = ((2 * rows, GROUP_WIDTH), jnp.float32)
    sums = [
        run(
            functools.partial(query_kernel, near, False), [partial_sum] * 2, scalars,
            [own_rows, other_rows] + [query[g].found[d] for d in near], waits=[parcel],
        )
        for g in range(2)
    ]
    back_four = two_chips_on(back_two)
    even = chip % 2 == 0
    crossed = swap_chips(jnp.concatenate([jnp.where(even, parcel, back_four), back_two], axis=0))
    window = 5 * 2 * rows
    keys_t, values, lowest = run(
        window_kernel,
        [((2, 2, 128, window), jnp.bfloat16), ((2, 2, window, 128), jnp.bfloat16), ((2 * rows, 128), jnp.int32)],
        scalars, [back_four, back_two, parcel, crossed], waits=sums[0][:1] + sums[1][:1],
    )

    middle = out_shard.shape[0] // 2
    out_ready = after(out_shard, query[0].found[3], query[1].found[3])
    query[0].advance()
    query[1].advance()
    out = [Ring(out_ready[g * middle:(g + 1) * middle], 1 - 2 * g) for g in range(2)]
    out[0].advance()
    out[1].advance()
    hidden_next = to_next_section(after(hidden, out_shard))

    sums = [
        run(
            functools.partial(query_kernel, far, True), [partial_sum] * 2, scalars,
            [own_rows, other_rows] + [query[g].found[d] for d in far] + list(sums[g]), waits=[keys_t],
        )
        for g in range(2)
    ]
    received = [swap_cores(sums[g][1]) for g in range(2)]
    out[0].advance(received[0])
    out[1].advance(received[1])
    attended = [None, None]
    attended[0] = attention(
        lowest, sums[0][0], received[0], keys_t[0], values[0], [out[0].found[1], out[1].found[1]]
    )
    out[0].advance(attended[0])
    out[1].advance(attended[0])
    attended[1] = attention(
        lowest, sums[1][0], received[1], keys_t[1], values[1], [out[0].found[2], out[1].found[2]]
    )
    kept, sent = run(functools.partial(split_kernel, False), [half, half], scalars, [hidden_next])
    adds = [kept, swap_cores(sent)]
    out[0].advance(attended[1])
    out[1].advance(attended[1])
    arrived = []
    for g in range(2):
        mine = to_next_section(attended[g])
        arrived += [mine, swap_cores(mine)]

    def made(some, mode, before=()):
        shards = [out[g].found[d] for d in some for g in range(2)]
        outs = [((rows, out_shard.shape[1]), jnp.bfloat16)] * 2 if mode == "alone" else [half, half]
        taken = arrived + adds + shards
        aliases = {1 + len(taken) + i: i for i in range(2)} if before else {}
        return run(
            functools.partial(out_kernel, some, mode), outs, scalars, taken + list(before), aliases=aliases
        )

    most = made([0, 1, chips - 1, 2, chips - 2], "first")
    most = made([3, chips - 3], "more", most)
    other_most = swap_cores(most[1])
    last = made([chips // 2], "alone")
    joined, = run(
        functools.partial(join_kernel, chips // 2), [((rows, width), jnp.bfloat16)], scalars,
        [most[0], other_most, last[0], swap_cores(last[1])],
    )
    return joined[None]


def solution(mesh):
    return jax.shard_map(
        body,
        mesh=mesh,
        in_specs=(
            P("section", "fsdp", None),
            P("section", "fsdp"),
            P("section", "fsdp", None),
            P("section", "fsdp", None),
            P("section", None, "fsdp"),
        ),
        out_specs=P("section", "fsdp", None),
        check_vma=False,
    )
```

time: 340 us -> 318 us (0.935)
  starting transfers between devices: 18.5 us -> 63.5 us
  waiting for transfers between devices: 174 us -> 130 us
  Pallas kernels: 40.2 us -> 71.4 us
  other arithmetic: 25.8 us -> 3.17 us
  between operations: 14.2 us -> 0.44 us
  matrix products: 12 us -> 0 us
    ppermute x0 -> x35, waiting for transfers between devices: none -> 110 us  [along_ring(): return lax.ppermute(value, 'fsdp', pairs)]
    all_gather x2 -> x0, waiting for transfers between devices: 81.7 us -> none  [gathered(): lax.all_gather(value, 'fsdp', axis=0, tiled=False, axis_index_groups=groups)]
    ppermute x0 -> x35, starting transfers between devices: none -> 47.9 us  [along_ring(): return lax.ppermute(value, 'fsdp', pairs)]
    ppermute x4, waiting for transfers between devices: 61.8 us -> 18.2 us  [to_next_section(): lax.ppermute(value, 'section', [(i, (i + 1) % count) for i in range(count)])]
    pallas_call x3 -> x34, Pallas kernels: 40.2 us -> 71.4 us  [the longest x13 40 us: run(): pl.pallas_call(only, in_specs=[pl.BlockSpec(memory_space=pltpu.SMEM)] + [...]
    unnamed x56 -> x128, local copies, waits for them, and re-layouts: 14.1 us -> 39.3 us
    ppermute x2, waiting for transfers between devices: 18.7 us -> 0.01 us  [two_chips_on(): return lax.ppermute(value, 'fsdp', [(i, i + 4) for i in range(count - 4)])]
    dynamic_slice x6 -> x0, local copies, waits for them, and re-layouts: 15.1 us -> none  [the longest x2 13.7 us: own_features(): lax.dynamic_index_in_dim(parts, core, 2, keepdims=False).reshape(rows, -1)]
  transfers between devices with their start and end apart: 17 -> 51, of which waited for: 9 -> 21; matrix products, arithmetic and copies ran while one was open for 22% -> 6% of each run, Pallas kernels for 9% -> 18%
where the time goes in v1:
time: 318 us; the launch traced here: 317 us
  waiting for transfers between devices  130 us (41%)
  Pallas kernels  71.4 us (22%)
  starting transfers between devices  63.5 us (20%)
  local copies, waits for them, and re-layouts  48.3 us (15%)
    ppermute x35, waiting for transfers between devices, along_ring(): return lax.ppermute(value, 'fsdp', pairs)  110 us
    ppermute x35, starting transfers between devices, along_ring(): return lax.ppermute(value, 'fsdp', pairs)  47.9 us
    pallas_call x13, Pallas kernels, run(): pl.pallas_call(only, in_specs=[pl.BlockSpec(memory_space=pltpu.SMEM)] + [...  40 us
    unnamed x128, local copies, waits for them, and re-layouts  39.3 us
    pallas_call x2, Pallas kernels, attention(): pl.pallas_call(only, grid=(rows // TILE,), in_specs=[pl.BlockSpec((TILE,...  31.4 us
    ppermute x4, waiting for transfers between devices, to_next_section(): lax.ppermute(value, 'section', [(i, (i + 1) % count) for i in range(count)])  18.2 us
    ppermute x2, starting transfers between devices, two_chips_on(): return lax.ppermute(value, 'fsdp', [(i, i + 4) for i in range(count - 4)])  7.45 us
  transfers between devices with their start and end apart: 51, of which 21 were waited for; matrix products, arithmetic and copies ran while one was open for 6% of the time, Pallas kernels for 18%

profile of v1, /device:TPU:0, one launch (start us, length us, event | category | flops | bytes accessed | tf_op | source)
XLA Modules:
  0.0 316.7 jit_solution(12943231624137330245)
XLA Ops:
  0.0 3.2 %copy.50 = bf16[1,256,4096]{2,1,0:T(8,128)(2,1)} copy(bf16[1,256,4096]{2,1,0:T(8,128)(2,1)} %param.6) | data formatting | bytes 4194304
  8.2 3.4 %shard_map.64 = (bf16[256,2048]{1,0:T(8,128)(2,1)S(1)}, bf16[256,2048]{1,0:T(8,128)(2,1)}) custom-call(s32[10]{0:T(128)S(1)} %pad_add_fusion.refs_0_, bf16[256,4096]{1,0:T(8,128)(2,1)} %bitcast.3.refs_1_.refs_0_), custom_call_target="tpu_custom_call" | custom-call | flops 1000000 | bytes 100000 | tf_op jit(solution)/shard_map/pallas_call | solution.py:62
  24.7 11.3 %collective-permute-done.2.refs_6_ = bf16[256,512]{1,0:T(8,128)(2,1)} collective-permute-done((bf16[256,512]{1,0:T(8,128)(2,1)}, bf16[256,512]{1,0:T(8,128)(2,1)}, u32[]{:S(2)}, u32[]{:S(2)}) %collective-permute-start.2) | collective-permute-done | bytes 262176 | tf_op jit(solution)/shard_map/ppermute | solution.py:52
  39.4 3.7 %collective-permute-done.3.refs_7_ = bf16[256,512]{1,0:T(8,128)(2,1)} collective-permute-done((bf16[256,512]{1,0:T(8,128)(2,1)}, bf16[256,512]{1,0:T(8,128)(2,1)}, u32[]{:S(2)}, u32[]{:S(2)}) %collective-permute-start.3) | collective-permute-done | bytes 262176 | tf_op jit(solution)/shard_map/ppermute | solution.py:52
  47.7 3.4 %shard_map.66 = (f32[512,256]{1,0:T(8,128)S(1)}, f32[520,256]{1,0:T(8,128)}) custom-call(s32[10]{0:T(128)S(1)} %pad_add_fusion.refs_0_, s32[1,256]{1,0:T(1,128)S(1)} %copy-done.58, bf16[256,2048]{1,0:T(8,128)(2,1)S(1)} %get-tuple-element.30.refs_2_.refs_1_, bf16[256,2048]{1,0:T(8,128)(2,1)S(1)} %collective-permute-done.refs_3_.refs_2_, ...), custom_call_target="tpu_custom_call" | custom-call | flops 1000000 | bytes 100000 | tf_op jit(solution)/shard_map/pallas_call | solution.py:62
  60.2 3.2 %collective-permute-start.10 = (bf16[528,256]{1,0:T(8,128)(2,1)S(1)}, bf16[528,256]{1,0:T(8,128)(2,1)}, u32[]{:S(2)}, u32[]{:S(2)}) collective-permute-start(bf16[528,256]{1,0:T(8,128)(2,1)S(1)} %shard_map.67.refs_8_.refs_3_), channel_id=1, source_target_pairs={{0,4},{1,5},{2,6},{3,7},{4,8},{5,9},{6,10},{7,11},{8,12},{9,13},{1... | collective-permute-start | bytes 811016 | tf_op jit(solution)/shard_map/ppermute | solution.py:37
  68.8 10.4 %collective-permute-done.18.refs_6_.refs_0_ = bf16[256,1024]{1,0:T(8,128)(2,1)} collective-permute-done((bf16[256,1024]{1,0:T(8,128)(2,1)}, bf16[256,1024]{1,0:T(8,128)(2,1)}, u32[]{:S(2)}, u32[]{:S(2)}) %collective-permute-start.18) | collective-permute-done | bytes 524320 | tf_op jit(solution)/shard_map/ppermute | solution.py:52
  80.8 4.2 %collective-permute-start.11 = (bf16[528,256]{1,0:T(8,128)(2,1)}, bf16[528,256]{1,0:T(8,128)(2,1)}, u32[]{:S(2)}, u32[]{:S(2)}) collective-permute-start(bf16[528,256]{1,0:T(8,128)(2,1)} %collective-permute-done.10.refs_2_), channel_id=1, source_target_pairs={{0,4},{1,5},{2,6},{3,7},{4,8},{5,9},{6,10},{7,11},{8,12},{9,13},{1... | collective-permute-start | bytes 811016 | tf_op jit(solution)/shard_map/ppermute | solution.py:37
  92.8 4.6 %collective-permute-start.25 = (bf16[256,1024]{1,0:T(8,128)(2,1)}, bf16[256,1024]{1,0:T(8,128)(2,1)}, u32[]{:S(2)}, u32[]{:S(2)}) collective-permute-start(bf16[256,1024]{1,0:T(8,128)(2,1)} %shard_map.76), channel_id=1, source_target_pairs={{0,2},{1,3},{4,0},{5,1},{8,4},{9,5},{12,8},{13,9},{14,12},{15,13},... | collective-permute-start | bytes 1572872 | tf_op jit(solution)/shard_map/ppermute | solution.py:52
  112.8 6.4 %collective-permute-done.21.refs_5_ = bf16[256,1024]{1,0:T(8,128)(2,1)} collective-permute-done((bf16[256,1024]{1,0:T(8,128)(2,1)}, bf16[256,1024]{1,0:T(8,128)(2,1)}, u32[]{:S(2)}, u32[]{:S(2)}) %collective-permute-start.21) | collective-permute-done | bytes 524320 | tf_op jit(solution)/shard_map/ppermute | solution.py:52
  127.2 14.7 %collective-permute-done.31.refs_5_ = bf16[256,1024]{1,0:T(8,128)(2,1)} collective-permute-done((bf16[256,1024]{1,0:T(8,128)(2,1)}, bf16[256,1024]{1,0:T(8,128)(2,1)}, u32[]{:S(2)}, u32[]{:S(2)}) %collective-permute-start.31) | collective-permute-done | bytes 524320 | tf_op jit(solution)/shard_map/ppermute | solution.py:52
  152.7 3.2 %shard_map.75 = (f32[512,512]{1,0:T(8,128)S(1)}, f32[512,512]{1,0:T(8,128)}) custom-call(s32[10]{0:T(128)S(1)} %pad_add_fusion.refs_0_, bf16[256,2048]{1,0:T(8,128)(2,1)S(1)} %get-tuple-element.30.refs_2_.refs_1_, bf16[256,2048]{1,0:T(8,128)(2,1)S(1)} %collective-permute-done.refs_3_.refs_2_, bf16[256,1024]{1,0:T(8,128)(2,1)S(1)} %copy-done.39, ...), custom_call_target="tpu_custom_call" | custom-call | flops 1000000 | bytes 100000 | tf_op jit(solution)/shard_map/pallas_call | solution.py:62
  159.2 4.6 %collective-permute-done.26.refs_5_.refs_9_ = bf16[1024,256]{1,0:T(8,128)(2,1)S(1)} collective-permute-done((bf16[1024,256]{1,0:T(8,128)(2,1)}, bf16[1024,256]{1,0:T(8,128)(2,1)S(1)}, u32[]{:S(2)}, u32[]{:S(2)}) %collective-permute-start.26) | collective-permute-done | bytes 524320 | tf_op jit(solution)/shard_map/ppermute | solution.py:52
  174.8 9.9 %collective-permute-done.37.refs_1_ = bf16[256,4096]{1,0:T(8,128)(2,1)} collective-permute-done((bf16[256,4096]{1,0:T(8,128)(2,1)}, bf16[256,4096]{1,0:T(8,128)(2,1)}, u32[]{:S(2)}, u32[]{:S(2)}) %collective-permute-start.37) | collective-permute-done | bytes 2097184 | tf_op jit(solution)/shard_map/ppermute | solution.py:42
  187.6 15.2 %shard_map.78.refs_1_ = bf16[512,512]{1,0:T(8,128)(2,1)S(1)} custom-call(s32[512,128]{1,0:T(8,128)S(1)} %get-tuple-element.36.refs_0_, f32[512,512]{1,0:T(8,128)S(1)} %copy-done.47, f32[512,512]{1,0:T(8,128)S(1)} %copy-done.4, bf16[2,128,2560]{2,1,0:T(8,128)(2,1)S(1)} %copy-done.8, bf16[2,2560,128]{2,1,0:T(8,128)(2,1)S(1)} %get-tuple-element.54.refs_4_, ...), custom_call_target="tpu_custom_call" | custom-call | flops 1000000 | bytes 100000 | tf_op jit(solution)/shard_map/pallas_call | solution.py:277
  204.4 16.2 %shard_map.83.refs_1_ = bf16[512,512]{1,0:T(8,128)(2,1)} custom-call(s32[512,128]{1,0:T(8,128)S(1)} %get-tuple-element.36.refs_0_, f32[512,512]{1,0:T(8,128)S(1)} %copy-done.45, f32[512,512]{1,0:T(8,128)S(1)} %copy-done.2, bf16[2,128,2560]{2,1,0:T(8,128)(2,1)S(1)} %copy-done.7, bf16[2,2560,128]{2,1,0:T(8,128)(2,1)S(1)} %get-tuple-element.53.refs_4_, ...), custom_call_target="tpu_custom_call" | custom-call | flops 1000000 | bytes 100000 | tf_op jit(solution)/shard_map/pallas_call | solution.py:277
  226.7 8.2 %collective-permute-done.35.refs_3_ = bf16[512,512]{1,0:T(8,128)(2,1)} collective-permute-done((bf16[512,512]{1,0:T(8,128)(2,1)}, bf16[512,512]{1,0:T(8,128)(2,1)}, u32[]{:S(2)}, u32[]{:S(2)}) %collective-permute-start.35) | collective-permute-done | bytes 524320 | tf_op jit(solution)/shard_map/ppermute | solution.py:42
  235.0 5.1 %collective-permute-done.45.refs_0_.refs_16_ = bf16[1024,256]{1,0:T(8,128)(2,1)} collective-permute-done((bf16[1024,256]{1,0:T(8,128)(2,1)}, bf16[1024,256]{1,0:T(8,128)(2,1)}, u32[]{:S(2)}, u32[]{:S(2)}) %collective-permute-start.45) | collective-permute-done | bytes 524320 | tf_op jit(solution)/shard_map/ppermute | solution.py:52
  240.1 10.1 %collective-permute-done.42.refs_0_.refs_15_ = bf16[1024,256]{1,0:T(8,128)(2,1)S(1)} collective-permute-done((bf16[1024,256]{1,0:T(8,128)(2,1)}, bf16[1024,256]{1,0:T(8,128)(2,1)S(1)}, u32[]{:S(2)}, u32[]{:S(2)}) %collective-permute-start.42) | collective-permute-done | bytes 524320 | tf_op jit(solution)/shard_map/ppermute | solution.py:52
  253.3 6.0 %shard_map.92 = (bf16[256,2048]{1,0:T(8,128)(2,1)S(1)}, bf16[256,2048]{1,0:T(8,128)(2,1)}) custom-call(s32[10]{0:T(128)S(1)} %pad_add_fusion.refs_0_, bf16[512,512]{1,0:T(8,128)(2,1)} %collective-permute-done.28.refs_1_, bf16[512,512]{1,0:T(8,128)(2,1)S(1)} %collective-permute-done.29.refs_2_, bf16[512,512]{1,0:T(8,128)(2,1)} %collective-permute-done.35.refs_3_, ...), custom_call_target="tpu_custom_call" | custom-call | flops 1000000 | bytes 100000 | tf_op jit(solution)/shard_map/pallas_call | solution.py:62
  265.9 11.1 %collective-permute-done.46.refs_10_ = bf16[1024,256]{1,0:T(8,128)(2,1)} collective-permute-done((bf16[1024,256]{1,0:T(8,128)(2,1)}, bf16[1024,256]{1,0:T(8,128)(2,1)}, u32[]{:S(2)}, u32[]{:S(2)}) %collective-permute-start.46) | collective-permute-done | bytes 524320 | tf_op jit(solution)/shard_map/ppermute | solution.py:52
  277.0 9.3 %collective-permute-done.43.refs_9_.refs_0_ = bf16[1024,256]{1,0:T(8,128)(2,1)} collective-permute-done((bf16[1024,256]{1,0:T(8,128)(2,1)}, bf16[1024,256]{1,0:T(8,128)(2,1)}, u32[]{:S(2)}, u32[]{:S(2)}) %collective-permute-start.43) | collective-permute-done | bytes 524320 | tf_op jit(solution)/shard_map/ppermute | solution.py:52
  289.2 4.5 %shard_map.93 = (bf16[256,2048]{1,0:T(8,128)(2,1)S(1)}, bf16[256,2048]{1,0:T(8,128)(2,1)}) custom-call(s32[10]{0:T(128)S(1)} %pad_add_fusion.refs_0_, bf16[512,512]{1,0:T(8,128)(2,1)} %collective-permute-done.28.refs_1_, bf16[512,512]{1,0:T(8,128)(2,1)S(1)} %collective-permute-done.29.refs_2_, ...), custom_call_target="tpu_custom_call", output_to_operand_aliasing={{0}: (11, {}), {1}: (12, {})} | custom-call | flops 1000000 | bytes 100000 | tf_op jit(solution)/shard_map/pallas_call | solution.py:62
  296.7 12.6 %collective-permute-done.49.refs_8_ = bf16[1024,256]{1,0:T(8,128)(2,1)} collective-permute-done((bf16[1024,256]{1,0:T(8,128)(2,1)}, bf16[1024,256]{1,0:T(8,128)(2,1)}, u32[]{:S(2)}, u32[]{:S(2)}) %collective-permute-start.49) | collective-permute-done | bytes 524320 | tf_op jit(solution)/shard_map/ppermute | solution.py:52
  (251 shorter events, 131.9 us)
Async XLA Ops:
  11.6 31.5 %collective-permute-start = (bf16[256,2048]{1,0:T(8,128)(2,1)}, bf16[256,2048]{1,0:T(8,128)(2,1)S(1)}, u32[]{:S(2)}, u32[]{:S(2)}) collective-permute-start(bf16[256,2048]{1,0:T(8,128)(2,1)} %get-tuple-element.31), channel_id=1, source_target_pairs={{0,1},{1,0},{2,3},{3,2},{4,5},{5,4},{6,7},{7,6},{8,9},{9,8},{10,11... | collective-permute-start | bytes 3145736 | tf_op jit(solution)/shard_map/ppermute | solution.py:27
  23.1 30.9 %collective-permute-start.14 = (bf16[256,1024]{1,0:T(8,128)(2,1)}, bf16[256,1024]{1,0:T(8,128)(2,1)S(1)}, u32[]{:S(2)}, u32[]{:S(2)}) collective-permute-start(bf16[256,1024]{1,0:T(8,128)(2,1)} %get-tuple-element.59.refs_3_), channel_id=1, source_target_pairs={{0,4},{1,5},{4,8},{5,9},{8,12},{9,13},{12,14},{13,15},{14,10},{15,... | collective-permute-start | bytes 1572872 | tf_op jit(solution)/shard_map/ppermute | solution.py:52
  54.7 24.5 %collective-permute-start.18 = (bf16[256,1024]{1,0:T(8,128)(2,1)}, bf16[256,1024]{1,0:T(8,128)(2,1)}, u32[]{:S(2)}, u32[]{:S(2)}) collective-permute-start(bf16[256,1024]{1,0:T(8,128)(2,1)} %shard_map.69), channel_id=1, source_target_pairs={{0,2},{1,3},{4,0},{5,1},{8,4},{9,5},{12,8},{13,9},{14,12},{15,13},... | collective-permute-start | bytes 1572872 | tf_op jit(solution)/shard_map/ppermute | solution.py:52
  56.5 52.3 %collective-permute-start.24 = (bf16[2048,256]{1,0:T(8,128)(2,1)}, bf16[2048,256]{1,0:T(8,128)(2,1)}, u32[]{:S(2)}, u32[]{:S(2)}) collective-permute-start(bf16[2048,256]{1,0:T(8,128)(2,1)} %bitcast.21), channel_id=1, source_target_pairs={{0,16},{16,0},{1,17},{17,1},{2,18},{18,2},{3,19},{19,3},{4,20},{20... | collective-permute-start | bytes 3145736 | tf_op jit(solution)/shard_map/ppermute | solution.py:42
  68.8 23.1 %collective-permute-start.15 = (bf16[256,1024]{1,0:T(8,128)(2,1)}, bf16[256,1024]{1,0:T(8,128)(2,1)S(1)}, u32[]{:S(2)}, u32[]{:S(2)}) collective-permute-start(bf16[256,1024]{1,0:T(8,128)(2,1)} %collective-permute-done.13.refs_4_), channel_id=1, source_target_pairs={{0,2},{1,3},{4,0},{5,1},{8,4},{9,5},{12,8},{13,9},{14,12},{15,13},... | collective-permute-start | bytes 1572872 | tf_op jit(solution)/shard_map/ppermute | solution.py:52
  80.8 23.6 %collective-permute-start.11 = (bf16[528,256]{1,0:T(8,128)(2,1)}, bf16[528,256]{1,0:T(8,128)(2,1)}, u32[]{:S(2)}, u32[]{:S(2)}) collective-permute-start(bf16[528,256]{1,0:T(8,128)(2,1)} %collective-permute-done.10.refs_2_), channel_id=1, source_target_pairs={{0,4},{1,5},{2,6},{3,7},{4,8},{5,9},{6,10},{7,11},{8,12},{9,13},{1... | collective-permute-start | bytes 811016 | tf_op jit(solution)/shard_map/ppermute | solution.py:37
  106.2 35.7 %collective-permute-start.12 = (bf16[1056,256]{1,0:T(8,128)(2,1)}, bf16[1056,256]{1,0:T(8,128)(2,1)S(1)}, u32[]{:S(2)}, u32[]{:S(2)}) collective-permute-start(bf16[1056,256]{1,0:T(8,128)(2,1)} %pad_maximum_fusion), channel_id=1, source_target_pairs={{0,2},{1,3},{2,0},{3,1},{4,6},{5,7},{6,4},{7,5},{8,10},{9,11},{10,... | collective-permute-start | bytes 1622024 | tf_op jit(solution)/shard_map/ppermute | solution.py:32
  108.7 33.2 %collective-permute-start.31 = (bf16[256,1024]{1,0:T(8,128)(2,1)}, bf16[256,1024]{1,0:T(8,128)(2,1)}, u32[]{:S(2)}, u32[]{:S(2)}) collective-permute-start(bf16[256,1024]{1,0:T(8,128)(2,1)} %shard_map.79), channel_id=1, source_target_pairs={{0,4},{1,5},{4,8},{5,9},{8,12},{9,13},{12,14},{13,15},{14,10},{15,... | collective-permute-start | bytes 1572872 | tf_op jit(solution)/shard_map/ppermute | solution.py:52
  110.3 38.8 %collective-permute-start.30 = (bf16[256,1024]{1,0:T(8,128)(2,1)}, bf16[256,1024]{1,0:T(8,128)(2,1)}, u32[]{:S(2)}, u32[]{:S(2)}) collective-permute-start(bf16[256,1024]{1,0:T(8,128)(2,1)} %collective-permute-done.25.refs_2_.refs_3_), channel_id=1, source_target_pairs={{0,2},{1,3},{4,0},{5,1},{8,4},{9,5},{12,8},{13,9},{14,12},{15,13},... | collective-permute-start | bytes 1572872 | tf_op jit(solution)/shard_map/ppermute | solution.py:52
  119.1 33.5 %collective-permute-start.22 = (bf16[256,1024]{1,0:T(8,128)(2,1)}, bf16[256,1024]{1,0:T(8,128)(2,1)}, u32[]{:S(2)}, u32[]{:S(2)}) collective-permute-start(bf16[256,1024]{1,0:T(8,128)(2,1)} %collective-permute-done.21.refs_5_), channel_id=1, source_target_pairs={{0,4},{1,5},{4,8},{5,9},{8,12},{9,13},{12,14},{13,15},{14,10},{15,... | collective-permute-start | bytes 1572872 | tf_op jit(solution)/shard_map/ppermute | solution.py:52
  124.5 31.9 %collective-permute-start.27 = (bf16[1024,256]{1,0:T(8,128)(2,1)}, bf16[1024,256]{1,0:T(8,128)(2,1)S(1)}, u32[]{:S(2)}, u32[]{:S(2)}) collective-permute-start(bf16[1024,256]{1,0:T(8,128)(2,1)} %get-tuple-element.57.refs_8_), channel_id=1, source_target_pairs={{0,2},{1,3},{4,0},{5,1},{8,4},{9,5},{12,8},{13,9},{14,12},{15,13},... | collective-permute-start | bytes 1572872 | tf_op jit(solution)/shard_map/ppermute | solution.py:52
  141.9 21.9 %collective-permute-start.26 = (bf16[1024,256]{1,0:T(8,128)(2,1)}, bf16[1024,256]{1,0:T(8,128)(2,1)S(1)}, u32[]{:S(2)}, u32[]{:S(2)}) collective-permute-start(bf16[1024,256]{1,0:T(8,128)(2,1)} %get-tuple-element.58.refs_7_), channel_id=1, source_target_pairs={{0,2},{1,3},{4,0},{5,1},{8,4},{9,5},{12,8},{13,9},{14,12},{15,13},... | collective-permute-start | bytes 1572872 | tf_op jit(solution)/shard_map/ppermute | solution.py:52
  142.8 41.9 %collective-permute-start.37 = (bf16[256,4096]{1,0:T(8,128)(2,1)}, bf16[256,4096]{1,0:T(8,128)(2,1)}, u32[]{:S(2)}, u32[]{:S(2)}) collective-permute-start(bf16[256,4096]{1,0:T(8,128)(2,1)} %shard_map.84), channel_id=1, source_target_pairs={{0,16},{16,0},{1,17},{17,1},{2,18},{18,2},{3,19},{19,3},{4,20},{20... | collective-permute-start | bytes 6291464 | tf_op jit(solution)/shard_map/ppermute | solution.py:42
  156.4 64.8 %collective-permute-start.44 = (bf16[1024,256]{1,0:T(8,128)(2,1)}, bf16[1024,256]{1,0:T(8,128)(2,1)}, u32[]{:S(2)}, u32[]{:S(2)}) collective-permute-start(bf16[1024,256]{1,0:T(8,128)(2,1)} %get-tuple-element.57.refs_8_), channel_id=1, source_target_pairs={{0,4},{1,5},{4,8},{5,9},{8,12},{9,13},{12,14},{13,15},{14,10},{15,... | collective-permute-start | bytes 1572872 | tf_op jit(solution)/shard_map/ppermute | solution.py:52
  163.8 59.2 %collective-permute-start.41 = (bf16[1024,256]{1,0:T(8,128)(2,1)}, bf16[1024,256]{1,0:T(8,128)(2,1)}, u32[]{:S(2)}, u32[]{:S(2)}) collective-permute-start(bf16[1024,256]{1,0:T(8,128)(2,1)} %get-tuple-element.58.refs_7_), channel_id=1, source_target_pairs={{0,4},{1,5},{4,8},{5,9},{8,12},{9,13},{12,14},{13,15},{14,10},{15,... | collective-permute-start | bytes 1572872 | tf_op jit(solution)/shard_map/ppermute | solution.py:52
  167.4 35.5 %collective-permute-start.34 = (bf16[1024,256]{1,0:T(8,128)(2,1)}, bf16[1024,256]{1,0:T(8,128)(2,1)S(1)}, u32[]{:S(2)}, u32[]{:S(2)}) collective-permute-start(bf16[1024,256]{1,0:T(8,128)(2,1)} %shard_map.82), channel_id=1, source_target_pairs={{0,2},{1,3},{4,0},{5,1},{8,4},{9,5},{12,8},{13,9},{14,12},{15,13},... | collective-permute-start | bytes 1572872 | tf_op jit(solution)/shard_map/ppermute | solution.py:52
  170.7 33.7 %collective-permute-start.33 = (bf16[1024,256]{1,0:T(8,128)(2,1)}, bf16[1024,256]{1,0:T(8,128)(2,1)S(1)}, u32[]{:S(2)}, u32[]{:S(2)}) collective-permute-start(bf16[1024,256]{1,0:T(8,128)(2,1)} %shard_map.81), channel_id=1, source_target_pairs={{0,2},{1,3},{4,0},{5,1},{8,4},{9,5},{12,8},{13,9},{14,12},{15,13},... | collective-permute-start | bytes 1572872 | tf_op jit(solution)/shard_map/ppermute | solution.py:52
  187.5 47.4 %collective-permute-start.38 = (bf16[256,2048]{1,0:T(8,128)(2,1)}, bf16[256,2048]{1,0:T(8,128)(2,1)S(1)}, u32[]{:S(2)}, u32[]{:S(2)}) collective-permute-start(bf16[256,2048]{1,0:T(8,128)(2,1)} %get-tuple-element.46), channel_id=1, source_target_pairs={{0,1},{1,0},{2,3},{3,2},{4,5},{5,4},{6,7},{7,6},{8,9},{9,8},{10,11... | collective-permute-start | bytes 3145736 | tf_op jit(solution)/shard_map/ppermute | solution.py:27
  202.9 23.8 %collective-permute-start.28 = (bf16[512,512]{1,0:T(8,128)(2,1)S(1)}, bf16[512,512]{1,0:T(8,128)(2,1)}, u32[]{:S(2)}, u32[]{:S(2)}) collective-permute-start(bf16[512,512]{1,0:T(8,128)(2,1)S(1)} %shard_map.78.refs_1_), channel_id=1, source_target_pairs={{0,16},{16,0},{1,17},{17,1},{2,18},{18,2},{3,19},{19,3},{4,20},{20... | collective-permute-start | bytes 1572872 | tf_op jit(solution)/shard_map/ppermute | solution.py:42
  226.7 23.5 %collective-permute-start.42 = (bf16[1024,256]{1,0:T(8,128)(2,1)}, bf16[1024,256]{1,0:T(8,128)(2,1)S(1)}, u32[]{:S(2)}, u32[]{:S(2)}) collective-permute-start(bf16[1024,256]{1,0:T(8,128)(2,1)} %shard_map.88), channel_id=1, source_target_pairs={{0,4},{1,5},{4,8},{5,9},{8,12},{9,13},{12,14},{13,15},{14,10},{15,... | collective-permute-start | bytes 1572872 | tf_op jit(solution)/shard_map/ppermute | solution.py:52
  226.7 23.4 %collective-permute-start.29 = (bf16[512,512]{1,0:T(8,128)(2,1)}, bf16[512,512]{1,0:T(8,128)(2,1)S(1)}, u32[]{:S(2)}, u32[]{:S(2)}) collective-permute-start(bf16[512,512]{1,0:T(8,128)(2,1)} %collective-permute-done.28.refs_1_), channel_id=1, source_target_pairs={{0,1},{1,0},{2,3},{3,2},{4,5},{5,4},{6,7},{7,6},{8,9},{9,8},{10,11... | collective-permute-start | bytes 1572872 | tf_op jit(solution)/shard_map/ppermute | solution.py:27
  263.6 22.7 %collective-permute-start.43 = (bf16[1024,256]{1,0:T(8,128)(2,1)}, bf16[1024,256]{1,0:T(8,128)(2,1)}, u32[]{:S(2)}, u32[]{:S(2)}) collective-permute-start(bf16[1024,256]{1,0:T(8,128)(2,1)} %shard_map.89), channel_id=1, source_target_pairs={{0,4},{1,5},{4,8},{5,9},{8,12},{9,13},{12,14},{13,15},{14,10},{15,... | collective-permute-start | bytes 1572872 | tf_op jit(solution)/shard_map/ppermute | solution.py:52
  263.9 22.4 %collective-permute-start.40 = (bf16[1024,256]{1,0:T(8,128)(2,1)}, bf16[1024,256]{1,0:T(8,128)(2,1)}, u32[]{:S(2)}, u32[]{:S(2)}) collective-permute-start(bf16[1024,256]{1,0:T(8,128)(2,1)} %shard_map.87), channel_id=1, source_target_pairs={{0,2},{1,3},{4,0},{5,1},{8,4},{9,5},{12,8},{13,9},{14,12},{15,13},... | collective-permute-start | bytes 1572872 | tf_op jit(solution)/shard_map/ppermute | solution.py:52
  265.6 22.4 %collective-permute-start.39 = (bf16[1024,256]{1,0:T(8,128)(2,1)}, bf16[1024,256]{1,0:T(8,128)(2,1)S(1)}, u32[]{:S(2)}, u32[]{:S(2)}) collective-permute-start(bf16[1024,256]{1,0:T(8,128)(2,1)} %shard_map.86), channel_id=1, source_target_pairs={{0,2},{1,3},{4,0},{5,1},{8,4},{9,5},{12,8},{13,9},{14,12},{15,13},... | collective-permute-start | bytes 1572872 | tf_op jit(solution)/shard_map/ppermute | solution.py:52
  (87 other events, 816.1 us)

commit v2 on v1

v2 whole, which is shorter than its diff:
```python
import functools

import jax
import jax.numpy as jnp
from jax import lax
from jax.experimental import pallas as pl
from jax.experimental.pallas import tpu as pltpu
from jax.sharding import PartitionSpec as P

QUERY_HEADS = 32
KEY_HEADS = 4
HEAD_SIZE = 64
LOOKBACK_SPAN = 2048
GROUP = QUERY_HEADS // KEY_HEADS
GROUP_WIDTH = GROUP * HEAD_SIZE
TILE = 256
MASKED = -1e30
MARK_ROWS = 16


def ring_order(chips):
    return list(range(0, chips, 2)) + list(range(chips - 1, 0, -2))


def swap_cores(value):
    count = lax.axis_size("fsdp")
    return lax.ppermute(value, "fsdp", [(i, i ^ 1) for i in range(count)])


def swap_chips(value):
    count = lax.axis_size("fsdp")
    return lax.ppermute(value, "fsdp", [(i, i ^ 2) for i in range(count)])


def two_chips_on(value):
    count = lax.axis_size("fsdp")
    return lax.ppermute(value, "fsdp", [(i, i + 4) for i in range(count - 4)])


def to_next_section(value, other_core=False):
    sections, count = lax.axis_size("section"), lax.axis_size("fsdp")
    pairs = []
    for section in range(sections):
        for i in range(count):
            target = i ^ 1 if other_core else i
            pairs.append((section * count + i, (section + 1) % sections * count + target))
    return lax.ppermute(value, ("section", "fsdp"), pairs)


def along_ring(value, step):
    chips = lax.axis_size("fsdp") // 2
    order = ring_order(chips)
    pairs = []
    for place in range(chips):
        target = order[(place + step) % chips]
        pairs += [(2 * order[place] + core, 2 * target + core) for core in range(2)]
    return lax.ppermute(value, "fsdp", pairs)


def run(kernel, outs, scalars, arrays, waits=(), aliases=None, scratch=()):
    whole = pl.BlockSpec(memory_space=pltpu.VMEM)
    taken = 1 + len(arrays)

    def only(*refs):
        kernel(*refs[:taken], *refs[taken + len(waits):])

    return pl.pallas_call(
        only,
        in_specs=[pl.BlockSpec(memory_space=pltpu.SMEM)] + [whole] * len(arrays)
        + [pl.BlockSpec(memory_space=pl.ANY)] * len(waits),
        out_specs=[whole] * len(outs),
        out_shape=[jax.ShapeDtypeStruct(shape, dtype) for shape, dtype in outs],
        scratch_shapes=list(scratch),
        input_output_aliases=aliases or {},
        compiler_params=pltpu.CompilerParams(vmem_limit_bytes=40 * 1024 * 1024),
        cost_estimate=pl.CostEstimate(flops=1000000, bytes_accessed=100000, transcendentals=0),
    )(scalars, *arrays, *waits)


def around(shard):
    chips = lax.axis_size("fsdp") // 2
    found, moving = {0: [(0, shard)]}, {1: shard, -1: shard}
    for step in range(1, (chips - 1) // 2 + 1):
        for way in (1, -1):
            moving[way] = along_ring(moving[way], way)
            found[-way * step % chips] = [(0, moving[way])]
    if chips % 2 == 0:
        half = shard.shape[0] // 2
        found[chips // 2] = [
            (0, along_ring(moving[1][:half], 1)), (half, along_ring(moving[-1][half:], -1))
        ]
    return found


def block(index, size):
    return pl.ds(pl.multiple_of(index * size, size), size)


def split_kernel(norm, scal_ref, rows_ref, kept_ref, sent_ref):
    core = scal_ref[0]
    count, width = rows_ref.shape
    size, some = 256, 64
    for first in range(0, count, some):
        at = slice(first, first + some)
        if norm:
            values = rows_ref[at, :].astype(jnp.float32)
            scale = lax.rsqrt(jnp.mean(values * values, axis=1, keepdims=True) + 1e-05)
        for j in range(width // (2 * size)):
            for out_ref, which in ((kept_ref, core), (sent_ref, 1 - core)):
                part = rows_ref[at, block(2 * j + which, size)]
                if norm:
                    part = (part.astype(jnp.float32) * scale).astype(jnp.bfloat16)
                out_ref[at, j * size:(j + 1) * size] = part


def keyval_kernel(scal_ref, segs_ref, own_ref, other_ref, weight_ref, kept_ref, sent_ref):
    core = scal_ref[0]
    rows = own_ref.shape[0]
    size = 256
    total = None
    for j in range(own_ref.shape[1] // size):
        for ref, which in ((own_ref, core), (other_ref, 1 - core)):
            found = jnp.dot(
                ref[:, j * size:(j + 1) * size], weight_ref[0, block(2 * j + which, size), :],
                preferred_element_type=jnp.float32,
            )
            total = found if total is None else total + found
    lane = lax.broadcasted_iota(jnp.int32, (rows, 128), 1)
    for part in range(2):
        low = total[:, part * 256:part * 256 + 128]
        high = total[:, part * 256 + 128:part * 256 + 256]
        zero = jnp.where(lane < HEAD_SIZE, low, pltpu.roll(high, HEAD_SIZE, 1))
        one = jnp.where(lane < HEAD_SIZE, pltpu.roll(low, HEAD_SIZE, 1), high)
        at = slice(part * 128, part * 128 + 128)
        kept_ref[:, at] = jnp.where(core == 0, zero, one).astype(kept_ref.dtype)
        sent_ref[:rows, at] = jnp.where(core == 0, one, zero).astype(sent_ref.dtype)
    marks = (segs_ref[...] + 1).astype(jnp.float32)
    sent_ref[rows:, :] = jnp.broadcast_to(marks, (MARK_ROWS, rows)).astype(sent_ref.dtype)


def parcel_kernel(scal_ref, segs_ref, kept_ref, received_ref, out_ref):
    core = scal_ref[0]
    rows = kept_ref.shape[0]
    out_ref[block(core, rows), :] = kept_ref[...]
    out_ref[block(1 - core, rows), :] = received_ref[:rows, :]
    own = (segs_ref[...] + 1).astype(jnp.float32)
    other = received_ref[rows:, :].astype(jnp.float32)[0:1, :]
    first, second = jnp.where(core == 0, own, other), jnp.where(core == 0, other, own)
    row = lax.broadcasted_iota(jnp.int32, (MARK_ROWS, rows), 0)
    marks = jnp.where(row == 0, first, jnp.where(row == 1, second, 0.0))
    out_ref[2 * rows:, :] = marks.astype(out_ref.dtype)


def window_kernel(scal_ref, four_ref, two_ref, own_ref, crossed_ref, kt_ref, v_ref, lo_ref):
    odd = scal_ref[1]
    length = own_ref.shape[0]
    count = length - MARK_ROWS
    half = count // 2
    second = pl.multiple_of(odd * length, MARK_ROWS)
    fourth = pl.multiple_of((1 - odd) * length, MARK_ROWS)
    places = [(four_ref, 0), (crossed_ref, second), (two_ref, 0), (crossed_ref, fourth), (own_ref, 0)]
    lane = lax.broadcasted_iota(jnp.int32, (count, 128), 1)
    blank = jnp.zeros((HEAD_SIZE, count), jnp.bfloat16)
    marks = []
    for i, (ref, first) in enumerate(places):
        at = slice(i * count, (i + 1) * count)
        keys = ref[pl.ds(first, count), 0:128].astype(jnp.float32).T.astype(jnp.bfloat16)
        values = ref[pl.ds(first, count), 128:256].astype(jnp.float32)
        turned = pltpu.roll(values, HEAD_SIZE, 1)
        for g in range(2):
            head = keys[g * HEAD_SIZE:(g + 1) * HEAD_SIZE]
            kt_ref[g, 0, :HEAD_SIZE, at] = head
            kt_ref[g, 0, HEAD_SIZE:, at] = blank
            kt_ref[g, 1, :HEAD_SIZE, at] = blank
            kt_ref[g, 1, HEAD_SIZE:, at] = head
            low, high = (values, turned) if g == 0 else (turned, values)
            v_ref[g, 0, at, :] = jnp.where(lane < HEAD_SIZE, low, 0.0).astype(jnp.bfloat16)
            v_ref[g, 1, at, :] = jnp.where(lane < HEAD_SIZE, 0.0, high).astype(jnp.bfloat16)
        found = ref[pl.ds(first + count, MARK_ROWS), :].astype(jnp.float32)
        marks += [found[0:1, :], found[1:2, :]]
    across = lax.broadcasted_iota(jnp.int32, (half, half), 1)
    down = lax.broadcasted_iota(jnp.int32, (half, half), 0)
    for part in range(2):
        mine = jnp.sum(jnp.where(across == down, marks[-2 + part], 0.0), axis=1, keepdims=True)
        earlier = jnp.zeros((half, half), jnp.float32)
        for row in marks:
            earlier = earlier + jnp.where(row < mine, 1.0, 0.0)
        earlier = jnp.sum(earlier, axis=1, keepdims=True).astype(jnp.int32)
        place = lax.broadcasted_iota(jnp.int32, (half, 128), 0) + (part * half + 1)
        lo_ref[part * half:(part + 1) * half, :] = jnp.maximum(earlier, place)


def query_kernel(pieces, g, more, scal_ref, own_ref, other_ref, *refs):
    weights, refs = refs[: len(pieces)], refs[len(pieces):]
    core = scal_ref[0]
    rows = own_ref.shape[0]
    outs = refs[-2:]
    for rows_ref, which in ((own_ref, core), (other_ref, 1 - core)):
        at = block(which, rows)
        for i, column in enumerate((core, 1 - core)):
            total = refs[i][at, :] if more else None
            for (distance, first), weight_ref in zip(pieces, weights):
                depth = weight_ref.shape[0]
                start = pl.multiple_of(scal_ref[2 + distance] * rows + first, depth)
                found = jnp.dot(
                    rows_ref[:, pl.ds(start, depth)], weight_ref[:, block(2 * g + column, GROUP_WIDTH)],
                    preferred_element_type=jnp.float32,
                )
                total = found if total is None else total + found
            outs[i][at, :] = total


def attention_kernel(
    scal_ref, lo_ref, kept_ref, received_ref, kt_ref, v_ref, same_ref, cross_ref, query_ref, score_ref, out_ref
):
    step = pl.program_id(0)
    tile = jnp.where(step == 0, scal_ref[0], 1 - scal_ref[0])
    start = pl.multiple_of(tile * TILE, TILE)
    span = LOOKBACK_SPAN + TILE
    lo = lo_ref[pl.ds(start, TILE), :] - start
    lane = lax.broadcasted_iota(jnp.int32, (TILE, 128), 1)
    row = lax.broadcasted_iota(jnp.int32, (TILE, 128), 0)
    blocks = span // TILE
    queries = (kept_ref[pl.ds(start, TILE), :] + received_ref[pl.ds(start, TILE), :]).astype(jnp.bfloat16)
    query_ref[...] = queries * jnp.bfloat16(HEAD_SIZE ** -0.5)

    def scores_of(pair, parity):
        q = query_ref[:, pair * 128:(pair + 1) * 128]
        peak = jnp.full((TILE, 128), MASKED, jnp.float32)
        for i in range(blocks):
            first = pl.multiple_of(start + i * TILE, TILE)
            found = jnp.dot(q, kt_ref[parity, :, pl.ds(first, TILE)], preferred_element_type=jnp.float32)
            for part in range(TILE // 128):
                at = i * TILE + part * 128
                visible = lane + at >= lo
                if at >= LOOKBACK_SPAN:
                    visible = visible & (lane + (at - LOOKBACK_SPAN) <= row)
                kept = jnp.where(visible, found[:, part * 128:(part + 1) * 128], MASKED)
                peak = jnp.maximum(peak, kept)
                score_ref[parity, :, at:at + 128] = kept
        return jnp.max(peak, axis=1, keepdims=True)

    def mixed_of(parity, peak):
        total = jnp.zeros((TILE, 128), jnp.float32)
        mixed = jnp.zeros((TILE, 128), jnp.float32)
        for i in range(blocks):
            first = pl.multiple_of(start + i * TILE, TILE)
            weights = jnp.exp(score_ref[parity, :, i * TILE:(i + 1) * TILE] - peak)
            for part in range(TILE // 128):
                total = total + weights[:, part * 128:(part + 1) * 128]
            mixed = mixed + jnp.dot(
                weights.astype(jnp.bfloat16), v_ref[parity, pl.ds(first, TILE), :],
                preferred_element_type=jnp.float32,
            )
        return mixed * (1.0 / jnp.sum(total, axis=1, keepdims=True))

    for pair in range(GROUP // 2):
        peaks = [scores_of(pair, parity) for parity in range(2)]
        parts = [mixed_of(parity, peaks[parity]) for parity in range(2)]
        out_ref[:, pair * 128:(pair + 1) * 128] = (parts[0] + parts[1]).astype(out_ref.dtype)

    @pl.when(step == 0)
    def _():
        same_ref[...] = out_ref[...]

    @pl.when(step == 1)
    def _():
        cross_ref[...] = out_ref[...]


def attention(scalars, lo, kept, received, keys_t, values):
    rows = kept.shape[0]
    span = LOOKBACK_SPAN + TILE
    arrays = [lo, kept, received, keys_t, values]
    part = (TILE, GROUP_WIDTH)
    return pl.pallas_call(
        attention_kernel,
        grid=(rows // TILE,),
        in_specs=[pl.BlockSpec(memory_space=pltpu.SMEM)]
        + [pl.BlockSpec(memory_space=pltpu.VMEM)] * len(arrays),
        out_specs=[pl.BlockSpec(memory_space=pltpu.VMEM)] * 2,
        out_shape=[jax.ShapeDtypeStruct(part, jnp.bfloat16)] * 2,
        scratch_shapes=[
            pltpu.VMEM(part, jnp.bfloat16), pltpu.VMEM((2, TILE, span), jnp.float32),
            pltpu.VMEM(part, jnp.bfloat16),
        ],
        compiler_params=pltpu.CompilerParams(vmem_limit_bytes=40 * 1024 * 1024),
        cost_estimate=pl.CostEstimate(flops=1000000, bytes_accessed=100000, transcendentals=0),
    )(scalars, *arrays)


def out_kernel(scal_ref, *refs):
    attended, (weight_ref, add_ref, out_ref) = refs[:4], refs[4:]
    core = scal_ref[0]
    total = add_ref[...].astype(jnp.float32)
    for g in range(2):
        for side, column in enumerate((core, 1 - core)):
            total = total + jnp.dot(
                attended[2 * g + side][...], weight_ref[0, block(2 * g + column, GROUP_WIDTH), :],
                preferred_element_type=jnp.float32,
            )
    out_ref[...] = total.astype(out_ref.dtype)


def projected_out(scalars, attended, weights, add):
    count, depth, columns = weights.shape
    rows = add.shape[0]
    return pl.pallas_call(
        out_kernel,
        grid=(count,),
        in_specs=[pl.BlockSpec(memory_space=pltpu.SMEM)]
        + [pl.BlockSpec(memory_space=pltpu.VMEM)] * len(attended)
        + [
            pl.BlockSpec((1, depth, columns), lambda i: (i, 0, 0)),
            pl.BlockSpec((rows, columns), lambda i: (0, i)),
        ],
        out_specs=pl.BlockSpec((rows, columns), lambda i: (0, i)),
        out_shape=jax.ShapeDtypeStruct(add.shape, add.dtype),
        compiler_params=pltpu.CompilerParams(vmem_limit_bytes=40 * 1024 * 1024),
        cost_estimate=pl.CostEstimate(
            flops=2 * rows * depth * count * columns, bytes_accessed=20 * 1024 * 1024, transcendentals=0
        ),
    )(scalars, *attended, weights, add)


def body(section_input, segment_ids, query_weight, keyval_weight, out_weight):
    hidden = section_input[0]
    rows, width = hidden.shape
    device = lax.axis_index("fsdp")
    chips = lax.axis_size("fsdp") // 2
    chip, core = device // 2, device % 2
    order = jnp.array(ring_order(chips), jnp.int32)
    place = jnp.argmax(order == chip).astype(jnp.int32)
    sources = order[(place + jnp.arange(chips, dtype=jnp.int32)) % chips]
    scalars = jnp.concatenate([jnp.stack([core, chip % 2]).astype(jnp.int32), sources])

    query_pieces = around(query_weight[0])
    keyval_full = lax.all_gather(keyval_weight, "fsdp", axis=1, tiled=True)
    out_full = lax.all_gather(to_next_section(out_weight[0]), "fsdp", axis=0, tiled=False)

    half = ((rows, width // 2), jnp.bfloat16)
    own_rows, sent_rows = run(functools.partial(split_kernel, True), [half, half], scalars, [hidden])
    other_rows = swap_cores(sent_rows)

    kept, sent = run(
        keyval_kernel, [((rows, 256), jnp.bfloat16), ((rows + MARK_ROWS, 256), jnp.bfloat16)],
        scalars, [segment_ids, own_rows, sent_rows, keyval_full],
    )
    parcel, = run(
        parcel_kernel, [((2 * rows + MARK_ROWS, 256), jnp.bfloat16)], scalars,
        [segment_ids, kept, swap_cores(sent)],
    )
    back_two = two_chips_on(parcel)
    back_four = two_chips_on(back_two)
    even = chip % 2 == 0
    crossed = swap_chips(jnp.concatenate([jnp.where(even, parcel, back_four), back_two], axis=0))
    window = 5 * 2 * rows
    keys_t, values, lowest = run(
        window_kernel,
        [((2, 2, 128, window), jnp.bfloat16), ((2, 2, window, 128), jnp.bfloat16), ((2 * rows, 128), jnp.int32)],
        scalars, [back_four, back_two, parcel, crossed],
    )

    def query_sums(distances, g, waits, before=()):
        pieces = [(d, first) for d in distances for first, _ in query_pieces[d]]
        shards = [shard for d in distances for _, shard in query_pieces[d]]
        return run(
            functools.partial(query_kernel, pieces, g, bool(before)),
            [((2 * rows, GROUP_WIDTH), jnp.float32)] * 2, scalars,
            [own_rows, other_rows] + shards + list(before), waits=waits,
        )

    near = [0, 1, chips - 1, 2, chips - 2]
    far = [d for d in range(chips) if d not in near]
    sums = [query_sums(near, g, [parcel]) for g in range(2)]
    sums = [query_sums(far, g, [keys_t], sums[g]) for g in range(2)]
    arrived = []
    for g in range(2):
        same, cross = attention(
            scalars, lowest, sums[g][0], swap_cores(sums[g][1]), keys_t[g], values[g]
        )
        arrived += [to_next_section(same), to_next_section(cross, other_core=True)]
    return projected_out(scalars, arrived, out_full, to_next_section(hidden))[None]


def solution(mesh):
    return jax.shard_map(
        body,
        mesh=mesh,
        in_specs=(
            P("section", "fsdp", None),
            P("section", "fsdp"),
            P("section", "fsdp", None),
            P("section", "fsdp", None),
            P("section", None, "fsdp"),
        ),
        out_specs=P("section", "fsdp", None),
        check_vma=False,
    )
```

time: 318 us -> 308 us (0.969)
  the two profiles are of different devices: /device:TPU:0 before, /device:TPU:27 now
where the time goes in v2:
time: 308 us; the launch traced here: 307 us
  waiting for transfers between devices  161 us (52%)
  Pallas kernels  65.3 us (21%)
  starting transfers between devices  54.4 us (18%)
  between operations  13.7 us (4%)
  local copies, waits for them, and re-layouts  10.2 us (3%)
    ppermute x8, waiting for transfers between devices, along_ring(): return lax.ppermute(value, 'fsdp', pairs)  75.4 us
    ppermute x4, starting transfers between devices, swap_cores(): return lax.ppermute(value, 'fsdp', [(i, i ^ 1) for i in range(count)])  41.5 us
    ppermute x2, waiting for transfers between devices, two_chips_on(): return lax.ppermute(value, 'fsdp', [(i, i + 4) for i in range(count - 4)])  38.3 us
    ppermute x6, waiting for transfers between devices, to_next_section(): return lax.ppermute(value, ('section', 'fsdp'), pairs)  35 us
    pallas_call x2, Pallas kernels, attention(): pl.pallas_call(attention_kernel, grid=(rows // TILE,), in_specs=[pl.Block...  31.8 us
    pallas_call x8, Pallas kernels, run(): pl.pallas_call(only, in_specs=[pl.BlockSpec(memory_space=pltpu.SMEM)] + [...  17.9 us
    pallas_call x1, Pallas kernels, projected_out(): pl.pallas_call(out_kernel, grid=(count,), in_specs=[pl.BlockSpec(memory_s...  15.6 us
    ppermute x1, waiting for transfers between devices, swap_chips(): return lax.ppermute(value, 'fsdp', [(i, i ^ 2) for i in range(count)])  10.4 us
  transfers between devices with their start and end apart: 23, of which 11 were waited for; matrix products, arithmetic and copies ran while one was open for 1% of the time, Pallas kernels for 16%

profile of v2, /device:TPU:27, one launch (start us, length us, event | category | flops | bytes accessed | tf_op | source)
XLA Modules:
  0.0 306.8 jit_solution(7417912990560856870)
XLA Ops:
  7.6 24.1 %collective-permute-done.19 = bf16[2048,256]{1,0:T(8,128)(2,1)S(1)} collective-permute-done((bf16[2048,256]{1,0:T(8,128)(2,1)}, bf16[2048,256]{1,0:T(8,128)(2,1)S(1)}, u32[]{:S(2)}, u32[]{:S(2)}) %collective-permute-start.19) | collective-permute-done | bytes 1048608 | tf_op jit(solution)/shard_map/ppermute | solution.py:47
  34.3 38.6 %collective-permute-done.8.refs_5_ = bf16[256,2048]{1,0:T(8,128)(2,1)S(1)} collective-permute-done((bf16[256,2048]{1,0:T(8,128)(2,1)S(1)}, bf16[256,2048]{1,0:T(8,128)(2,1)S(1)}, u32[]{:S(2)}, u32[]{:S(2)}) %collective-permute-start.8) | collective-permute-done | bytes 1048608 | tf_op jit(solution)/shard_map/ppermute | solution.py:57
  79.4 2.5 copy-done.4
  81.9 1.9 shard_map.65
  83.8 3.0 collective-permute-start
  89.7 18.4 %collective-permute-done.9.refs_7_ = bf16[256,2048]{1,0:T(8,128)(2,1)} collective-permute-done((bf16[256,2048]{1,0:T(8,128)(2,1)S(1)}, bf16[256,2048]{1,0:T(8,128)(2,1)}, u32[]{:S(2)}, u32[]{:S(2)}) %collective-permute-start.9) | collective-permute-done | bytes 1048608 | tf_op jit(solution)/shard_map/ppermute | solution.py:57
  109.5 16.3 %collective-permute-done.1.refs_2_ = bf16[528,256]{1,0:T(8,128)(2,1)} collective-permute-done((bf16[528,256]{1,0:T(8,128)(2,1)S(1)}, bf16[528,256]{1,0:T(8,128)(2,1)}, u32[]{:S(2)}, u32[]{:S(2)}) %collective-permute-start.1) | collective-permute-done | bytes 270368 | tf_op jit(solution)/shard_map/ppermute | solution.py:37
  127.1 15.2 %collective-permute-start.4 = (bf16[256,2048]{1,0:T(8,128)(2,1)}, bf16[256,2048]{1,0:T(8,128)(2,1)S(1)}, u32[]{:S(2)}, u32[]{:S(2)}) collective-permute-start(bf16[256,2048]{1,0:T(8,128)(2,1)} %copy-done.8), channel_id=1, source_target_pairs={{0,1},{1,0},{2,3},{3,2},{4,5},{5,4},{6,7},{7,6},{8,9},{9,8},{10,11... | collective-permute-start | bytes 3145736 | tf_op jit(solution)/shard_map/ppermute | solution.py:27
  142.3 22.0 %collective-permute-done.2.refs_1_ = bf16[528,256]{1,0:T(8,128)(2,1)} collective-permute-done((bf16[528,256]{1,0:T(8,128)(2,1)}, bf16[528,256]{1,0:T(8,128)(2,1)}, u32[]{:S(2)}, u32[]{:S(2)}) %collective-permute-start.2) | collective-permute-done | bytes 270368 | tf_op jit(solution)/shard_map/ppermute | solution.py:37
  168.4 3.4 %shard_map.71 = (f32[512,512]{1,0:T(8,128)S(1)}, f32[512,512]{1,0:T(8,128)S(1)}) custom-call(s32[10]{0:T(128)S(1)} %pad_add_fusion.refs_0_.scal_ref, bf16[256,2048]{1,0:T(8,128)(2,1)S(1)} %get-tuple-element.26.refs_2_.refs_1_, bf16[256,2048]{1,0:T(8,128)(2,1)S(1)} %collective-permute-done.4.refs_2_, bf16[256,2048]{1,0:T(8,128)(2,1)S(1)} %bitcast.19, ...), custom_call_target="tpu_custom_call" | custom-call | flops 1000000 | bytes 100000 | tf_op jit(solution)/shard_map/pallas_call | solution.py:67
  171.8 3.4 %shard_map.68 = (f32[512,512]{1,0:T(8,128)S(1)}, f32[512,512]{1,0:T(8,128)S(1)}) custom-call(s32[10]{0:T(128)S(1)} %pad_add_fusion.refs_0_.scal_ref, bf16[256,2048]{1,0:T(8,128)(2,1)S(1)} %get-tuple-element.26.refs_2_.refs_1_, bf16[256,2048]{1,0:T(8,128)(2,1)S(1)} %collective-permute-done.4.refs_2_, bf16[256,2048]{1,0:T(8,128)(2,1)S(1)} %bitcast.20, ...), custom_call_target="tpu_custom_call" | custom-call | flops 1000000 | bytes 100000 | tf_op jit(solution)/shard_map/pallas_call | solution.py:67
  175.2 10.4 %collective-permute-done.3.refs_4_ = bf16[1056,256]{1,0:T(8,128)(2,1)S(1)} collective-permute-done((bf16[1056,256]{1,0:T(8,128)(2,1)S(1)}, bf16[1056,256]{1,0:T(8,128)(2,1)S(1)}, u32[]{:S(2)}, u32[]{:S(2)}) %collective-permute-start.3) | collective-permute-done | bytes 540704 | tf_op jit(solution)/shard_map/ppermute | solution.py:32
  185.6 2.2 shard_map.67
  187.9 15.5 %collective-permute-done.11.refs_4_ = bf16[128,2048]{1,0:T(8,128)(2,1)S(1)} collective-permute-done((bf16[128,2048]{1,0:T(8,128)(2,1)S(1)}, bf16[128,2048]{1,0:T(8,128)(2,1)S(1)}, u32[]{:S(2)}, u32[]{:S(2)}) %collective-permute-start.11) | collective-permute-done | bytes 524320 | tf_op jit(solution)/shard_map/ppermute | solution.py:57
  203.4 2.9 collective-permute-done.12.refs_5_
  206.3 2.5 shard_map.72
  208.8 23.1 %collective-permute-start.16 = (f32[512,512]{1,0:T(8,128)S(1)}, f32[512,512]{1,0:T(8,128)S(1)}, u32[]{:S(2)}, u32[]{:S(2)}) collective-permute-start(f32[512,512]{1,0:T(8,128)S(1)} %get-tuple-element.42), channel_id=1, source_target_pairs={{0,1},{1,0},{2,3},{3,2},{4,5},{5,4},{6,7},{7,6},{8,9},{9,8},{10,11... | collective-permute-start | bytes 3145736 | tf_op jit(solution)/shard_map/ppermute | solution.py:27
  231.9 2.6 shard_map.69
  235.1 16.0 %shard_map.73 = (bf16[256,512]{1,0:T(8,128)(2,1)S(1)}, bf16[256,512]{1,0:T(8,128)(2,1)S(1)}) custom-call(s32[10]{0:T(128)S(1)} %pad_add_fusion.refs_0_.scal_ref, s32[512,128]{1,0:T(8,128)S(1)} %get-tuple-element.30.lo_ref, f32[512,512]{1,0:T(8,128)S(1)} %get-tuple-element.41.kept_ref, f32[512,512]{1,0:T(8,128)S(1)} %collective-permute-done.16.received_ref, ...), custom_call_target="tpu_custom_call" | custom-call | flops 1000000 | bytes 100000 | tf_op jit(solution)/shard_map/pallas_call | solution.py:276
  251.4 1.8 collective-permute-start.18
  253.2 15.8 %shard_map.70 = (bf16[256,512]{1,0:T(8,128)(2,1)S(1)}, bf16[256,512]{1,0:T(8,128)(2,1)S(1)}) custom-call(s32[10]{0:T(128)S(1)} %pad_add_fusion.refs_0_.scal_ref, s32[512,128]{1,0:T(8,128)S(1)} %get-tuple-element.30.lo_ref, f32[512,512]{1,0:T(8,128)S(1)} %get-tuple-element.34.kept_ref, f32[512,512]{1,0:T(8,128)S(1)} %collective-permute-done.13.received_ref, ...), custom_call_target="tpu_custom_call" | custom-call | flops 1000000 | bytes 100000 | tf_op jit(solution)/shard_map/pallas_call | solution.py:276
  271.8 5.3 %collective-permute-done.14.refs_0_ = bf16[256,512]{1,0:T(8,128)(2,1)S(1)} collective-permute-done((bf16[256,512]{1,0:T(8,128)(2,1)S(1)}, bf16[256,512]{1,0:T(8,128)(2,1)S(1)}, u32[]{:S(2)}, u32[]{:S(2)}) %collective-permute-start.14) | collective-permute-done | bytes 262176 | tf_op jit(solution)/shard_map/ppermute | solution.py:47
  277.1 5.6 %collective-permute-done.15.refs_1_ = bf16[256,512]{1,0:T(8,128)(2,1)S(1)} collective-permute-done((bf16[256,512]{1,0:T(8,128)(2,1)S(1)}, bf16[256,512]{1,0:T(8,128)(2,1)S(1)}, u32[]{:S(2)}, u32[]{:S(2)}) %collective-permute-start.15) | collective-permute-done | bytes 262176 | tf_op jit(solution)/shard_map/ppermute | solution.py:47
  284.4 15.6 %shard_map.74 = bf16[256,4096]{1,0:T(8,128)(2,1)} custom-call(s32[10]{0:T(128)S(1)} %pad_add_fusion.refs_0_.scal_ref, bf16[256,512]{1,0:T(8,128)(2,1)S(1)} %collective-permute-done.14.refs_0_, bf16[256,512]{1,0:T(8,128)(2,1)S(1)} %collective-permute-done.15.refs_1_, bf16[256,512]{1,0:T(8,128)(2,1)S(1)} %collective-permute-done.17.refs_2_, ...), custom_call_target="tpu_custom_call" | custom-call | flops 4294967296 | bytes 20971520 | tf_op jit(solution)/shard_map/pallas_call | solution.py:308
  (70 shorter events, 25.0 us)
Async XLA Ops:
  6.5 67.8 %copy-start.10 = (s32[8]{0:T(128)S(1)}, s32[8]{0:T(128)}, u32[]{:S(2)}) copy-start(s32[8]{0:T(128)} %constant.58.clone) | copy-start | bytes 100
  6.5 72.8 %all-gather.4.cloned.1.call-start = ((), (), s32[]{:S(2)}) async-start(), calls=%async_computation | async-start | bytes 4456448 | tf_op jit(solution)/shard_map/all_gather | solution.py:338
  7.3 275.5 %all-gather.6.cloned.1.call-start = ((), (), s32[]{:S(2)}) async-start(), calls=%async_computation.1 | async-start | bytes 17825792 | tf_op jit(solution)/shard_map/all_gather | solution.py:339
  7.3 24.4 %collective-permute-start.19 = (bf16[2048,256]{1,0:T(8,128)(2,1)}, bf16[2048,256]{1,0:T(8,128)(2,1)S(1)}, u32[]{:S(2)}, u32[]{:S(2)}) collective-permute-start(bf16[2048,256]{1,0:T(8,128)(2,1)} %bitcast.24), channel_id=1, source_target_pairs={{0,16},{1,17},{2,18},{3,19},{4,20},{5,21},{6,22},{7,23},{8,24},{9,... | collective-permute-start | bytes 3145736 | tf_op jit(solution)/shard_map/ppermute | solution.py:47
  32.8 40.1 %collective-permute-start.8 = (bf16[256,2048]{1,0:T(8,128)(2,1)S(1)}, bf16[256,2048]{1,0:T(8,128)(2,1)S(1)}, u32[]{:S(2)}, u32[]{:S(2)}) collective-permute-start(bf16[256,2048]{1,0:T(8,128)(2,1)S(1)} %bitcast.17), channel_id=1, source_target_pairs={{0,4},{1,5},{4,8},{5,9},{8,12},{9,13},{12,14},{13,15},{14,10},{15,... | collective-permute-start | bytes 3145736 | tf_op jit(solution)/shard_map/ppermute | solution.py:57
  34.0 38.9 %collective-permute-start.5 = (bf16[256,2048]{1,0:T(8,128)(2,1)S(1)}, bf16[256,2048]{1,0:T(8,128)(2,1)}, u32[]{:S(2)}, u32[]{:S(2)}) collective-permute-start(bf16[256,2048]{1,0:T(8,128)(2,1)S(1)} %bitcast.18), channel_id=1, source_target_pairs={{0,2},{1,3},{4,0},{5,1},{8,4},{9,5},{12,8},{13,9},{14,12},{15,13},... | collective-permute-start | bytes 3145736 | tf_op jit(solution)/shard_map/ppermute | solution.py:57
  72.9 35.2 %collective-permute-start.9 = (bf16[256,2048]{1,0:T(8,128)(2,1)S(1)}, bf16[256,2048]{1,0:T(8,128)(2,1)}, u32[]{:S(2)}, u32[]{:S(2)}) collective-permute-start(bf16[256,2048]{1,0:T(8,128)(2,1)S(1)} %collective-permute-done.8.refs_5_), channel_id=1, source_target_pairs={{0,4},{1,5},{4,8},{5,9},{8,12},{9,13},{12,14},{13,15},{14,10},{15,... | collective-permute-start | bytes 3145736 | tf_op jit(solution)/shard_map/ppermute | solution.py:57
  72.9 35.2 %collective-permute-start.6 = (bf16[256,2048]{1,0:T(8,128)(2,1)}, bf16[256,2048]{1,0:T(8,128)(2,1)}, u32[]{:S(2)}, u32[]{:S(2)}) collective-permute-start(bf16[256,2048]{1,0:T(8,128)(2,1)} %collective-permute-done.5.refs_4_), channel_id=1, source_target_pairs={{0,2},{1,3},{4,0},{5,1},{8,4},{9,5},{12,8},{13,9},{14,12},{15,13},... | collective-permute-start | bytes 3145736 | tf_op jit(solution)/shard_map/ppermute | solution.py:57
  83.8 4.0 %collective-permute-start = (bf16[272,256]{1,0:T(8,128)(2,1)S(1)}, bf16[272,256]{1,0:T(8,128)(2,1)S(1)}, u32[]{:S(2)}, u32[]{:S(2)}) collective-permute-start(bf16[272,256]{1,0:T(8,128)(2,1)S(1)} %get-tuple-element.29), channel_id=1, source_target_pairs={{0,1},{1,0},{2,3},{3,2},{4,5},{5,4},{6,7},{7,6},{8,9},{9,8},{10,11... | collective-permute-start | bytes 417800 | tf_op jit(solution)/shard_map/ppermute | solution.py:27
  88.4 37.4 %collective-permute-start.1 = (bf16[528,256]{1,0:T(8,128)(2,1)S(1)}, bf16[528,256]{1,0:T(8,128)(2,1)}, u32[]{:S(2)}, u32[]{:S(2)}) collective-permute-start(bf16[528,256]{1,0:T(8,128)(2,1)S(1)} %shard_map.66.refs_3_.refs_8_), channel_id=1, source_target_pairs={{0,4},{1,5},{2,6},{3,7},{4,8},{5,9},{6,10},{7,11},{8,12},{9,13},{1... | collective-permute-start | bytes 811016 | tf_op jit(solution)/shard_map/ppermute | solution.py:37
  108.1 57.4 %collective-permute-start.10 = (bf16[256,2048]{1,0:T(8,128)(2,1)}, bf16[256,2048]{1,0:T(8,128)(2,1)S(1)}, u32[]{:S(2)}, u32[]{:S(2)}) collective-permute-start(bf16[256,2048]{1,0:T(8,128)(2,1)} %collective-permute-done.9.refs_7_), channel_id=1, source_target_pairs={{0,4},{1,5},{4,8},{5,9},{8,12},{9,13},{12,14},{13,15},{14,10},{15,... | collective-permute-start | bytes 3145736 | tf_op jit(solution)/shard_map/ppermute | solution.py:57
  108.1 59.0 %collective-permute-start.7 = (bf16[256,2048]{1,0:T(8,128)(2,1)}, bf16[256,2048]{1,0:T(8,128)(2,1)}, u32[]{:S(2)}, u32[]{:S(2)}) collective-permute-start(bf16[256,2048]{1,0:T(8,128)(2,1)} %collective-permute-done.6.refs_6_), channel_id=1, source_target_pairs={{0,2},{1,3},{4,0},{5,1},{8,4},{9,5},{12,8},{13,9},{14,12},{15,13},... | collective-permute-start | bytes 3145736 | tf_op jit(solution)/shard_map/ppermute | solution.py:57
  125.8 38.5 %collective-permute-start.2 = (bf16[528,256]{1,0:T(8,128)(2,1)}, bf16[528,256]{1,0:T(8,128)(2,1)}, u32[]{:S(2)}, u32[]{:S(2)}) collective-permute-start(bf16[528,256]{1,0:T(8,128)(2,1)} %collective-permute-done.1.refs_2_), channel_id=1, source_target_pairs={{0,4},{1,5},{2,6},{3,7},{4,8},{5,9},{6,10},{7,11},{8,12},{9,13},{1... | collective-permute-start | bytes 811016 | tf_op jit(solution)/shard_map/ppermute | solution.py:37
  127.1 41.3 %collective-permute-start.4 = (bf16[256,2048]{1,0:T(8,128)(2,1)}, bf16[256,2048]{1,0:T(8,128)(2,1)S(1)}, u32[]{:S(2)}, u32[]{:S(2)}) collective-permute-start(bf16[256,2048]{1,0:T(8,128)(2,1)} %copy-done.8), channel_id=1, source_target_pairs={{0,1},{1,0},{2,3},{3,2},{4,5},{5,4},{6,7},{7,6},{8,9},{9,8},{10,11... | collective-permute-start | bytes 3145736 | tf_op jit(solution)/shard_map/ppermute | solution.py:27
  165.4 20.2 %collective-permute-start.3 = (bf16[1056,256]{1,0:T(8,128)(2,1)S(1)}, bf16[1056,256]{1,0:T(8,128)(2,1)S(1)}, u32[]{:S(2)}, u32[]{:S(2)}) collective-permute-start(bf16[1056,256]{1,0:T(8,128)(2,1)S(1)} %pad_maximum_fusion), channel_id=1, source_target_pairs={{0,2},{1,3},{2,0},{3,1},{4,6},{5,7},{6,4},{7,5},{8,10},{9,11},{10,... | collective-permute-start | bytes 1622024 | tf_op jit(solution)/shard_map/ppermute | solution.py:32
  165.5 37.9 %collective-permute-start.11 = (bf16[128,2048]{1,0:T(8,128)(2,1)S(1)}, bf16[128,2048]{1,0:T(8,128)(2,1)S(1)}, u32[]{:S(2)}, u32[]{:S(2)}) collective-permute-start(bf16[128,2048]{1,0:T(8,128)(2,1)S(1)} %slice.26), channel_id=1, source_target_pairs={{0,4},{1,5},{4,8},{5,9},{8,12},{9,13},{12,14},{13,15},{14,10},{15,... | collective-permute-start | bytes 1572872 | tf_op jit(solution)/shard_map/ppermute | solution.py:57
  168.1 38.2 %collective-permute-start.12 = (bf16[128,2048]{1,0:T(8,128)(2,1)S(1)}, bf16[128,2048]{1,0:T(8,128)(2,1)S(1)}, u32[]{:S(2)}, u32[]{:S(2)}) collective-permute-start(bf16[128,2048]{1,0:T(8,128)(2,1)S(1)} %slice.27), channel_id=1, source_target_pairs={{0,2},{1,3},{4,0},{5,1},{8,4},{9,5},{12,8},{13,9},{14,12},{15,13},... | collective-permute-start | bytes 1572872 | tf_op jit(solution)/shard_map/ppermute | solution.py:57
  168.2 102.3 %collective-permute-start.20 = (bf16[256,4096]{1,0:T(8,128)(2,1)}, bf16[256,4096]{1,0:T(8,128)(2,1)S(1)}, u32[]{:S(2)}, u32[]{:S(2)}) collective-permute-start(bf16[256,4096]{1,0:T(8,128)(2,1)} %bitcast.21), channel_id=1, source_target_pairs={{0,16},{1,17},{2,18},{3,19},{4,20},{5,21},{6,22},{7,23},{8,24},{9,... | collective-permute-start | bytes 6291464 | tf_op jit(solution)/shard_map/ppermute | solution.py:47
  208.8 26.3 %collective-permute-start.16 = (f32[512,512]{1,0:T(8,128)S(1)}, f32[512,512]{1,0:T(8,128)S(1)}, u32[]{:S(2)}, u32[]{:S(2)}) collective-permute-start(f32[512,512]{1,0:T(8,128)S(1)} %get-tuple-element.42), channel_id=1, source_target_pairs={{0,1},{1,0},{2,3},{3,2},{4,5},{5,4},{6,7},{7,6},{8,9},{9,8},{10,11... | collective-permute-start | bytes 3145736 | tf_op jit(solution)/shard_map/ppermute | solution.py:27
  234.6 18.7 %collective-permute-start.13 = (f32[512,512]{1,0:T(8,128)S(1)}, f32[512,512]{1,0:T(8,128)S(1)}, u32[]{:S(2)}, u32[]{:S(2)}) collective-permute-start(f32[512,512]{1,0:T(8,128)S(1)} %get-tuple-element.35), channel_id=1, source_target_pairs={{0,1},{1,0},{2,3},{3,2},{4,5},{5,4},{6,7},{7,6},{8,9},{9,8},{10,11... | collective-permute-start | bytes 3145736 | tf_op jit(solution)/shard_map/ppermute | solution.py:27
  251.1 20.8 %collective-permute-start.17 = (bf16[256,512]{1,0:T(8,128)(2,1)S(1)}, bf16[256,512]{1,0:T(8,128)(2,1)S(1)}, u32[]{:S(2)}, u32[]{:S(2)}) collective-permute-start(bf16[256,512]{1,0:T(8,128)(2,1)S(1)} %get-tuple-element.43), channel_id=1, source_target_pairs={{0,16},{1,17},{2,18},{3,19},{4,20},{5,21},{6,22},{7,23},{8,24},{9,... | collective-permute-start | bytes 786440 | tf_op jit(solution)/shard_map/ppermute | solution.py:47
  251.4 20.5 %collective-permute-start.18 = (bf16[256,512]{1,0:T(8,128)(2,1)S(1)}, bf16[256,512]{1,0:T(8,128)(2,1)S(1)}, u32[]{:S(2)}, u32[]{:S(2)}) collective-permute-start(bf16[256,512]{1,0:T(8,128)(2,1)S(1)} %get-tuple-element.44), channel_id=1, source_target_pairs={{0,17},{1,16},{2,19},{3,18},{4,21},{5,20},{6,23},{7,22},{8,25},{9,... | collective-permute-start | bytes 786440 | tf_op jit(solution)/shard_map/ppermute | solution.py:47
  269.0 8.1 %collective-permute-start.14 = (bf16[256,512]{1,0:T(8,128)(2,1)S(1)}, bf16[256,512]{1,0:T(8,128)(2,1)S(1)}, u32[]{:S(2)}, u32[]{:S(2)}) collective-permute-start(bf16[256,512]{1,0:T(8,128)(2,1)S(1)} %get-tuple-element.37), channel_id=1, source_target_pairs={{0,16},{1,17},{2,18},{3,19},{4,20},{5,21},{6,22},{7,23},{8,24},{9,... | collective-permute-start | bytes 786440 | tf_op jit(solution)/shard_map/ppermute | solution.py:47
  269.2 13.5 %collective-permute-start.15 = (bf16[256,512]{1,0:T(8,128)(2,1)S(1)}, bf16[256,512]{1,0:T(8,128)(2,1)S(1)}, u32[]{:S(2)}, u32[]{:S(2)}) collective-permute-start(bf16[256,512]{1,0:T(8,128)(2,1)S(1)} %get-tuple-element.38), channel_id=1, source_target_pairs={{0,17},{1,16},{2,19},{3,18},{4,21},{5,20},{6,23},{7,22},{8,25},{9,... | collective-permute-start | bytes 786440 | tf_op jit(solution)/shard_map/ppermute | solution.py:47
  (11 other events, 55.0 us)
Sparse Core Ops, SparseCore 0:
  9.5 63.5 all-gather.3
  75.3 177.8 all-gather.5

commit v3 on v2

--- a/solution.py
+++ b/solution.py
@@ -37,14 +37,9 @@
     return lax.ppermute(value, "fsdp", [(i, i + 4) for i in range(count - 4)])
 
 
-def to_next_section(value, other_core=False):
-    sections, count = lax.axis_size("section"), lax.axis_size("fsdp")
-    pairs = []
-    for section in range(sections):
-        for i in range(count):
-            target = i ^ 1 if other_core else i
-            pairs.append((section * count + i, (section + 1) % sections * count + target))
-    return lax.ppermute(value, ("section", "fsdp"), pairs)
+def to_next_section(value):
+    count = lax.axis_size("section")
+    return lax.ppermute(value, "section", [(i, (i + 1) % count) for i in range(count)])
 
 
 def along_ring(value, step):
@@ -75,6 +70,22 @@
         compiler_params=pltpu.CompilerParams(vmem_limit_bytes=40 * 1024 * 1024),
         cost_estimate=pl.CostEstimate(flops=1000000, bytes_accessed=100000, transcendentals=0),
     )(scalars, *arrays, *waits)
+
+
+def tied_kernel(*refs):
+    pass
+
+
+def after(value, *others):
+    anywhere = pl.BlockSpec(memory_space=pl.ANY)
+    return pl.pallas_call(
+        tied_kernel,
+        in_specs=[anywhere] * (1 + len(others)),
+        out_specs=anywhere,
+        out_shape=jax.ShapeDtypeStruct(value.shape, value.dtype),
+        input_output_aliases={0: 0},
+        cost_estimate=pl.CostEstimate(flops=0, bytes_accessed=0, transcendentals=0),
+    )(value, *others)
 
 
 def around(shard):
@@ -210,18 +221,15 @@
             outs[i][at, :] = total
 
 
-def attention_kernel(
-    scal_ref, lo_ref, kept_ref, received_ref, kt_ref, v_ref, same_ref, cross_ref, query_ref, score_ref, out_ref
-):
-    step = pl.program_id(0)
-    tile = jnp.where(step == 0, scal_ref[0], 1 - scal_ref[0])
+def attention_kernel(lo_ref, kept_ref, received_ref, kt_ref, v_ref, out_ref, query_ref, score_ref):
+    tile = pl.program_id(0)
     start = pl.multiple_of(tile * TILE, TILE)
     span = LOOKBACK_SPAN + TILE
-    lo = lo_ref[pl.ds(start, TILE), :] - start
+    lo = lo_ref[...] - start
     lane = lax.broadcasted_iota(jnp.int32, (TILE, 128), 1)
     row = lax.broadcasted_iota(jnp.int32, (TILE, 128), 0)
     blocks = span // TILE
-    queries = (kept_ref[pl.ds(start, TILE), :] + received_ref[pl.ds(start, TILE), :]).astype(jnp.bfloat16)
+    queries = (kept_ref[...] + received_ref[...]).astype(jnp.bfloat16)
     query_ref[...] = queries * jnp.bfloat16(HEAD_SIZE ** -0.5)
 
     def scores_of(pair, parity):
@@ -259,68 +267,79 @@
         parts = [mixed_of(parity, peaks[parity]) for parity in range(2)]
         out_ref[:, pair * 128:(pair + 1) * 128] = (parts[0] + parts[1]).astype(out_ref.dtype)
 
-    @pl.when(step == 0)
-    def _():
-        same_ref[...] = out_ref[...]
-
-    @pl.when(step == 1)
-    def _():
-        cross_ref[...] = out_ref[...]
-
-
-def attention(scalars, lo, kept, received, keys_t, values):
+
+def attention(lo, kept, received, keys_t, values, waits):
     rows = kept.shape[0]
+    window = keys_t.shape[2]
     span = LOOKBACK_SPAN + TILE
-    arrays = [lo, kept, received, keys_t, values]
-    part = (TILE, GROUP_WIDTH)
+
+    def only(*refs):
+        attention_kernel(*refs[:5], *refs[5 + len(waits):])
+
     return pl.pallas_call(
-        attention_kernel,
+        only,
         grid=(rows // TILE,),
-        in_specs=[pl.BlockSpec(memory_space=pltpu.SMEM)]
-        + [pl.BlockSpec(memory_space=pltpu.VMEM)] * len(arrays),
-        out_specs=[pl.BlockSpec(memory_space=pltpu.VMEM)] * 2,
-        out_shape=[jax.ShapeDtypeStruct(part, jnp.bfloat16)] * 2,
+        in_specs=[
+            pl.BlockSpec((TILE, 128), lambda t: (t, 0)),
+            pl.BlockSpec((TILE, GROUP_WIDTH), lambda t: (t, 0)),
+            pl.BlockSpec((TILE, GROUP_WIDTH), lambda t: (t, 0)),
+            pl.BlockSpec((2, 128, window), lambda t: (0, 0, 0)),
+            pl.BlockSpec((2, window, 128), lambda t: (0, 0, 0)),
+        ] + [pl.BlockSpec(memory_space=pl.ANY)] * len(waits),
+        out_specs=pl.BlockSpec((TILE, GROUP_WIDTH), lambda t: (t, 0)),
+        out_shape=jax.ShapeDtypeStruct((rows, GROUP_WIDTH), jnp.bfloat16),
         scratch_shapes=[
-            pltpu.VMEM(part, jnp.bfloat16), pltpu.VMEM((2, TILE, span), jnp.float32),
-            pltpu.VMEM(part, jnp.bfloat16),
+            pltpu.VMEM((TILE, GROUP_WIDTH), jnp.bfloat16), pltpu.VMEM((2, TILE, span), jnp.float32)
         ],
         compiler_params=pltpu.CompilerParams(vmem_limit_bytes=40 * 1024 * 1024),
         cost_estimate=pl.CostEstimate(flops=1000000, bytes_accessed=100000, transcendentals=0),
-    )(scalars, *arrays)
-
-
-def out_kernel(scal_ref, *refs):
-    attended, (weight_ref, add_ref, out_ref) = refs[:4], refs[4:]
-    core = scal_ref[0]
-    total = add_ref[...].astype(jnp.float32)
-    for g in range(2):
-        for side, column in enumerate((core, 1 - core)):
-            total = total + jnp.dot(
-                attended[2 * g + side][...], weight_ref[0, block(2 * g + column, GROUP_WIDTH), :],
-                preferred_element_type=jnp.float32,
-            )
-    out_ref[...] = total.astype(out_ref.dtype)
-
-
-def projected_out(scalars, attended, weights, add):
-    count, depth, columns = weights.shape
-    rows = add.shape[0]
-    return pl.pallas_call(
-        out_kernel,
-        grid=(count,),
-        in_specs=[pl.BlockSpec(memory_space=pltpu.SMEM)]
-        + [pl.BlockSpec(memory_space=pltpu.VMEM)] * len(attended)
-        + [
-            pl.BlockSpec((1, depth, columns), lambda i: (i, 0, 0)),
-            pl.BlockSpec((rows, columns), lambda i: (0, i)),
-        ],
-        out_specs=pl.BlockSpec((rows, columns), lambda i: (0, i)),
-        out_shape=jax.ShapeDtypeStruct(add.shape, add.dtype),
-        compiler_params=pltpu.CompilerParams(vmem_limit_bytes=40 * 1024 * 1024),
-        cost_estimate=pl.CostEstimate(
-            flops=2 * rows * depth * count * columns, bytes_accessed=20 * 1024 * 1024, transcendentals=0
-        ),
-    )(scalars, *attended, weights, add)
+    )(lo, kept, received, keys_t, values, *waits)
+
+
+def out_kernel(distances, mode, scal_ref, *refs):
+    attended, refs = refs[:4], refs[4:]
+    adds, refs = refs[:2], refs[2:]
+    count = sum(len(pieces) for _, pieces in distances)
+    weights, refs = refs[:count], refs[count:]
+    outs = refs[-2:]
+    core = scal_ref[0]
+    rows = adds[0].shape[0]
+    depth = attended[0].shape[1]
+    if mode != "alone":
+        for i in range(2):
+            outs[i][...] = refs[i][...] if mode == "more" else jnp.zeros_like(outs[i])
+    for i, which in enumerate((core, 1 - core)):
+        taken = 0
+        for distance, pieces in distances:
+            shard = weights[taken:taken + len(pieces)]
+            taken += len(pieces)
+            columns = shard[0].shape[1]
+            at = block(scal_ref[2 + distance], columns)
+            total = adds[i][:, at].astype(jnp.float32)
+            for g in range(2):
+                ref, first = shard[g * len(shard) // 2], 2 * g if len(shard) == 1 else 0
+                for side, column in enumerate((core, 1 - core)):
+                    total = total + jnp.dot(
+                        attended[2 * g + side][block(which, rows), :],
+                        ref[block(first + column, depth), :],
+                        preferred_element_type=jnp.float32,
+                    )
+            if mode == "alone":
+                outs[i][...] = total.astype(outs[i].dtype)
+            else:
+                outs[i][:, at] = total.astype(outs[i].dtype)
+
+
+def join_kernel(last, scal_ref, own_ref, other_ref, own_last_ref, other_last_ref, out_ref):
+    core = scal_ref[0]
+    size = own_last_ref.shape[1]
+    for j in range(own_ref.shape[1] // size):
+        at = slice(j * size, (j + 1) * size)
+        out_ref[:, block(2 * j + core, size)] = own_ref[:, at]
+        out_ref[:, block(2 * j + 1 - core, size)] = other_ref[:, at]
+    j = scal_ref[2 + last]
+    out_ref[:, block(2 * j + core, size)] = own_last_ref[...]
+    out_ref[:, block(2 * j + 1 - core, size)] = other_last_ref[...]
 
 
 def body(section_input, segment_ids, query_weight, keyval_weight, out_weight):
@@ -336,11 +355,11 @@
 
     query_pieces = around(query_weight[0])
     keyval_full = lax.all_gather(keyval_weight, "fsdp", axis=1, tiled=True)
-    out_full = lax.all_gather(to_next_section(out_weight[0]), "fsdp", axis=0, tiled=False)
 
     half = ((rows, width // 2), jnp.bfloat16)
     own_rows, sent_rows = run(functools.partial(split_kernel, True), [half, half], scalars, [hidden])
     other_rows = swap_cores(sent_rows)
+    out_shard = to_next_section(after(out_weight[0], own_rows))
 
     kept, sent = run(
         keyval_kernel, [((rows, 256), jnp.bfloat16), ((rows + MARK_ROWS, 256), jnp.bfloat16)],
@@ -371,16 +390,45 @@
         )
 
     near = [0, 1, chips - 1, 2, chips - 2]
-    far = [d for d in range(chips) if d not in near]
+    next_far = [3, chips - 3]
+    far = [chips // 2]
+    out_shard = after(out_shard, query_pieces[3][0][1], query_pieces[chips - 3][0][1])
+    out_pieces = around(out_shard)
     sums = [query_sums(near, g, [parcel]) for g in range(2)]
-    sums = [query_sums(far, g, [keys_t], sums[g]) for g in range(2)]
+    sums = [query_sums(next_far + far, g, [keys_t, out_shard], sums[g]) for g in range(2)]
+    attended = []
+    for g in range(2):
+        waits = [out_pieces[d][0][1] for d in (1, chips - 1)] if g else []
+        attended.append(attention(lowest, sums[g][0], swap_cores(sums[g][1]), keys_t[g], values[g], waits))
+    attended[1] = after(attended[1], *[out_pieces[d][0][1] for d in (2, chips - 2)])
+    kept, sent = run(
+        functools.partial(split_kernel, False), [half, half], scalars, [to_next_section(hidden)]
+    )
+    adds = [kept, swap_cores(sent)]
     arrived = []
     for g in range(2):
-        same, cross = attention(
-            scalars, lowest, sums[g][0], swap_cores(sums[g][1]), keys_t[g], values[g]
+        mine = to_next_section(attended[g])
+        arrived += [mine, swap_cores(mine)]
+
+    def made(some, mode, before=()):
+        distances = [(d, [first for first, _ in out_pieces[d]]) for d in some]
+        shards = [shard for d in some for _, shard in out_pieces[d]]
+        outs = [((rows, out_shard.shape[1]), jnp.bfloat16)] * 2 if mode == "alone" else [half, half]
+        taken = arrived + adds + shards
+        aliases = {1 + len(taken) + i: i for i in range(2)} if before else {}
+        return run(
+            functools.partial(out_kernel, distances, mode), outs, scalars, taken + list(before), aliases=aliases
         )
-        arrived += [to_next_section(same), to_next_section(cross, other_core=True)]
-    return projected_out(scalars, arrived, out_full, to_next_section(hidden))[None]
+
+    most = made(near, "first")
+    most = made(next_far, "more", most)
+    other_most = swap_cores(most[1])
+    last = made(far, "alone")
+    joined, = run(
+        functools.partial(join_kernel, chips // 2), [((rows, width), jnp.bfloat16)], scalars,
+        [most[0], other_most, last[0], swap_cores(last[1])],
+    )
+    return joined[None]
 
 
 def solution(mesh):

time: 308 us -> 267 us (0.87)
  the two profiles are of different devices: /device:TPU:27 before, /device:TPU:0 now
where the time goes in v3:
time: 267 us; the launch traced here: 266 us
  waiting for transfers between devices  139 us (52%)
  Pallas kernels  66.6 us (25%)
  starting transfers between devices  32.7 us (12%)
  between operations  13.7 us (5%)
  local copies, waits for them, and re-layouts  12.1 us (5%)
    ppermute x16, waiting for transfers between devices, along_ring(): return lax.ppermute(value, 'fsdp', pairs)  93 us
    pallas_call x13, Pallas kernels, run(): pl.pallas_call(only, in_specs=[pl.BlockSpec(memory_space=pltpu.SMEM)] + [...  35.3 us
    pallas_call x2, Pallas kernels, attention(): pl.pallas_call(only, grid=(rows // TILE,), in_specs=[pl.BlockSpec((TILE,...  31.2 us
    ppermute x2, waiting for transfers between devices, two_chips_on(): return lax.ppermute(value, 'fsdp', [(i, i + 4) for i in range(count - 4)])  21.1 us
    ppermute x16, starting transfers between devices, along_ring(): return lax.ppermute(value, 'fsdp', pairs)  16.7 us
    ppermute x4, waiting for transfers between devices, to_next_section(): lax.ppermute(value, 'section', [(i, (i + 1) % count) for i in range(count)])  11.3 us
    ppermute x2, starting transfers between devices, two_chips_on(): return lax.ppermute(value, 'fsdp', [(i, i + 4) for i in range(count - 4)])  9.35 us
    ppermute x1, waiting for transfers between devices, swap_chips(): return lax.ppermute(value, 'fsdp', [(i, i ^ 2) for i in range(count)])  8.97 us
  transfers between devices with their start and end apart: 33, of which 15 were waited for; matrix products, arithmetic and copies ran while one was open for 2% of the time, Pallas kernels for 23%

profile of v3, /device:TPU:0, one launch (start us, length us, event | category | flops | bytes accessed | tf_op | source)
XLA Modules:
  0.0 266.4 jit_solution(12755314360128384720)
XLA Ops:
  8.9 3.0 %collective-permute-start.5 = (bf16[256,2048]{1,0:T(8,128)(2,1)S(1)}, bf16[256,2048]{1,0:T(8,128)(2,1)S(1)}, u32[]{:S(2)}, u32[]{:S(2)}) collective-permute-start(bf16[256,2048]{1,0:T(8,128)(2,1)S(1)} %bitcast.16), channel_id=1, source_target_pairs={{0,2},{1,3},{4,0},{5,1},{8,4},{9,5},{12,8},{13,9},{14,12},{15,13},... | collective-permute-start | bytes 3145736 | tf_op jit(solution)/shard_map/ppermute | solution.py:52
  12.1 31.5 %collective-permute-done.5.refs_4_ = bf16[256,2048]{1,0:T(8,128)(2,1)S(1)} collective-permute-done((bf16[256,2048]{1,0:T(8,128)(2,1)S(1)}, bf16[256,2048]{1,0:T(8,128)(2,1)S(1)}, u32[]{:S(2)}, u32[]{:S(2)}) %collective-permute-start.5) | collective-permute-done | bytes 1048608 | tf_op jit(solution)/shard_map/ppermute | solution.py:52
  54.5 30.4 %collective-permute-done.6.refs_6_ = bf16[256,2048]{1,0:T(8,128)(2,1)} collective-permute-done((bf16[256,2048]{1,0:T(8,128)(2,1)S(1)}, bf16[256,2048]{1,0:T(8,128)(2,1)}, u32[]{:S(2)}, u32[]{:S(2)}) %collective-permute-start.6) | collective-permute-done | bytes 1048608 | tf_op jit(solution)/shard_map/ppermute | solution.py:52
  89.1 2.6 shard_map.65
  93.7 4.1 %collective-permute-start.1 = (bf16[528,256]{1,0:T(8,128)(2,1)S(1)}, bf16[528,256]{1,0:T(8,128)(2,1)}, u32[]{:S(2)}, u32[]{:S(2)}) collective-permute-start(bf16[528,256]{1,0:T(8,128)(2,1)S(1)} %shard_map.66.refs_3_.refs_8_), channel_id=1, source_target_pairs={{0,4},{1,5},{2,6},{3,7},{4,8},{5,9},{6,10},{7,11},{8,12},{9,13},{1... | collective-permute-start | bytes 811016 | tf_op jit(solution)/shard_map/ppermute | solution.py:37
  97.8 16.7 %collective-permute-done.1.refs_2_ = bf16[528,256]{1,0:T(8,128)(2,1)} collective-permute-done((bf16[528,256]{1,0:T(8,128)(2,1)S(1)}, bf16[528,256]{1,0:T(8,128)(2,1)}, u32[]{:S(2)}, u32[]{:S(2)}) %collective-permute-start.1) | collective-permute-done | bytes 270368 | tf_op jit(solution)/shard_map/ppermute | solution.py:37
  114.6 5.2 %collective-permute-start.2 = (bf16[528,256]{1,0:T(8,128)(2,1)}, bf16[528,256]{1,0:T(8,128)(2,1)}, u32[]{:S(2)}, u32[]{:S(2)}) collective-permute-start(bf16[528,256]{1,0:T(8,128)(2,1)} %collective-permute-done.1.refs_2_), channel_id=1, source_target_pairs={{0,4},{1,5},{2,6},{3,7},{4,8},{5,9},{6,10},{7,11},{8,12},{9,13},{1... | collective-permute-start | bytes 811016 | tf_op jit(solution)/shard_map/ppermute | solution.py:37
  121.9 4.4 %collective-permute-done.2.refs_1_ = bf16[528,256]{1,0:T(8,128)(2,1)} collective-permute-done((bf16[528,256]{1,0:T(8,128)(2,1)}, bf16[528,256]{1,0:T(8,128)(2,1)}, u32[]{:S(2)}, u32[]{:S(2)}) %collective-permute-start.2) | collective-permute-done | bytes 270368 | tf_op jit(solution)/shard_map/ppermute | solution.py:37
  131.2 2.5 collective-permute-start.11
  133.8 2.9 %shard_map.77 = (bf16[256,2048]{1,0:T(8,128)(2,1)S(1)}, bf16[256,2048]{1,0:T(8,128)(2,1)}) custom-call(s32[10]{0:T(128)S(1)} %pad_add_fusion.refs_0_, bf16[256,4096]{1,0:T(8,128)(2,1)} %collective-permute-done.24.refs_1_), custom_call_target="tpu_custom_call" | custom-call | flops 1000000 | bytes 100000 | tf_op jit(solution)/shard_map/pallas_call | solution.py:62
  137.6 3.4 %shard_map.68 = (f32[512,512]{1,0:T(8,128)S(1)}, f32[512,512]{1,0:T(8,128)S(1)}) custom-call(s32[10]{0:T(128)S(1)} %pad_add_fusion.refs_0_, bf16[256,2048]{1,0:T(8,128)(2,1)S(1)} %copy-done.1, bf16[256,2048]{1,0:T(8,128)(2,1)S(1)} %collective-permute-done.4.refs_2_, bf16[256,2048]{1,0:T(8,128)(2,1)S(1)} %bitcast.18, bf16[256,2048]{1,0:T(8,128)(2,1)S(1)} %copy-done.9, ...), custom_call_target="tpu_custom_call" | custom-call | flops 1000000 | bytes 100000 | tf_op jit(solution)/shard_map/pallas_call | solution.py:62
  141.0 3.4 %shard_map.73 = (f32[512,512]{1,0:T(8,128)S(1)}, f32[512,512]{1,0:T(8,128)S(1)}) custom-call(s32[10]{0:T(128)S(1)} %pad_add_fusion.refs_0_, bf16[256,2048]{1,0:T(8,128)(2,1)S(1)} %copy-done.1, bf16[256,2048]{1,0:T(8,128)(2,1)S(1)} %collective-permute-done.4.refs_2_, bf16[256,2048]{1,0:T(8,128)(2,1)S(1)} %bitcast.19, bf16[256,2048]{1,0:T(8,128)(2,1)S(1)} %copy-done.9, ...), custom_call_target="tpu_custom_call" | custom-call | flops 1000000 | bytes 100000 | tf_op jit(solution)/shard_map/pallas_call | solution.py:62
  146.3 2.5 collective-permute-done.19.refs_6_.refs_9_
  149.4 9.0 %collective-permute-done.3.refs_4_ = bf16[1056,256]{1,0:T(8,128)(2,1)S(1)} collective-permute-done((bf16[1056,256]{1,0:T(8,128)(2,1)S(1)}, bf16[1056,256]{1,0:T(8,128)(2,1)S(1)}, u32[]{:S(2)}, u32[]{:S(2)}) %collective-permute-start.3) | collective-permute-done | bytes 540704 | tf_op jit(solution)/shard_map/ppermute | solution.py:32
  160.7 9.0 %collective-permute-done.11.refs_5_ = bf16[128,2048]{1,0:T(8,128)(2,1)S(1)} collective-permute-done((bf16[128,2048]{1,0:T(8,128)(2,1)S(1)}, bf16[128,2048]{1,0:T(8,128)(2,1)S(1)}, u32[]{:S(2)}, u32[]{:S(2)}) %collective-permute-start.11) | collective-permute-done | bytes 524320 | tf_op jit(solution)/shard_map/ppermute | solution.py:52
  169.7 2.8 %shard_map.71 = (f32[512,512]{1,0:T(8,128)S(1)}, f32[512,512]{1,0:T(8,128)S(1)}) custom-call(s32[10]{0:T(128)S(1)} %pad_add_fusion.refs_0_, bf16[256,2048]{1,0:T(8,128)(2,1)S(1)} %copy-done.1, bf16[256,2048]{1,0:T(8,128)(2,1)S(1)} %collective-permute-done.4.refs_2_, bf16[256,2048]{1,0:T(8,128)(2,1)} %collective-permute-done.7.refs_1_.refs_3_, ...), custom_call_target="tpu_custom_call" | custom-call | flops 1000000 | bytes 100000 | tf_op jit(solution)/shard_map/pallas_call | solution.py:62
  172.6 2.8 %shard_map.74 = (f32[512,512]{1,0:T(8,128)S(1)}, f32[512,512]{1,0:T(8,128)S(1)}) custom-call(s32[10]{0:T(128)S(1)} %pad_add_fusion.refs_0_, bf16[256,2048]{1,0:T(8,128)(2,1)S(1)} %copy-done.1, bf16[256,2048]{1,0:T(8,128)(2,1)S(1)} %collective-permute-done.4.refs_2_, bf16[256,2048]{1,0:T(8,128)(2,1)} %collective-permute-done.7.refs_1_.refs_3_, ...), custom_call_target="tpu_custom_call" | custom-call | flops 1000000 | bytes 100000 | tf_op jit(solution)/shard_map/pallas_call | solution.py:62
  176.3 16.0 %shard_map.72 = bf16[512,512]{1,0:T(8,128)(2,1)} custom-call(s32[512,128]{1,0:T(8,128)S(1)} %get-tuple-element.34.refs_0_, f32[512,512]{1,0:T(8,128)S(1)} %get-tuple-element.38.refs_1_, f32[512,512]{1,0:T(8,128)S(1)} %collective-permute-done.14.refs_2_, bf16[2,128,2560]{2,1,0:T(8,128)(2,1)S(1)} %get-tuple-element.56.refs_3_, ...), custom_call_target="tpu_custom_call" | custom-call | flops 1000000 | bytes 100000 | tf_op jit(solution)/shard_map/pallas_call | solution.py:279
  193.8 15.2 %shard_map.75.refs_0_ = bf16[512,512]{1,0:T(8,128)(2,1)S(1)} custom-call(s32[512,128]{1,0:T(8,128)S(1)} %get-tuple-element.34.refs_0_, f32[512,512]{1,0:T(8,128)S(1)} %get-tuple-element.43.refs_1_, f32[512,512]{1,0:T(8,128)S(1)} %collective-permute-done.17.refs_2_, bf16[2,128,2560]{2,1,0:T(8,128)(2,1)S(1)} %get-tuple-element.55.refs_3_, ...), custom_call_target="tpu_custom_call" | custom-call | flops 1000000 | bytes 100000 | tf_op jit(solution)/shard_map/pallas_call | solution.py:279
  212.5 11.3 %collective-permute-done.22.refs_3_ = bf16[512,512]{1,0:T(8,128)(2,1)S(1)} collective-permute-done((bf16[512,512]{1,0:T(8,128)(2,1)}, bf16[512,512]{1,0:T(8,128)(2,1)S(1)}, u32[]{:S(2)}, u32[]{:S(2)}) %collective-permute-start.22) | collective-permute-done | bytes 524320 | tf_op jit(solution)/shard_map/ppermute | solution.py:42
  225.7 5.5 %shard_map.78 = (bf16[256,2048]{1,0:T(8,128)(2,1)S(1)}, bf16[256,2048]{1,0:T(8,128)(2,1)S(1)}) custom-call(s32[10]{0:T(128)S(1)} %pad_add_fusion.refs_0_, bf16[512,512]{1,0:T(8,128)(2,1)S(1)} %collective-permute-done.15.refs_1_, bf16[512,512]{1,0:T(8,128)(2,1)S(1)} %collective-permute-done.16.refs_2_, bf16[512,512]{1,0:T(8,128)(2,1)S(1)} %collective-permute-done.22.refs_3_, ...), custom_call_target="tpu_custom_call" | custom-call | flops 1000000 | bytes 100000 | tf_op jit(solution)/shard_map/pallas_call | solution.py:62
  231.2 4.0 %collective-permute-done.26.refs_7_ = bf16[2048,256]{1,0:T(8,128)(2,1)S(1)} collective-permute-done((bf16[2048,256]{1,0:T(8,128)(2,1)}, bf16[2048,256]{1,0:T(8,128)(2,1)S(1)}, u32[]{:S(2)}, u32[]{:S(2)}) %collective-permute-start.26) | collective-permute-done | bytes 1048608 | tf_op jit(solution)/shard_map/ppermute | solution.py:52
  235.2 2.7 %shard_map.79 = (bf16[256,2048]{1,0:T(8,128)(2,1)S(1)}, bf16[256,2048]{1,0:T(8,128)(2,1)S(1)}) custom-call(s32[10]{0:T(128)S(1)} %pad_add_fusion.refs_0_, bf16[512,512]{1,0:T(8,128)(2,1)S(1)} %collective-permute-done.15.refs_1_, bf16[512,512]{1,0:T(8,128)(2,1)S(1)} %collective-permute-done.16.refs_2_, ...), custom_call_target="tpu_custom_call", output_to_operand_aliasing={{0}: (9, {}), {1}: (10, {})} | custom-call | flops 1000000 | bytes 100000 | tf_op jit(solution)/shard_map/pallas_call | solution.py:62
  240.2 12.2 %collective-permute-done.29.refs_7_ = bf16[1024,256]{1,0:T(8,128)(2,1)S(1)} collective-permute-done((bf16[1024,256]{1,0:T(8,128)(2,1)S(1)}, bf16[1024,256]{1,0:T(8,128)(2,1)S(1)}, u32[]{:S(2)}, u32[]{:S(2)}) %collective-permute-start.29) | collective-permute-done | bytes 524320 | tf_op jit(solution)/shard_map/ppermute | solution.py:52
  (105 shorter events, 49.5 us)
Async XLA Ops:
  6.5 80.4 %all-gather.2.cloned.1.call-start = ((), (), s32[]{:S(2)}) async-start(), calls=%async_computation | async-start | bytes 4456448 | tf_op jit(solution)/shard_map/all_gather | solution.py:357
  8.9 34.7 %collective-permute-start.5 = (bf16[256,2048]{1,0:T(8,128)(2,1)S(1)}, bf16[256,2048]{1,0:T(8,128)(2,1)S(1)}, u32[]{:S(2)}, u32[]{:S(2)}) collective-permute-start(bf16[256,2048]{1,0:T(8,128)(2,1)S(1)} %bitcast.16), channel_id=1, source_target_pairs={{0,2},{1,3},{4,0},{5,1},{8,4},{9,5},{12,8},{13,9},{14,12},{15,13},... | collective-permute-start | bytes 3145736 | tf_op jit(solution)/shard_map/ppermute | solution.py:52
  12.0 32.4 %collective-permute-start.8 = (bf16[256,2048]{1,0:T(8,128)(2,1)S(1)}, bf16[256,2048]{1,0:T(8,128)(2,1)}, u32[]{:S(2)}, u32[]{:S(2)}) collective-permute-start(bf16[256,2048]{1,0:T(8,128)(2,1)S(1)} %bitcast.17), channel_id=1, source_target_pairs={{0,4},{1,5},{4,8},{5,9},{8,12},{9,13},{12,14},{13,15},{14,10},{15,... | collective-permute-start | bytes 3145736 | tf_op jit(solution)/shard_map/ppermute | solution.py:52
  43.6 41.3 %collective-permute-start.6 = (bf16[256,2048]{1,0:T(8,128)(2,1)S(1)}, bf16[256,2048]{1,0:T(8,128)(2,1)}, u32[]{:S(2)}, u32[]{:S(2)}) collective-permute-start(bf16[256,2048]{1,0:T(8,128)(2,1)S(1)} %collective-permute-done.5.refs_4_), channel_id=1, source_target_pairs={{0,2},{1,3},{4,0},{5,1},{8,4},{9,5},{12,8},{13,9},{14,12},{15,13},... | collective-permute-start | bytes 3145736 | tf_op jit(solution)/shard_map/ppermute | solution.py:52
  44.4 41.0 %collective-permute-start.9 = (bf16[256,2048]{1,0:T(8,128)(2,1)}, bf16[256,2048]{1,0:T(8,128)(2,1)}, u32[]{:S(2)}, u32[]{:S(2)}) collective-permute-start(bf16[256,2048]{1,0:T(8,128)(2,1)} %collective-permute-done.8.refs_5_), channel_id=1, source_target_pairs={{0,4},{1,5},{4,8},{5,9},{8,12},{9,13},{12,14},{13,15},{14,10},{15,... | collective-permute-start | bytes 3145736 | tf_op jit(solution)/shard_map/ppermute | solution.py:52
  52.5 45.4 %collective-permute-start.13 = (bf16[2048,256]{1,0:T(8,128)(2,1)}, bf16[2048,256]{1,0:T(8,128)(2,1)S(1)}, u32[]{:S(2)}, u32[]{:S(2)}) collective-permute-start(bf16[2048,256]{1,0:T(8,128)(2,1)} %shard_map.69), channel_id=1, source_target_pairs={{0,16},{16,0},{1,17},{17,1},{2,18},{18,2},{3,19},{19,3},{4,20},{20... | collective-permute-start | bytes 3145736 | tf_op jit(solution)/shard_map/ppermute | solution.py:42
  54.1 79.6 %collective-permute-start.24 = (bf16[256,4096]{1,0:T(8,128)(2,1)}, bf16[256,4096]{1,0:T(8,128)(2,1)}, u32[]{:S(2)}, u32[]{:S(2)}) collective-permute-start(bf16[256,4096]{1,0:T(8,128)(2,1)} %bitcast.20), channel_id=1, source_target_pairs={{0,16},{16,0},{1,17},{17,1},{2,18},{18,2},{3,19},{19,3},{4,20},{20... | collective-permute-start | bytes 6291464 | tf_op jit(solution)/shard_map/ppermute | solution.py:42
  84.9 34.9 %collective-permute-start.7 = (bf16[256,2048]{1,0:T(8,128)(2,1)}, bf16[256,2048]{1,0:T(8,128)(2,1)}, u32[]{:S(2)}, u32[]{:S(2)}) collective-permute-start(bf16[256,2048]{1,0:T(8,128)(2,1)} %collective-permute-done.6.refs_6_), channel_id=1, source_target_pairs={{0,2},{1,3},{4,0},{5,1},{8,4},{9,5},{12,8},{13,9},{14,12},{15,13},... | collective-permute-start | bytes 3145736 | tf_op jit(solution)/shard_map/ppermute | solution.py:52
  85.4 34.4 %collective-permute-start.10 = (bf16[256,2048]{1,0:T(8,128)(2,1)}, bf16[256,2048]{1,0:T(8,128)(2,1)}, u32[]{:S(2)}, u32[]{:S(2)}) collective-permute-start(bf16[256,2048]{1,0:T(8,128)(2,1)} %collective-permute-done.9.refs_7_), channel_id=1, source_target_pairs={{0,4},{1,5},{4,8},{5,9},{8,12},{9,13},{12,14},{13,15},{14,10},{15,... | collective-permute-start | bytes 3145736 | tf_op jit(solution)/shard_map/ppermute | solution.py:52
  93.7 20.9 %collective-permute-start.1 = (bf16[528,256]{1,0:T(8,128)(2,1)S(1)}, bf16[528,256]{1,0:T(8,128)(2,1)}, u32[]{:S(2)}, u32[]{:S(2)}) collective-permute-start(bf16[528,256]{1,0:T(8,128)(2,1)S(1)} %shard_map.66.refs_3_.refs_8_), channel_id=1, source_target_pairs={{0,4},{1,5},{2,6},{3,7},{4,8},{5,9},{6,10},{7,11},{8,12},{9,13},{1... | collective-permute-start | bytes 811016 | tf_op jit(solution)/shard_map/ppermute | solution.py:37
  97.8 33.4 %collective-permute-start.4 = (bf16[256,2048]{1,0:T(8,128)(2,1)}, bf16[256,2048]{1,0:T(8,128)(2,1)S(1)}, u32[]{:S(2)}, u32[]{:S(2)}) collective-permute-start(bf16[256,2048]{1,0:T(8,128)(2,1)} %get-tuple-element.31.refs_3_), channel_id=1, source_target_pairs={{0,1},{1,0},{2,3},{3,2},{4,5},{5,4},{6,7},{7,6},{8,9},{9,8},{10,11... | collective-permute-start | bytes 3145736 | tf_op jit(solution)/shard_map/ppermute | solution.py:27
  119.8 26.5 %collective-permute-start.18 = (bf16[2048,256]{1,0:T(8,128)(2,1)}, bf16[2048,256]{1,0:T(8,128)(2,1)}, u32[]{:S(2)}, u32[]{:S(2)}) collective-permute-start(bf16[2048,256]{1,0:T(8,128)(2,1)} %shard_map.70.refs_10_.refs_7_), channel_id=1, source_target_pairs={{0,2},{1,3},{4,0},{5,1},{8,4},{9,5},{12,8},{13,9},{14,12},{15,13},... | collective-permute-start | bytes 3145736 | tf_op jit(solution)/shard_map/ppermute | solution.py:52
  120.5 28.2 %collective-permute-start.19 = (bf16[2048,256]{1,0:T(8,128)(2,1)}, bf16[2048,256]{1,0:T(8,128)(2,1)}, u32[]{:S(2)}, u32[]{:S(2)}) collective-permute-start(bf16[2048,256]{1,0:T(8,128)(2,1)} %shard_map.70.refs_10_.refs_7_), channel_id=1, source_target_pairs={{0,4},{1,5},{4,8},{5,9},{8,12},{9,13},{12,14},{13,15},{14,10},{15,... | collective-permute-start | bytes 3145736 | tf_op jit(solution)/shard_map/ppermute | solution.py:52
  127.3 31.1 %collective-permute-start.3 = (bf16[1056,256]{1,0:T(8,128)(2,1)S(1)}, bf16[1056,256]{1,0:T(8,128)(2,1)S(1)}, u32[]{:S(2)}, u32[]{:S(2)}) collective-permute-start(bf16[1056,256]{1,0:T(8,128)(2,1)S(1)} %pad_maximum_fusion), channel_id=1, source_target_pairs={{0,2},{1,3},{2,0},{3,1},{4,6},{5,7},{6,4},{7,5},{8,10},{9,11},{10,... | collective-permute-start | bytes 1622024 | tf_op jit(solution)/shard_map/ppermute | solution.py:32
  131.2 38.4 %collective-permute-start.11 = (bf16[128,2048]{1,0:T(8,128)(2,1)S(1)}, bf16[128,2048]{1,0:T(8,128)(2,1)S(1)}, u32[]{:S(2)}, u32[]{:S(2)}) collective-permute-start(bf16[128,2048]{1,0:T(8,128)(2,1)S(1)} %slice.34), channel_id=1, source_target_pairs={{0,4},{1,5},{4,8},{5,9},{8,12},{9,13},{12,14},{13,15},{14,10},{15,... | collective-permute-start | bytes 1572872 | tf_op jit(solution)/shard_map/ppermute | solution.py:52
  133.8 35.9 %collective-permute-start.12 = (bf16[128,2048]{1,0:T(8,128)(2,1)S(1)}, bf16[128,2048]{1,0:T(8,128)(2,1)S(1)}, u32[]{:S(2)}, u32[]{:S(2)}) collective-permute-start(bf16[128,2048]{1,0:T(8,128)(2,1)S(1)} %slice.35), channel_id=1, source_target_pairs={{0,2},{1,3},{4,0},{5,1},{8,4},{9,5},{12,8},{13,9},{14,12},{15,13},... | collective-permute-start | bytes 1572872 | tf_op jit(solution)/shard_map/ppermute | solution.py:52
  146.2 77.5 %collective-permute-start.25 = (bf16[256,2048]{1,0:T(8,128)(2,1)}, bf16[256,2048]{1,0:T(8,128)(2,1)}, u32[]{:S(2)}, u32[]{:S(2)}) collective-permute-start(bf16[256,2048]{1,0:T(8,128)(2,1)} %get-tuple-element.46), channel_id=1, source_target_pairs={{0,1},{1,0},{2,3},{3,2},{4,5},{5,4},{6,7},{7,6},{8,9},{9,8},{10,11... | collective-permute-start | bytes 3145736 | tf_op jit(solution)/shard_map/ppermute | solution.py:27
  148.7 61.2 %collective-permute-start.20 = (bf16[2048,256]{1,0:T(8,128)(2,1)}, bf16[2048,256]{1,0:T(8,128)(2,1)}, u32[]{:S(2)}, u32[]{:S(2)}) collective-permute-start(bf16[2048,256]{1,0:T(8,128)(2,1)} %collective-permute-done.18.refs_5_.refs_8_), channel_id=1, source_target_pairs={{0,2},{1,3},{4,0},{5,1},{8,4},{9,5},{12,8},{13,9},{14,12},{15,13},... | collective-permute-start | bytes 3145736 | tf_op jit(solution)/shard_map/ppermute | solution.py:52
  158.4 51.5 %collective-permute-start.21 = (bf16[2048,256]{1,0:T(8,128)(2,1)}, bf16[2048,256]{1,0:T(8,128)(2,1)}, u32[]{:S(2)}, u32[]{:S(2)}) collective-permute-start(bf16[2048,256]{1,0:T(8,128)(2,1)} %collective-permute-done.19.refs_6_.refs_9_), channel_id=1, source_target_pairs={{0,4},{1,5},{4,8},{5,9},{8,12},{9,13},{12,14},{13,15},{14,10},{15,... | collective-permute-start | bytes 3145736 | tf_op jit(solution)/shard_map/ppermute | solution.py:52
  175.4 18.4 %collective-permute-start.17 = (f32[512,512]{1,0:T(8,128)S(1)}, f32[512,512]{1,0:T(8,128)S(1)}, u32[]{:S(2)}, u32[]{:S(2)}) collective-permute-start(f32[512,512]{1,0:T(8,128)S(1)} %get-tuple-element.44), channel_id=1, source_target_pairs={{0,1},{1,0},{2,3},{3,2},{4,5},{5,4},{6,7},{7,6},{8,9},{9,8},{10,11... | collective-permute-start | bytes 3145736 | tf_op jit(solution)/shard_map/ppermute | solution.py:27
  192.3 20.2 %collective-permute-start.15 = (bf16[512,512]{1,0:T(8,128)(2,1)}, bf16[512,512]{1,0:T(8,128)(2,1)S(1)}, u32[]{:S(2)}, u32[]{:S(2)}) collective-permute-start(bf16[512,512]{1,0:T(8,128)(2,1)} %shard_map.72), channel_id=1, source_target_pairs={{0,16},{16,0},{1,17},{17,1},{2,18},{18,2},{3,19},{19,3},{4,20},{20... | collective-permute-start | bytes 1572872 | tf_op jit(solution)/shard_map/ppermute | solution.py:42
  210.5 24.7 %collective-permute-start.26 = (bf16[2048,256]{1,0:T(8,128)(2,1)}, bf16[2048,256]{1,0:T(8,128)(2,1)S(1)}, u32[]{:S(2)}, u32[]{:S(2)}) collective-permute-start(bf16[2048,256]{1,0:T(8,128)(2,1)} %collective-permute-done.20.refs_1_.refs_10_), channel_id=1, source_target_pairs={{0,2},{1,3},{4,0},{5,1},{8,4},{9,5},{12,8},{13,9},{14,12},{15,13},... | collective-permute-start | bytes 3145736 | tf_op jit(solution)/shard_map/ppermute | solution.py:52
  210.5 24.7 %collective-permute-start.27 = (bf16[2048,256]{1,0:T(8,128)(2,1)}, bf16[2048,256]{1,0:T(8,128)(2,1)S(1)}, u32[]{:S(2)}, u32[]{:S(2)}) collective-permute-start(bf16[2048,256]{1,0:T(8,128)(2,1)} %collective-permute-done.21.refs_2_.refs_11_), channel_id=1, source_target_pairs={{0,4},{1,5},{4,8},{5,9},{8,12},{9,13},{12,14},{13,15},{14,10},{15,... | collective-permute-start | bytes 3145736 | tf_op jit(solution)/shard_map/ppermute | solution.py:52
  237.9 19.4 %collective-permute-start.28 = (bf16[256,2048]{1,0:T(8,128)(2,1)S(1)}, bf16[256,2048]{1,0:T(8,128)(2,1)S(1)}, u32[]{:S(2)}, u32[]{:S(2)}) collective-permute-start(bf16[256,2048]{1,0:T(8,128)(2,1)S(1)} %get-tuple-element.50), channel_id=1, source_target_pairs={{0,1},{1,0},{2,3},{3,2},{4,5},{5,4},{6,7},{7,6},{8,9},{9,8},{10,11... | collective-permute-start | bytes 3145736 | tf_op jit(solution)/shard_map/ppermute | solution.py:27
  (24 other events, 274.5 us)
Sparse Core Ops, SparseCore 0:
  9.5 73.1 all-gather.1

commit v4 on v3

--- a/solution.py
+++ b/solution.py
@@ -88,18 +88,20 @@
     )(value, *others)
 
 
-def around(shard):
+def around(shard, halved=True):
     chips = lax.axis_size("fsdp") // 2
     found, moving = {0: [(0, shard)]}, {1: shard, -1: shard}
     for step in range(1, (chips - 1) // 2 + 1):
         for way in (1, -1):
             moving[way] = along_ring(moving[way], way)
             found[-way * step % chips] = [(0, moving[way])]
-    if chips % 2 == 0:
+    if chips % 2 == 0 and halved:
         half = shard.shape[0] // 2
         found[chips // 2] = [
             (0, along_ring(moving[1][:half], 1)), (half, along_ring(moving[-1][half:], -1))
         ]
+    elif chips % 2 == 0:
+        found[chips // 2] = [(0, along_ring(moving[1], 1))]
     return found
 
 
@@ -124,42 +126,41 @@
                 out_ref[at, j * size:(j + 1) * size] = part
 
 
-def keyval_kernel(scal_ref, segs_ref, own_ref, other_ref, weight_ref, kept_ref, sent_ref):
+def keyval_kernel(distances, scal_ref, segs_ref, own_ref, other_ref, *refs):
+    weights, (kept_ref, sent_ref) = refs[: len(distances)], refs[len(distances):]
     core = scal_ref[0]
     rows = own_ref.shape[0]
-    size = 256
-    total = None
-    for j in range(own_ref.shape[1] // size):
-        for ref, which in ((own_ref, core), (other_ref, 1 - core)):
+    lane = lax.broadcasted_iota(jnp.int32, (rows, 128), 1)
+    for rows_ref, which in ((own_ref, core), (other_ref, 1 - core)):
+        total = None
+        for distance, weight_ref in zip(distances, weights):
             found = jnp.dot(
-                ref[:, j * size:(j + 1) * size], weight_ref[0, block(2 * j + which, size), :],
+                rows_ref[:, block(scal_ref[2 + distance], weight_ref.shape[0])], weight_ref[...],
                 preferred_element_type=jnp.float32,
             )
             total = found if total is None else total + found
-    lane = lax.broadcasted_iota(jnp.int32, (rows, 128), 1)
-    for part in range(2):
-        low = total[:, part * 256:part * 256 + 128]
-        high = total[:, part * 256 + 128:part * 256 + 256]
-        zero = jnp.where(lane < HEAD_SIZE, low, pltpu.roll(high, HEAD_SIZE, 1))
-        one = jnp.where(lane < HEAD_SIZE, pltpu.roll(low, HEAD_SIZE, 1), high)
-        at = slice(part * 128, part * 128 + 128)
-        kept_ref[:, at] = jnp.where(core == 0, zero, one).astype(kept_ref.dtype)
-        sent_ref[:rows, at] = jnp.where(core == 0, one, zero).astype(sent_ref.dtype)
+        for part in range(2):
+            low = total[:, part * 256:part * 256 + 128]
+            high = total[:, part * 256 + 128:part * 256 + 256]
+            zero = jnp.where(lane < HEAD_SIZE, low, pltpu.roll(high, HEAD_SIZE, 1))
+            one = jnp.where(lane < HEAD_SIZE, pltpu.roll(low, HEAD_SIZE, 1), high)
+            at = slice(part * 128, part * 128 + 128)
+            kept_ref[block(which, rows), at] = jnp.where(core == 0, zero, one)
+            sent_ref[block(which, rows), at] = jnp.where(core == 0, one, zero)
     marks = (segs_ref[...] + 1).astype(jnp.float32)
-    sent_ref[rows:, :] = jnp.broadcast_to(marks, (MARK_ROWS, rows)).astype(sent_ref.dtype)
+    sent_ref[2 * rows:, :] = jnp.broadcast_to(marks, (8, marks.shape[1]))
 
 
 def parcel_kernel(scal_ref, segs_ref, kept_ref, received_ref, out_ref):
     core = scal_ref[0]
-    rows = kept_ref.shape[0]
-    out_ref[block(core, rows), :] = kept_ref[...]
-    out_ref[block(1 - core, rows), :] = received_ref[:rows, :]
+    count = kept_ref.shape[0]
+    out_ref[:count, :] = (kept_ref[...] + received_ref[:count, :]).astype(out_ref.dtype)
     own = (segs_ref[...] + 1).astype(jnp.float32)
-    other = received_ref[rows:, :].astype(jnp.float32)[0:1, :]
+    other = received_ref[count:count + 1, :]
     first, second = jnp.where(core == 0, own, other), jnp.where(core == 0, other, own)
-    row = lax.broadcasted_iota(jnp.int32, (MARK_ROWS, rows), 0)
+    row = lax.broadcasted_iota(jnp.int32, (MARK_ROWS, own.shape[1]), 0)
     marks = jnp.where(row == 0, first, jnp.where(row == 1, second, 0.0))
-    out_ref[2 * rows:, :] = marks.astype(out_ref.dtype)
+    out_ref[count:, :] = marks.astype(out_ref.dtype)
 
 
 def window_kernel(scal_ref, four_ref, two_ref, own_ref, crossed_ref, kt_ref, v_ref, lo_ref):
@@ -353,17 +354,18 @@
     sources = order[(place + jnp.arange(chips, dtype=jnp.int32)) % chips]
     scalars = jnp.concatenate([jnp.stack([core, chip % 2]).astype(jnp.int32), sources])
 
+    keyval_pieces = around(keyval_weight[0], halved=False)
     query_pieces = around(query_weight[0])
-    keyval_full = lax.all_gather(keyval_weight, "fsdp", axis=1, tiled=True)
 
     half = ((rows, width // 2), jnp.bfloat16)
     own_rows, sent_rows = run(functools.partial(split_kernel, True), [half, half], scalars, [hidden])
     other_rows = swap_cores(sent_rows)
-    out_shard = to_next_section(after(out_weight[0], own_rows))
+    out_shard = to_next_section(out_weight[0])
 
     kept, sent = run(
-        keyval_kernel, [((rows, 256), jnp.bfloat16), ((rows + MARK_ROWS, 256), jnp.bfloat16)],
-        scalars, [segment_ids, own_rows, sent_rows, keyval_full],
+        functools.partial(keyval_kernel, list(range(chips))),
+        [((2 * rows, 256), jnp.float32), ((2 * rows + 8, 256), jnp.float32)],
+        scalars, [segment_ids, own_rows, other_rows] + [keyval_pieces[d][0][1] for d in range(chips)],
     )
     parcel, = run(
         parcel_kernel, [((2 * rows + MARK_ROWS, 256), jnp.bfloat16)], scalars,
@@ -392,7 +394,7 @@
     near = [0, 1, chips - 1, 2, chips - 2]
     next_far = [3, chips - 3]
     far = [chips // 2]
-    out_shard = after(out_shard, query_pieces[3][0][1], query_pieces[chips - 3][0][1])
+    out_shard = after(out_shard, *[piece for _, piece in query_pieces[chips // 2]])
     out_pieces = around(out_shard)
     sums = [query_sums(near, g, [parcel]) for g in range(2)]
     sums = [query_sums(next_far + far, g, [keys_t, out_shard], sums[g]) for g in range(2)]
@@ -402,7 +404,7 @@
         attended.append(attention(lowest, sums[g][0], swap_cores(sums[g][1]), keys_t[g], values[g], waits))
     attended[1] = after(attended[1], *[out_pieces[d][0][1] for d in (2, chips - 2)])
     kept, sent = run(
-        functools.partial(split_kernel, False), [half, half], scalars, [to_next_section(hidden)]
+        functools.partial(split_kernel, False), [half, half], scalars, [to_next_section(hidden)], waits=attended[:1]
     )
     adds = [kept, swap_cores(sent)]
     arrived = []

time: 267 us -> 262 us (0.981)
  between operations: 13.7 us -> 0.41 us
  starting transfers between devices: 32.7 us -> 43.4 us
  local copies, waits for them, and re-layouts: 12.1 us -> 7.88 us
  waiting for transfers between devices: 139 us -> 142 us
    ppermute x2, waiting for transfers between devices: 21.1 us -> 3.4 us  [two_chips_on(): return lax.ppermute(value, 'fsdp', [(i, i + 4) for i in range(count - 4)])]
    ppermute x1, waiting for transfers between devices: 8.97 us -> 21.3 us  [swap_chips(): return lax.ppermute(value, 'fsdp', [(i, i ^ 2) for i in range(count)])]
    ppermute x4, waiting for transfers between devices: 11.3 us -> 20.4 us  [to_next_section(): lax.ppermute(value, 'section', [(i, (i + 1) % count) for i in range(count)])]
    ppermute x16 -> x23, starting transfers between devices: 16.7 us -> 25.5 us  [along_ring(): return lax.ppermute(value, 'fsdp', pairs)]
    unnamed x31 -> x36, local copies, waits for them, and re-layouts: 8.93 us -> 6.05 us
    ppermute x16 -> x23, waiting for transfers between devices: 93 us -> 93.2 us  [along_ring(): return lax.ppermute(value, 'fsdp', pairs)]
  transfers between devices with their start and end apart: 33 -> 39, of which waited for: 15 -> 17; matrix products, arithmetic and copies ran while one was open for 2% -> 2% of each run, Pallas kernels for 23% -> 23%
where the time goes in v4:
time: 262 us; the launch traced here: 261 us
  waiting for transfers between devices  142 us (54%)
  Pallas kernels  64.3 us (25%)
  starting transfers between devices  43.4 us (17%)
  local copies, waits for them, and re-layouts  7.88 us (3%)
  other arithmetic  3.16 us (1%)
    ppermute x23, waiting for transfers between devices, along_ring(): return lax.ppermute(value, 'fsdp', pairs)  93.2 us
    pallas_call x13, Pallas kernels, run(): pl.pallas_call(only, in_specs=[pl.BlockSpec(memory_space=pltpu.SMEM)] + [...  33.1 us
    pallas_call x2, Pallas kernels, attention(): pl.pallas_call(only, grid=(rows // TILE,), in_specs=[pl.BlockSpec((TILE,...  31.2 us
    ppermute x23, starting transfers between devices, along_ring(): return lax.ppermute(value, 'fsdp', pairs)  25.5 us
    ppermute x1, waiting for transfers between devices, swap_chips(): return lax.ppermute(value, 'fsdp', [(i, i ^ 2) for i in range(count)])  21.3 us
    ppermute x4, waiting for transfers between devices, to_next_section(): lax.ppermute(value, 'section', [(i, (i + 1) % count) for i in range(count)])  20.4 us
    ppermute x2, starting transfers between devices, two_chips_on(): return lax.ppermute(value, 'fsdp', [(i, i + 4) for i in range(count - 4)])  8.51 us
    unnamed x36, local copies, waits for them, and re-layouts  6.05 us
  transfers between devices with their start and end apart: 39, of which 17 were waited for; matrix products, arithmetic and copies ran while one was open for 2% of the time, Pallas kernels for 23%

profile of v4, /device:TPU:0, one launch (start us, length us, event | category | flops | bytes accessed | tf_op | source)
XLA Modules:
  0.0 261.0 jit_solution(13181960713019108909)
XLA Ops:
  0.0 3.0 %collective-permute-start.12 = (bf16[256,2048]{1,0:T(8,128)(2,1)}, bf16[256,2048]{1,0:T(8,128)(2,1)S(1)}, u32[]{:S(2)}, u32[]{:S(2)}) collective-permute-start(bf16[256,2048]{1,0:T(8,128)(2,1)} %bitcast.17), channel_id=1, source_target_pairs={{0,2},{1,3},{4,0},{5,1},{8,4},{9,5},{12,8},{13,9},{14,12},{15,13},... | collective-permute-start | bytes 3145736 | tf_op jit(solution)/shard_map/ppermute | solution.py:52
  5.1 21.3 %collective-permute-done.12.refs_4_ = bf16[256,2048]{1,0:T(8,128)(2,1)S(1)} collective-permute-done((bf16[256,2048]{1,0:T(8,128)(2,1)}, bf16[256,2048]{1,0:T(8,128)(2,1)S(1)}, u32[]{:S(2)}, u32[]{:S(2)}) %collective-permute-start.12) | collective-permute-done | bytes 1048608 | tf_op jit(solution)/shard_map/ppermute | solution.py:52
  38.1 18.3 %collective-permute-done.1.refs_5_ = bf16[256,512]{1,0:T(8,128)(2,1)S(1)} collective-permute-done((bf16[256,512]{1,0:T(8,128)(2,1)S(1)}, bf16[256,512]{1,0:T(8,128)(2,1)S(1)}, u32[]{:S(2)}, u32[]{:S(2)}) %collective-permute-start.1) | collective-permute-done | bytes 262176 | tf_op jit(solution)/shard_map/ppermute | solution.py:52
  57.8 3.7 %collective-permute-done.5.refs_10_ = bf16[256,512]{1,0:T(8,128)(2,1)S(1)} collective-permute-done((bf16[256,512]{1,0:T(8,128)(2,1)}, bf16[256,512]{1,0:T(8,128)(2,1)S(1)}, u32[]{:S(2)}, u32[]{:S(2)}) %collective-permute-start.5) | collective-permute-done | bytes 262176 | tf_op jit(solution)/shard_map/ppermute | solution.py:52
  65.6 5.2 %collective-permute-done.6.refs_9_ = bf16[256,512]{1,0:T(8,128)(2,1)S(1)} collective-permute-done((bf16[256,512]{1,0:T(8,128)(2,1)S(1)}, bf16[256,512]{1,0:T(8,128)(2,1)S(1)}, u32[]{:S(2)}, u32[]{:S(2)}) %collective-permute-start.6) | collective-permute-done | bytes 262176 | tf_op jit(solution)/shard_map/ppermute | solution.py:52
  71.1 21.5 %collective-permute-done.3.refs_7_ = bf16[256,512]{1,0:T(8,128)(2,1)S(1)} collective-permute-done((bf16[256,512]{1,0:T(8,128)(2,1)S(1)}, bf16[256,512]{1,0:T(8,128)(2,1)S(1)}, u32[]{:S(2)}, u32[]{:S(2)}) %collective-permute-start.3) | collective-permute-done | bytes 262176 | tf_op jit(solution)/shard_map/ppermute | solution.py:52
  92.6 3.9 %collective-permute-done.7.refs_8_ = bf16[256,512]{1,0:T(8,128)(2,1)S(1)} collective-permute-done((bf16[256,512]{1,0:T(8,128)(2,1)S(1)}, bf16[256,512]{1,0:T(8,128)(2,1)S(1)}, u32[]{:S(2)}, u32[]{:S(2)}) %collective-permute-start.7) | collective-permute-done | bytes 262176 | tf_op jit(solution)/shard_map/ppermute | solution.py:52
  96.5 2.4 shard_map.65
  101.5 3.3 %collective-permute-start.9 = (bf16[528,256]{1,0:T(8,128)(2,1)S(1)}, bf16[528,256]{1,0:T(8,128)(2,1)}, u32[]{:S(2)}, u32[]{:S(2)}) collective-permute-start(bf16[528,256]{1,0:T(8,128)(2,1)S(1)} %shard_map.66.refs_3_.refs_8_), channel_id=1, source_target_pairs={{0,4},{1,5},{2,6},{3,7},{4,8},{5,9},{6,10},{7,11},{8,12},{9,13},{1... | collective-permute-start | bytes 811016 | tf_op jit(solution)/shard_map/ppermute | solution.py:37
  107.5 3.4 %collective-permute-done.9.refs_2_ = bf16[528,256]{1,0:T(8,128)(2,1)} collective-permute-done((bf16[528,256]{1,0:T(8,128)(2,1)S(1)}, bf16[528,256]{1,0:T(8,128)(2,1)}, u32[]{:S(2)}, u32[]{:S(2)}) %collective-permute-start.9) | collective-permute-done | bytes 270368 | tf_op jit(solution)/shard_map/ppermute | solution.py:37
  110.9 5.2 %collective-permute-start.10 = (bf16[528,256]{1,0:T(8,128)(2,1)}, bf16[528,256]{1,0:T(8,128)(2,1)}, u32[]{:S(2)}, u32[]{:S(2)}) collective-permute-start(bf16[528,256]{1,0:T(8,128)(2,1)} %collective-permute-done.9.refs_2_), channel_id=1, source_target_pairs={{0,4},{1,5},{2,6},{3,7},{4,8},{5,9},{6,10},{7,11},{8,12},{9,13},{1... | collective-permute-start | bytes 811016 | tf_op jit(solution)/shard_map/ppermute | solution.py:37
  116.1 8.4 %collective-permute-done.20.refs_0_ = bf16[2048,256]{1,0:T(8,128)(2,1)S(1)} collective-permute-done((bf16[2048,256]{1,0:T(8,128)(2,1)S(1)}, bf16[2048,256]{1,0:T(8,128)(2,1)S(1)}, u32[]{:S(2)}, u32[]{:S(2)}) %collective-permute-start.20) | collective-permute-done | bytes 1048608 | tf_op jit(solution)/shard_map/ppermute | solution.py:42
  128.8 3.5 %collective-permute-start.11 = (bf16[1056,256]{1,0:T(8,128)(2,1)S(1)}, bf16[1056,256]{1,0:T(8,128)(2,1)S(1)}, u32[]{:S(2)}, u32[]{:S(2)}) collective-permute-start(bf16[1056,256]{1,0:T(8,128)(2,1)S(1)} %pad_maximum_fusion), channel_id=1, source_target_pairs={{0,2},{1,3},{2,0},{3,1},{4,6},{5,7},{6,4},{7,5},{8,10},{9,11},{10,... | collective-permute-start | bytes 1622024 | tf_op jit(solution)/shard_map/ppermute | solution.py:32
  135.0 3.4 %shard_map.68 = (f32[512,512]{1,0:T(8,128)S(1)}, f32[512,512]{1,0:T(8,128)S(1)}) custom-call(s32[10]{0:T(128)S(1)} %pad_add_fusion.refs_0_, bf16[256,2048]{1,0:T(8,128)(2,1)S(1)} %get-tuple-element.30.refs_2_.refs_1_, bf16[256,2048]{1,0:T(8,128)(2,1)S(1)} %collective-permute-done.refs_3_.refs_2_, bf16[256,2048]{1,0:T(8,128)(2,1)S(1)} %bitcast.19, ...), custom_call_target="tpu_custom_call" | custom-call | flops 1000000 | bytes 100000 | tf_op jit(solution)/shard_map/pallas_call | solution.py:62
  138.5 3.8 %shard_map.72 = (f32[512,512]{1,0:T(8,128)S(1)}, f32[512,512]{1,0:T(8,128)S(1)}) custom-call(s32[10]{0:T(128)S(1)} %pad_add_fusion.refs_0_, bf16[256,2048]{1,0:T(8,128)(2,1)S(1)} %get-tuple-element.30.refs_2_.refs_1_, bf16[256,2048]{1,0:T(8,128)(2,1)S(1)} %collective-permute-done.refs_3_.refs_2_, bf16[256,2048]{1,0:T(8,128)(2,1)S(1)} %bitcast.20, ...), custom_call_target="tpu_custom_call" | custom-call | flops 1000000 | bytes 100000 | tf_op jit(solution)/shard_map/pallas_call | solution.py:62
  142.3 21.3 %collective-permute-done.11.refs_4_ = bf16[1056,256]{1,0:T(8,128)(2,1)S(1)} collective-permute-done((bf16[1056,256]{1,0:T(8,128)(2,1)S(1)}, bf16[1056,256]{1,0:T(8,128)(2,1)S(1)}, u32[]{:S(2)}, u32[]{:S(2)}) %collective-permute-start.11) | collective-permute-done | bytes 540704 | tf_op jit(solution)/shard_map/ppermute | solution.py:32
  169.5 3.3 %shard_map.73 = (f32[512,512]{1,0:T(8,128)S(1)}, f32[512,512]{1,0:T(8,128)}) custom-call(s32[10]{0:T(128)S(1)} %pad_add_fusion.refs_0_, bf16[256,2048]{1,0:T(8,128)(2,1)S(1)} %get-tuple-element.30.refs_2_.refs_1_, bf16[256,2048]{1,0:T(8,128)(2,1)S(1)} %collective-permute-done.refs_3_.refs_2_, bf16[256,2048]{1,0:T(8,128)(2,1)S(1)} %copy-done.5, ...), custom_call_target="tpu_custom_call" | custom-call | flops 1000000 | bytes 100000 | tf_op jit(solution)/shard_map/pallas_call | solution.py:62
  175.7 16.0 %shard_map.71.refs_2_ = bf16[512,512]{1,0:T(8,128)(2,1)} custom-call(s32[512,128]{1,0:T(8,128)S(1)} %get-tuple-element.34.refs_0_, f32[512,512]{1,0:T(8,128)S(1)} %get-tuple-element.38.refs_1_, f32[512,512]{1,0:T(8,128)S(1)} %collective-permute-done.21.refs_2_, bf16[2,128,2560]{2,1,0:T(8,128)(2,1)S(1)} %get-tuple-element.56.refs_3_, ...), custom_call_target="tpu_custom_call" | custom-call | flops 1000000 | bytes 100000 | tf_op jit(solution)/shard_map/pallas_call | solution.py:280
  195.0 15.2 %shard_map.74.refs_0_ = bf16[512,512]{1,0:T(8,128)(2,1)S(1)} custom-call(s32[512,128]{1,0:T(8,128)S(1)} %get-tuple-element.34.refs_0_, f32[512,512]{1,0:T(8,128)S(1)} %get-tuple-element.43.refs_1_, f32[512,512]{1,0:T(8,128)S(1)} %collective-permute-done.24.refs_2_, bf16[2,128,2560]{2,1,0:T(8,128)(2,1)S(1)} %get-tuple-element.55.refs_3_, ...), custom_call_target="tpu_custom_call" | custom-call | flops 1000000 | bytes 100000 | tf_op jit(solution)/shard_map/pallas_call | solution.py:280
  213.6 12.0 %collective-permute-done.29.refs_3_ = bf16[512,512]{1,0:T(8,128)(2,1)S(1)} collective-permute-done((bf16[512,512]{1,0:T(8,128)(2,1)}, bf16[512,512]{1,0:T(8,128)(2,1)S(1)}, u32[]{:S(2)}, u32[]{:S(2)}) %collective-permute-start.29) | collective-permute-done | bytes 524320 | tf_op jit(solution)/shard_map/ppermute | solution.py:42
  227.5 5.3 %shard_map.77 = (bf16[256,2048]{1,0:T(8,128)(2,1)S(1)}, bf16[256,2048]{1,0:T(8,128)(2,1)S(1)}) custom-call(s32[10]{0:T(128)S(1)} %pad_add_fusion.refs_0_, bf16[512,512]{1,0:T(8,128)(2,1)} %collective-permute-done.22.refs_1_, bf16[512,512]{1,0:T(8,128)(2,1)S(1)} %collective-permute-done.23.refs_2_, bf16[512,512]{1,0:T(8,128)(2,1)S(1)} %collective-permute-done.29.refs_3_, ...), custom_call_target="tpu_custom_call" | custom-call | flops 1000000 | bytes 100000 | tf_op jit(solution)/shard_map/pallas_call | solution.py:62
  232.9 4.2 %collective-permute-done.33.refs_7_ = bf16[2048,256]{1,0:T(8,128)(2,1)S(1)} collective-permute-done((bf16[2048,256]{1,0:T(8,128)(2,1)}, bf16[2048,256]{1,0:T(8,128)(2,1)S(1)}, u32[]{:S(2)}, u32[]{:S(2)}) %collective-permute-start.33) | collective-permute-done | bytes 1048608 | tf_op jit(solution)/shard_map/ppermute | solution.py:52
  237.1 2.5 shard_map.78
  241.9 12.2 %collective-permute-done.36.refs_7_ = bf16[1024,256]{1,0:T(8,128)(2,1)S(1)} collective-permute-done((bf16[1024,256]{1,0:T(8,128)(2,1)S(1)}, bf16[1024,256]{1,0:T(8,128)(2,1)S(1)}, u32[]{:S(2)}, u32[]{:S(2)}) %collective-permute-start.36) | collective-permute-done | bytes 524320 | tf_op jit(solution)/shard_map/ppermute | solution.py:52
  (120 shorter events, 58.3 us)
Async XLA Ops:
  0.0 26.4 %collective-permute-start.12 = (bf16[256,2048]{1,0:T(8,128)(2,1)}, bf16[256,2048]{1,0:T(8,128)(2,1)S(1)}, u32[]{:S(2)}, u32[]{:S(2)}) collective-permute-start(bf16[256,2048]{1,0:T(8,128)(2,1)} %bitcast.17), channel_id=1, source_target_pairs={{0,2},{1,3},{4,0},{5,1},{8,4},{9,5},{12,8},{13,9},{14,12},{15,13},... | collective-permute-start | bytes 3145736 | tf_op jit(solution)/shard_map/ppermute | solution.py:52
  3.0 26.4 %collective-permute-start.15 = (bf16[256,2048]{1,0:T(8,128)(2,1)}, bf16[256,2048]{1,0:T(8,128)(2,1)}, u32[]{:S(2)}, u32[]{:S(2)}) collective-permute-start(bf16[256,2048]{1,0:T(8,128)(2,1)} %bitcast.18), channel_id=1, source_target_pairs={{0,4},{1,5},{4,8},{5,9},{8,12},{9,13},{12,14},{13,15},{14,10},{15,... | collective-permute-start | bytes 3145736 | tf_op jit(solution)/shard_map/ppermute | solution.py:52
  3.0 35.0 %collective-permute-start.4 = (bf16[256,512]{1,0:T(8,128)(2,1)}, bf16[256,512]{1,0:T(8,128)(2,1)}, u32[]{:S(2)}, u32[]{:S(2)}) collective-permute-start(bf16[256,512]{1,0:T(8,128)(2,1)} %bitcast.23), channel_id=1, source_target_pairs={{0,4},{1,5},{4,8},{5,9},{8,12},{9,13},{12,14},{13,15},{14,10},{15,... | collective-permute-start | bytes 786440 | tf_op jit(solution)/shard_map/ppermute | solution.py:52
  26.4 37.2 %collective-permute-start.13 = (bf16[256,2048]{1,0:T(8,128)(2,1)S(1)}, bf16[256,2048]{1,0:T(8,128)(2,1)}, u32[]{:S(2)}, u32[]{:S(2)}) collective-permute-start(bf16[256,2048]{1,0:T(8,128)(2,1)S(1)} %collective-permute-done.12.refs_4_), channel_id=1, source_target_pairs={{0,2},{1,3},{4,0},{5,1},{8,4},{9,5},{12,8},{13,9},{14,12},{15,13},... | collective-permute-start | bytes 3145736 | tf_op jit(solution)/shard_map/ppermute | solution.py:52
  29.4 32.5 %collective-permute-start.16 = (bf16[256,2048]{1,0:T(8,128)(2,1)}, bf16[256,2048]{1,0:T(8,128)(2,1)}, u32[]{:S(2)}, u32[]{:S(2)}) collective-permute-start(bf16[256,2048]{1,0:T(8,128)(2,1)} %collective-permute-done.15.refs_5_), channel_id=1, source_target_pairs={{0,4},{1,5},{4,8},{5,9},{8,12},{9,13},{12,14},{13,15},{14,10},{15,... | collective-permute-start | bytes 3145736 | tf_op jit(solution)/shard_map/ppermute | solution.py:52
  35.9 56.7 %collective-permute-start = (bf16[256,2048]{1,0:T(8,128)(2,1)S(1)}, bf16[256,2048]{1,0:T(8,128)(2,1)S(1)}, u32[]{:S(2)}, u32[]{:S(2)}) collective-permute-start(bf16[256,2048]{1,0:T(8,128)(2,1)S(1)} %get-tuple-element.31), channel_id=1, source_target_pairs={{0,1},{1,0},{2,3},{3,2},{4,5},{5,4},{6,7},{7,6},{8,9},{9,8},{10,11... | collective-permute-start | bytes 3145736 | tf_op jit(solution)/shard_map/ppermute | solution.py:27
  36.0 20.5 %collective-permute-start.1 = (bf16[256,512]{1,0:T(8,128)(2,1)S(1)}, bf16[256,512]{1,0:T(8,128)(2,1)S(1)}, u32[]{:S(2)}, u32[]{:S(2)}) collective-permute-start(bf16[256,512]{1,0:T(8,128)(2,1)S(1)} %bitcast.24), channel_id=1, source_target_pairs={{0,2},{1,3},{4,0},{5,1},{8,4},{9,5},{12,8},{13,9},{14,12},{15,13},... | collective-permute-start | bytes 786440 | tf_op jit(solution)/shard_map/ppermute | solution.py:52
  38.0 23.5 %collective-permute-start.5 = (bf16[256,512]{1,0:T(8,128)(2,1)}, bf16[256,512]{1,0:T(8,128)(2,1)S(1)}, u32[]{:S(2)}, u32[]{:S(2)}) collective-permute-start(bf16[256,512]{1,0:T(8,128)(2,1)} %collective-permute-done.4.refs_11_), channel_id=1, source_target_pairs={{0,4},{1,5},{4,8},{5,9},{8,12},{9,13},{12,14},{13,15},{14,10},{15,... | collective-permute-start | bytes 786440 | tf_op jit(solution)/shard_map/ppermute | solution.py:52
  61.9 42.9 %collective-permute-start.17 = (bf16[256,2048]{1,0:T(8,128)(2,1)}, bf16[256,2048]{1,0:T(8,128)(2,1)S(1)}, u32[]{:S(2)}, u32[]{:S(2)}) collective-permute-start(bf16[256,2048]{1,0:T(8,128)(2,1)} %collective-permute-done.16.refs_7_), channel_id=1, source_target_pairs={{0,4},{1,5},{4,8},{5,9},{8,12},{9,13},{12,14},{13,15},{14,10},{15,... | collective-permute-start | bytes 3145736 | tf_op jit(solution)/shard_map/ppermute | solution.py:52
  63.6 42.0 %collective-permute-start.14 = (bf16[256,2048]{1,0:T(8,128)(2,1)}, bf16[256,2048]{1,0:T(8,128)(2,1)S(1)}, u32[]{:S(2)}, u32[]{:S(2)}) collective-permute-start(bf16[256,2048]{1,0:T(8,128)(2,1)} %collective-permute-done.13.refs_6_), channel_id=1, source_target_pairs={{0,2},{1,3},{4,0},{5,1},{8,4},{9,5},{12,8},{13,9},{14,12},{15,13},... | collective-permute-start | bytes 3145736 | tf_op jit(solution)/shard_map/ppermute | solution.py:52
  63.9 28.7 %collective-permute-start.3 = (bf16[256,512]{1,0:T(8,128)(2,1)S(1)}, bf16[256,512]{1,0:T(8,128)(2,1)S(1)}, u32[]{:S(2)}, u32[]{:S(2)}) collective-permute-start(bf16[256,512]{1,0:T(8,128)(2,1)S(1)} %collective-permute-done.2.refs_6_), channel_id=1, source_target_pairs={{0,2},{1,3},{4,0},{5,1},{8,4},{9,5},{12,8},{13,9},{14,12},{15,13},... | collective-permute-start | bytes 786440 | tf_op jit(solution)/shard_map/ppermute | solution.py:52
  70.7 25.7 %collective-permute-start.7 = (bf16[256,512]{1,0:T(8,128)(2,1)S(1)}, bf16[256,512]{1,0:T(8,128)(2,1)S(1)}, u32[]{:S(2)}, u32[]{:S(2)}) collective-permute-start(bf16[256,512]{1,0:T(8,128)(2,1)S(1)} %collective-permute-done.6.refs_9_), channel_id=1, source_target_pairs={{0,4},{1,5},{4,8},{5,9},{8,12},{9,13},{12,14},{13,15},{14,10},{15,... | collective-permute-start | bytes 786440 | tf_op jit(solution)/shard_map/ppermute | solution.py:52
  99.0 25.6 %collective-permute-start.20 = (bf16[2048,256]{1,0:T(8,128)(2,1)S(1)}, bf16[2048,256]{1,0:T(8,128)(2,1)S(1)}, u32[]{:S(2)}, u32[]{:S(2)}) collective-permute-start(bf16[2048,256]{1,0:T(8,128)(2,1)S(1)} %bitcast.26), channel_id=1, source_target_pairs={{0,16},{16,0},{1,17},{17,1},{2,18},{18,2},{3,19},{19,3},{4,20},{20... | collective-permute-start | bytes 3145736 | tf_op jit(solution)/shard_map/ppermute | solution.py:42
  125.8 47.5 %collective-permute-start.25 = (bf16[2048,256]{1,0:T(8,128)(2,1)}, bf16[2048,256]{1,0:T(8,128)(2,1)}, u32[]{:S(2)}, u32[]{:S(2)}) collective-permute-start(bf16[2048,256]{1,0:T(8,128)(2,1)} %shard_map.69.refs_10_.refs_7_), channel_id=1, source_target_pairs={{0,2},{1,3},{4,0},{5,1},{8,4},{9,5},{12,8},{13,9},{14,12},{15,13},... | collective-permute-start | bytes 3145736 | tf_op jit(solution)/shard_map/ppermute | solution.py:52
  127.3 46.3 %collective-permute-start.26 = (bf16[2048,256]{1,0:T(8,128)(2,1)}, bf16[2048,256]{1,0:T(8,128)(2,1)}, u32[]{:S(2)}, u32[]{:S(2)}) collective-permute-start(bf16[2048,256]{1,0:T(8,128)(2,1)} %shard_map.69.refs_10_.refs_7_), channel_id=1, source_target_pairs={{0,4},{1,5},{4,8},{5,9},{8,12},{9,13},{12,14},{13,15},{14,10},{15,... | collective-permute-start | bytes 3145736 | tf_op jit(solution)/shard_map/ppermute | solution.py:52
  128.8 34.8 %collective-permute-start.11 = (bf16[1056,256]{1,0:T(8,128)(2,1)S(1)}, bf16[1056,256]{1,0:T(8,128)(2,1)S(1)}, u32[]{:S(2)}, u32[]{:S(2)}) collective-permute-start(bf16[1056,256]{1,0:T(8,128)(2,1)S(1)} %pad_maximum_fusion), channel_id=1, source_target_pairs={{0,2},{1,3},{2,0},{3,1},{4,6},{5,7},{6,4},{7,5},{8,10},{9,11},{10,... | collective-permute-start | bytes 1622024 | tf_op jit(solution)/shard_map/ppermute | solution.py:32
  132.3 60.9 %collective-permute-start.31 = (bf16[256,4096]{1,0:T(8,128)(2,1)}, bf16[256,4096]{1,0:T(8,128)(2,1)S(1)}, u32[]{:S(2)}, u32[]{:S(2)}) collective-permute-start(bf16[256,4096]{1,0:T(8,128)(2,1)} %bitcast.21), channel_id=1, source_target_pairs={{0,16},{16,0},{1,17},{17,1},{2,18},{18,2},{3,19},{19,3},{4,20},{20... | collective-permute-start | bytes 6291464 | tf_op jit(solution)/shard_map/ppermute | solution.py:42
  172.8 22.2 %collective-permute-start.24 = (f32[512,512]{1,0:T(8,128)}, f32[512,512]{1,0:T(8,128)S(1)}, u32[]{:S(2)}, u32[]{:S(2)}) collective-permute-start(f32[512,512]{1,0:T(8,128)} %get-tuple-element.44), channel_id=1, source_target_pairs={{0,1},{1,0},{2,3},{3,2},{4,5},{5,4},{6,7},{7,6},{8,9},{9,8},{10,11... | collective-permute-start | bytes 3145736 | tf_op jit(solution)/shard_map/ppermute | solution.py:27
  173.3 37.7 %collective-permute-start.27 = (bf16[2048,256]{1,0:T(8,128)(2,1)}, bf16[2048,256]{1,0:T(8,128)(2,1)}, u32[]{:S(2)}, u32[]{:S(2)}) collective-permute-start(bf16[2048,256]{1,0:T(8,128)(2,1)} %collective-permute-done.25.refs_5_.refs_8_), channel_id=1, source_target_pairs={{0,2},{1,3},{4,0},{5,1},{8,4},{9,5},{12,8},{13,9},{14,12},{15,13},... | collective-permute-start | bytes 3145736 | tf_op jit(solution)/shard_map/ppermute | solution.py:52
  173.6 37.4 %collective-permute-start.28 = (bf16[2048,256]{1,0:T(8,128)(2,1)}, bf16[2048,256]{1,0:T(8,128)(2,1)}, u32[]{:S(2)}, u32[]{:S(2)}) collective-permute-start(bf16[2048,256]{1,0:T(8,128)(2,1)} %collective-permute-done.26.refs_6_.refs_9_), channel_id=1, source_target_pairs={{0,4},{1,5},{4,8},{5,9},{8,12},{9,13},{12,14},{13,15},{14,10},{15,... | collective-permute-start | bytes 3145736 | tf_op jit(solution)/shard_map/ppermute | solution.py:52
  191.7 21.9 %collective-permute-start.22 = (bf16[512,512]{1,0:T(8,128)(2,1)}, bf16[512,512]{1,0:T(8,128)(2,1)}, u32[]{:S(2)}, u32[]{:S(2)}) collective-permute-start(bf16[512,512]{1,0:T(8,128)(2,1)} %shard_map.71.refs_2_), channel_id=1, source_target_pairs={{0,16},{16,0},{1,17},{17,1},{2,18},{18,2},{3,19},{19,3},{4,20},{20... | collective-permute-start | bytes 1572872 | tf_op jit(solution)/shard_map/ppermute | solution.py:42
  195.0 30.6 %collective-permute-start.32 = (bf16[256,2048]{1,0:T(8,128)(2,1)}, bf16[256,2048]{1,0:T(8,128)(2,1)S(1)}, u32[]{:S(2)}, u32[]{:S(2)}) collective-permute-start(bf16[256,2048]{1,0:T(8,128)(2,1)} %get-tuple-element.46), channel_id=1, source_target_pairs={{0,1},{1,0},{2,3},{3,2},{4,5},{5,4},{6,7},{7,6},{8,9},{9,8},{10,11... | collective-permute-start | bytes 3145736 | tf_op jit(solution)/shard_map/ppermute | solution.py:27
  211.6 25.5 %collective-permute-start.33 = (bf16[2048,256]{1,0:T(8,128)(2,1)}, bf16[2048,256]{1,0:T(8,128)(2,1)S(1)}, u32[]{:S(2)}, u32[]{:S(2)}) collective-permute-start(bf16[2048,256]{1,0:T(8,128)(2,1)} %collective-permute-done.27.refs_1_.refs_10_), channel_id=1, source_target_pairs={{0,2},{1,3},{4,0},{5,1},{8,4},{9,5},{12,8},{13,9},{14,12},{15,13},... | collective-permute-start | bytes 3145736 | tf_op jit(solution)/shard_map/ppermute | solution.py:52
  211.9 25.2 %collective-permute-start.34 = (bf16[2048,256]{1,0:T(8,128)(2,1)}, bf16[2048,256]{1,0:T(8,128)(2,1)S(1)}, u32[]{:S(2)}, u32[]{:S(2)}) collective-permute-start(bf16[2048,256]{1,0:T(8,128)(2,1)} %collective-permute-done.28.refs_2_.refs_11_), channel_id=1, source_target_pairs={{0,4},{1,5},{4,8},{5,9},{8,12},{9,13},{12,14},{13,15},{14,10},{15,... | collective-permute-start | bytes 3145736 | tf_op jit(solution)/shard_map/ppermute | solution.py:52
  (33 other events, 413.0 us)

commit v5 on v4

--- a/solution.py
+++ b/solution.py
@@ -40,6 +40,13 @@
 def to_next_section(value):
     count = lax.axis_size("section")
     return lax.ppermute(value, "section", [(i, (i + 1) % count) for i in range(count)])
+
+
+def from_section_before(value):
+    if lax.axis_size("section") != 2:
+        return to_next_section(value)
+    both = lax.all_gather(value, "section", axis=0, tiled=False)
+    return lax.dynamic_index_in_dim(both, 1 - lax.axis_index("section"), 0, keepdims=False)
 
 
 def along_ring(value, step):
@@ -355,12 +362,12 @@
     scalars = jnp.concatenate([jnp.stack([core, chip % 2]).astype(jnp.int32), sources])
 
     keyval_pieces = around(keyval_weight[0], halved=False)
-    query_pieces = around(query_weight[0])
+    query_pieces = around(after(query_weight[0], keyval_pieces[chips // 2][0][1]))
 
     half = ((rows, width // 2), jnp.bfloat16)
     own_rows, sent_rows = run(functools.partial(split_kernel, True), [half, half], scalars, [hidden])
     other_rows = swap_cores(sent_rows)
-    out_shard = to_next_section(out_weight[0])
+    out_shard = from_section_before(out_weight[0])
 
     kept, sent = run(
         functools.partial(keyval_kernel, list(range(chips))),
@@ -371,15 +378,16 @@
         parcel_kernel, [((2 * rows + MARK_ROWS, 256), jnp.bfloat16)], scalars,
         [segment_ids, kept, swap_cores(sent)],
     )
-    back_two = two_chips_on(parcel)
-    back_four = two_chips_on(back_two)
+    steps = [[query_pieces[d][0][1] for d in (step, chips - step)] for step in range(1, 4)]
+    back_two = after(two_chips_on(parcel), *steps[0])
+    back_four = after(two_chips_on(back_two), *steps[1])
     even = chip % 2 == 0
     crossed = swap_chips(jnp.concatenate([jnp.where(even, parcel, back_four), back_two], axis=0))
     window = 5 * 2 * rows
     keys_t, values, lowest = run(
         window_kernel,
         [((2, 2, 128, window), jnp.bfloat16), ((2, 2, window, 128), jnp.bfloat16), ((2 * rows, 128), jnp.int32)],
-        scalars, [back_four, back_two, parcel, crossed],
+        scalars, [back_four, back_two, parcel, crossed], waits=steps[2],
     )
 
     def query_sums(distances, g, waits, before=()):
@@ -404,7 +412,7 @@
         attended.append(attention(lowest, sums[g][0], swap_cores(sums[g][1]), keys_t[g], values[g], waits))
     attended[1] = after(attended[1], *[out_pieces[d][0][1] for d in (2, chips - 2)])
     kept, sent = run(
-        functools.partial(split_kernel, False), [half, half], scalars, [to_next_section(hidden)], waits=attended[:1]
+        functools.partial(split_kernel, False), [half, half], scalars, [from_section_before(hidden)], waits=attended[:1]
     )
     adds = [kept, swap_cores(sent)]
     arrived = []

time: 262 us -> 303 us (1.16)
  local copies, waits for them, and re-layouts: 7.88 us -> 25.9 us
  between operations: 0.41 us -> 13.8 us
  waiting for transfers between devices: 142 us -> 150 us
  Pallas kernels: 64.3 us -> 68.1 us
    ppermute x2, waiting for transfers between devices: 3.4 us -> 28.9 us  [two_chips_on(): return lax.ppermute(value, 'fsdp', [(i, i + 4) for i in range(count - 4)])]
    ppermute x1, waiting for transfers between devices: 21.3 us -> 0.96 us  [swap_chips(): return lax.ppermute(value, 'fsdp', [(i, i ^ 2) for i in range(count)])]
    ppermute x23, waiting for transfers between devices: 93.2 us -> 105 us  [along_ring(): return lax.ppermute(value, 'fsdp', pairs)]
    unnamed x36 -> x61, local copies, waits for them, and re-layouts: 6.05 us -> 16.2 us
    ppermute x4 -> x2, waiting for transfers between devices: 20.4 us -> 12 us  [to_next_section(): lax.ppermute(value, 'section', [(i, (i + 1) % count) for i in range(count)])]
    squeeze x0 -> x2, local copies, waits for them, and re-layouts: none -> 4.3 us  [from_section_before(): lax.dynamic_index_in_dim(both, 1 - lax.axis_index('section'), 0, keepdims...]
    ppermute x4 -> x2, starting transfers between devices: 5.08 us -> 2.02 us  [to_next_section(): lax.ppermute(value, 'section', [(i, (i + 1) % count) for i in range(count)])]
  transfers between devices with their start and end apart: 39 -> 39, of which waited for: 17 -> 22; matrix products, arithmetic and copies ran while one was open for 2% -> 4% of each run, Pallas kernels for 23% -> 21%
where the time goes in v5:
time: 303 us; the launch traced here: 302 us
  waiting for transfers between devices  150 us (50%)
  Pallas kernels  68.1 us (22%)
  starting transfers between devices  41.7 us (14%)
  local copies, waits for them, and re-layouts  25.9 us (9%)
  between operations  13.8 us (5%)
  other arithmetic  3.24 us (1%)
    ppermute x23, waiting for transfers between devices, along_ring(): return lax.ppermute(value, 'fsdp', pairs)  105 us
    pallas_call x13, Pallas kernels, run(): pl.pallas_call(only, in_specs=[pl.BlockSpec(memory_space=pltpu.SMEM)] + [...  34.7 us
    pallas_call x2, Pallas kernels, attention(): pl.pallas_call(only, grid=(rows // TILE,), in_specs=[pl.BlockSpec((TILE,...  33.4 us
    ppermute x2, waiting for transfers between devices, two_chips_on(): return lax.ppermute(value, 'fsdp', [(i, i + 4) for i in range(count - 4)])  28.9 us
    ppermute x23, starting transfers between devices, along_ring(): return lax.ppermute(value, 'fsdp', pairs)  28.1 us
    unnamed x61, local copies, waits for them, and re-layouts  16.2 us
    ppermute x2, waiting for transfers between devices, to_next_section(): lax.ppermute(value, 'section', [(i, (i + 1) % count) for i in range(count)])  12 us
    ppermute x2, starting transfers between devices, two_chips_on(): return lax.ppermute(value, 'fsdp', [(i, i + 4) for i in range(count - 4)])  9.4 us
  transfers between devices with their start and end apart: 39, of which 22 were waited for; matrix products, arithmetic and copies ran while one was open for 4% of the time, Pallas kernels for 21%

profile of v5, /device:TPU:0, one launch (start us, length us, event | category | flops | bytes accessed | tf_op | source)
XLA Modules:
  0.0 302.4 jit_solution(1569918874249865498)
XLA Ops:
  12.0 6.2 %collective-permute-done.4.refs_11_ = bf16[256,512]{1,0:T(8,128)(2,1)S(1)} collective-permute-done((bf16[256,512]{1,0:T(8,128)(2,1)S(1)}, bf16[256,512]{1,0:T(8,128)(2,1)S(1)}, u32[]{:S(2)}, u32[]{:S(2)}) %collective-permute-start.4) | collective-permute-done | bytes 262176 | tf_op jit(solution)/shard_map/ppermute | solution.py:59
  20.8 5.0 %collective-permute-done.5.refs_10_ = bf16[256,512]{1,0:T(8,128)(2,1)S(1)} collective-permute-done((bf16[256,512]{1,0:T(8,128)(2,1)S(1)}, bf16[256,512]{1,0:T(8,128)(2,1)S(1)}, u32[]{:S(2)}, u32[]{:S(2)}) %collective-permute-start.5) | collective-permute-done | bytes 262176 | tf_op jit(solution)/shard_map/ppermute | solution.py:59
  28.0 4.5 %collective-permute-done.6.refs_9_ = bf16[256,512]{1,0:T(8,128)(2,1)S(1)} collective-permute-done((bf16[256,512]{1,0:T(8,128)(2,1)S(1)}, bf16[256,512]{1,0:T(8,128)(2,1)S(1)}, u32[]{:S(2)}, u32[]{:S(2)}) %collective-permute-start.6) | collective-permute-done | bytes 262176 | tf_op jit(solution)/shard_map/ppermute | solution.py:59
  34.4 4.5 %collective-permute-done.7.refs_8_.refs_1_ = bf16[256,512]{1,0:T(8,128)(2,1)S(1)} collective-permute-done((bf16[256,512]{1,0:T(8,128)(2,1)S(1)}, bf16[256,512]{1,0:T(8,128)(2,1)S(1)}, u32[]{:S(2)}, u32[]{:S(2)}) %collective-permute-start.7) | collective-permute-done | bytes 262176 | tf_op jit(solution)/shard_map/ppermute | solution.py:59
  47.9 15.1 %collective-permute-done.11.refs_2_.refs_5_ = bf16[256,2048]{1,0:T(8,128)(2,1)S(1)} collective-permute-done((bf16[256,2048]{1,0:T(8,128)(2,1)}, bf16[256,2048]{1,0:T(8,128)(2,1)S(1)}, u32[]{:S(2)}, u32[]{:S(2)}) %collective-permute-start.11) | collective-permute-done | bytes 1048608 | tf_op jit(solution)/shard_map/ppermute | solution.py:59
  68.0 4.7 %collective-permute-done.1.refs_5_ = bf16[256,512]{1,0:T(8,128)(2,1)S(1)} collective-permute-done((bf16[256,512]{1,0:T(8,128)(2,1)}, bf16[256,512]{1,0:T(8,128)(2,1)S(1)}, u32[]{:S(2)}, u32[]{:S(2)}) %collective-permute-start.1) | collective-permute-done | bytes 262176 | tf_op jit(solution)/shard_map/ppermute | solution.py:59
  73.5 24.4 %collective-permute-done.2.refs_6_ = bf16[256,512]{1,0:T(8,128)(2,1)S(1)} collective-permute-done((bf16[256,512]{1,0:T(8,128)(2,1)S(1)}, bf16[256,512]{1,0:T(8,128)(2,1)S(1)}, u32[]{:S(2)}, u32[]{:S(2)}) %collective-permute-start.2) | collective-permute-done | bytes 262176 | tf_op jit(solution)/shard_map/ppermute | solution.py:59
  98.7 5.5 %collective-permute-done.3.refs_7_ = bf16[256,512]{1,0:T(8,128)(2,1)S(1)} collective-permute-done((bf16[256,512]{1,0:T(8,128)(2,1)S(1)}, bf16[256,512]{1,0:T(8,128)(2,1)S(1)}, u32[]{:S(2)}, u32[]{:S(2)}) %collective-permute-start.3) | collective-permute-done | bytes 262176 | tf_op jit(solution)/shard_map/ppermute | solution.py:59
  112.8 4.2 %collective-permute-start.9 = (bf16[528,256]{1,0:T(8,128)(2,1)S(1)}, bf16[528,256]{1,0:T(8,128)(2,1)}, u32[]{:S(2)}, u32[]{:S(2)}) collective-permute-start(bf16[528,256]{1,0:T(8,128)(2,1)S(1)} %shard_map.66.refs_3_.refs_8_), channel_id=1, source_target_pairs={{0,4},{1,5},{2,6},{3,7},{4,8},{5,9},{6,10},{7,11},{8,12},{9,13},{1... | collective-permute-start | bytes 811016 | tf_op jit(solution)/shard_map/ppermute | solution.py:37
  117.0 23.8 %collective-permute-done.9.refs_0_ = bf16[528,256]{1,0:T(8,128)(2,1)} collective-permute-done((bf16[528,256]{1,0:T(8,128)(2,1)S(1)}, bf16[528,256]{1,0:T(8,128)(2,1)}, u32[]{:S(2)}, u32[]{:S(2)}) %collective-permute-start.9) | collective-permute-done | bytes 270368 | tf_op jit(solution)/shard_map/ppermute | solution.py:37
  140.8 5.2 %collective-permute-start.12 = (bf16[528,256]{1,0:T(8,128)(2,1)}, bf16[528,256]{1,0:T(8,128)(2,1)}, u32[]{:S(2)}, u32[]{:S(2)}) collective-permute-start(bf16[528,256]{1,0:T(8,128)(2,1)} %shard_map.68.refs_2_), channel_id=1, source_target_pairs={{0,4},{1,5},{2,6},{3,7},{4,8},{5,9},{6,10},{7,11},{8,12},{9,13},{1... | collective-permute-start | bytes 811016 | tf_op jit(solution)/shard_map/ppermute | solution.py:37
  146.0 5.2 %collective-permute-done.12.refs_0_ = bf16[528,256]{1,0:T(8,128)(2,1)} collective-permute-done((bf16[528,256]{1,0:T(8,128)(2,1)}, bf16[528,256]{1,0:T(8,128)(2,1)}, u32[]{:S(2)}, u32[]{:S(2)}) %collective-permute-start.12) | collective-permute-done | bytes 270368 | tf_op jit(solution)/shard_map/ppermute | solution.py:37
  162.2 5.0 %collective-permute-done.18.refs_1_.refs_5_ = bf16[128,2048]{1,0:T(8,128)(2,1)} collective-permute-done((bf16[128,2048]{1,0:T(8,128)(2,1)}, bf16[128,2048]{1,0:T(8,128)(2,1)}, u32[]{:S(2)}, u32[]{:S(2)}) %collective-permute-start.18) | collective-permute-done | bytes 524320 | tf_op jit(solution)/shard_map/ppermute | solution.py:59
  172.9 3.4 %shard_map.71 = (f32[512,512]{1,0:T(8,128)S(1)}, f32[512,512]{1,0:T(8,128)S(1)}) custom-call(s32[10]{0:T(128)S(1)} %pad_add_fusion.refs_0_, bf16[256,2048]{1,0:T(8,128)(2,1)S(1)} %get-tuple-element.30.refs_2_.refs_1_, bf16[256,2048]{1,0:T(8,128)(2,1)S(1)} %collective-permute-done.refs_3_.refs_2_, bf16[256,2048]{1,0:T(8,128)(2,1)S(1)} %copy-done.1, ...), custom_call_target="tpu_custom_call" | custom-call | flops 1000000 | bytes 100000 | tf_op jit(solution)/shard_map/pallas_call | solution.py:69
  176.3 3.5 %shard_map.75 = (f32[512,512]{1,0:T(8,128)S(1)}, f32[512,512]{1,0:T(8,128)S(1)}) custom-call(s32[10]{0:T(128)S(1)} %pad_add_fusion.refs_0_, bf16[256,2048]{1,0:T(8,128)(2,1)S(1)} %get-tuple-element.30.refs_2_.refs_1_, bf16[256,2048]{1,0:T(8,128)(2,1)S(1)} %collective-permute-done.refs_3_.refs_2_, bf16[256,2048]{1,0:T(8,128)(2,1)S(1)} %copy-done.1, ...), custom_call_target="tpu_custom_call" | custom-call | flops 1000000 | bytes 100000 | tf_op jit(solution)/shard_map/pallas_call | solution.py:69
  185.6 3.8 %shard_map.73 = (f32[512,512]{1,0:T(8,128)S(1)}, f32[512,512]{1,0:T(8,128)}) custom-call(s32[10]{0:T(128)S(1)} %pad_add_fusion.refs_0_, bf16[256,2048]{1,0:T(8,128)(2,1)S(1)} %get-tuple-element.30.refs_2_.refs_1_, bf16[256,2048]{1,0:T(8,128)(2,1)S(1)} %collective-permute-done.refs_3_.refs_2_, bf16[256,2048]{1,0:T(8,128)(2,1)} %collective-permute-done.16.refs_5_.refs_3_, ...), custom_call_target="tpu_custom_call" | custom-call | flops 1000000 | bytes 100000 | tf_op jit(solution)/shard_map/pallas_call | solution.py:69
  189.3 4.2 %shard_map.76 = (f32[512,512]{1,0:T(8,128)S(1)}, f32[512,512]{1,0:T(8,128)}) custom-call(s32[10]{0:T(128)S(1)} %pad_add_fusion.refs_0_, bf16[256,2048]{1,0:T(8,128)(2,1)S(1)} %get-tuple-element.30.refs_2_.refs_1_, bf16[256,2048]{1,0:T(8,128)(2,1)S(1)} %collective-permute-done.refs_3_.refs_2_, bf16[256,2048]{1,0:T(8,128)(2,1)} %collective-permute-done.16.refs_5_.refs_3_, ...), custom_call_target="tpu_custom_call" | custom-call | flops 1000000 | bytes 100000 | tf_op jit(solution)/shard_map/pallas_call | solution.py:69
  194.6 6.3 %collective-permute-done.24.refs_5_.refs_8_ = bf16[2048,256]{1,0:T(8,128)(2,1)} collective-permute-done((bf16[2048,256]{1,0:T(8,128)(2,1)}, bf16[2048,256]{1,0:T(8,128)(2,1)}, u32[]{:S(2)}, u32[]{:S(2)}) %collective-permute-start.24) | collective-permute-done | bytes 1048608 | tf_op jit(solution)/shard_map/ppermute | solution.py:59
  207.5 16.9 %shard_map.74.refs_2_ = bf16[512,512]{1,0:T(8,128)(2,1)} custom-call(s32[512,128]{1,0:T(8,128)S(1)} %copy-done.19, f32[512,512]{1,0:T(8,128)S(1)} %copy-done.15, f32[512,512]{1,0:T(8,128)} %collective-permute-done.20.refs_2_, bf16[2,128,2560]{2,1,0:T(8,128)(2,1)S(1)} %copy-done.7, bf16[2,2560,128]{2,1,0:T(8,128)(2,1)S(1)} %get-tuple-element.54.refs_4_), custom_call_target="tpu_custom_call" | custom-call | flops 1000000 | bytes 100000 | tf_op jit(solution)/shard_map/pallas_call | solution.py:287
  227.8 16.5 %shard_map.77.refs_0_ = bf16[512,512]{1,0:T(8,128)(2,1)S(1)} custom-call(s32[512,128]{1,0:T(8,128)S(1)} %copy-done.19, f32[512,512]{1,0:T(8,128)S(1)} %copy-done.17, f32[512,512]{1,0:T(8,128)} %collective-permute-done.23.refs_2_, bf16[2,128,2560]{2,1,0:T(8,128)(2,1)S(1)} %copy-done.8, bf16[2,2560,128]{2,1,0:T(8,128)(2,1)S(1)} %get-tuple-element.53.refs_4_, ...), custom_call_target="tpu_custom_call" | custom-call | flops 1000000 | bytes 100000 | tf_op jit(solution)/shard_map/pallas_call | solution.py:287
  247.6 12.0 %collective-permute-done.28.refs_3_ = bf16[512,512]{1,0:T(8,128)(2,1)S(1)} collective-permute-done((bf16[512,512]{1,0:T(8,128)(2,1)}, bf16[512,512]{1,0:T(8,128)(2,1)S(1)}, u32[]{:S(2)}, u32[]{:S(2)}) %collective-permute-start.28) | collective-permute-done | bytes 524320 | tf_op jit(solution)/shard_map/ppermute | solution.py:42
  261.5 5.4 %shard_map.80 = (bf16[256,2048]{1,0:T(8,128)(2,1)S(1)}, bf16[256,2048]{1,0:T(8,128)(2,1)S(1)}) custom-call(s32[10]{0:T(128)S(1)} %pad_add_fusion.refs_0_, bf16[512,512]{1,0:T(8,128)(2,1)} %collective-permute-done.21.refs_1_, bf16[512,512]{1,0:T(8,128)(2,1)S(1)} %collective-permute-done.22.refs_2_, bf16[512,512]{1,0:T(8,128)(2,1)S(1)} %collective-permute-done.28.refs_3_, ...), custom_call_target="tpu_custom_call" | custom-call | flops 1000000 | bytes 100000 | tf_op jit(solution)/shard_map/pallas_call | solution.py:69
  266.9 4.2 %collective-permute-done.31.refs_7_ = bf16[2048,256]{1,0:T(8,128)(2,1)S(1)} collective-permute-done((bf16[2048,256]{1,0:T(8,128)(2,1)}, bf16[2048,256]{1,0:T(8,128)(2,1)S(1)}, u32[]{:S(2)}, u32[]{:S(2)}) %collective-permute-start.31) | collective-permute-done | bytes 1048608 | tf_op jit(solution)/shard_map/ppermute | solution.py:59
  277.6 12.2 %collective-permute-done.34.refs_7_ = bf16[1024,256]{1,0:T(8,128)(2,1)S(1)} collective-permute-done((bf16[1024,256]{1,0:T(8,128)(2,1)S(1)}, bf16[1024,256]{1,0:T(8,128)(2,1)S(1)}, u32[]{:S(2)}, u32[]{:S(2)}) %collective-permute-start.34) | collective-permute-done | bytes 524320 | tf_op jit(solution)/shard_map/ppermute | solution.py:59
  (152 shorter events, 87.2 us)
Async XLA Ops:
  6.5 153.4 %all-gather.3.cloned.1.call-start = ((), (), s32[]{:S(2)}) async-start(), calls=%async_computation | async-start | bytes 3145728 | tf_op jit(solution)/shard_map/all_gather | solution.py:48
  8.9 194.5 %all-gather.5.cloned.1.call-start = ((), (), s32[]{:S(2)}) async-start(), calls=%async_computation.1 | async-start | bytes 6291456 | tf_op jit(solution)/shard_map/all_gather | solution.py:48
  39.6 23.4 %collective-permute-start.11 = (bf16[256,2048]{1,0:T(8,128)(2,1)}, bf16[256,2048]{1,0:T(8,128)(2,1)S(1)}, u32[]{:S(2)}, u32[]{:S(2)}) collective-permute-start(bf16[256,2048]{1,0:T(8,128)(2,1)} %shard_map.67.refs_3_), channel_id=1, source_target_pairs={{0,4},{1,5},{4,8},{5,9},{8,12},{9,13},{12,14},{13,15},{14,10},{15,... | collective-permute-start | bytes 3145736 | tf_op jit(solution)/shard_map/ppermute | solution.py:59
  40.7 26.4 %collective-permute-start.10 = (bf16[256,2048]{1,0:T(8,128)(2,1)}, bf16[256,2048]{1,0:T(8,128)(2,1)}, u32[]{:S(2)}, u32[]{:S(2)}) collective-permute-start(bf16[256,2048]{1,0:T(8,128)(2,1)} %shard_map.67.refs_3_), channel_id=1, source_target_pairs={{0,2},{1,3},{4,0},{5,1},{8,4},{9,5},{12,8},{13,9},{14,12},{15,13},... | collective-permute-start | bytes 3145736 | tf_op jit(solution)/shard_map/ppermute | solution.py:59
  46.6 57.6 %collective-permute-start = (bf16[256,2048]{1,0:T(8,128)(2,1)S(1)}, bf16[256,2048]{1,0:T(8,128)(2,1)S(1)}, u32[]{:S(2)}, u32[]{:S(2)}) collective-permute-start(bf16[256,2048]{1,0:T(8,128)(2,1)S(1)} %get-tuple-element.31), channel_id=1, source_target_pairs={{0,1},{1,0},{2,3},{3,2},{4,5},{5,4},{6,7},{7,6},{8,9},{9,8},{10,11... | collective-permute-start | bytes 3145736 | tf_op jit(solution)/shard_map/ppermute | solution.py:27
  46.7 25.9 %collective-permute-start.1 = (bf16[256,512]{1,0:T(8,128)(2,1)}, bf16[256,512]{1,0:T(8,128)(2,1)S(1)}, u32[]{:S(2)}, u32[]{:S(2)}) collective-permute-start(bf16[256,512]{1,0:T(8,128)(2,1)} %bitcast.22), channel_id=1, source_target_pairs={{0,2},{1,3},{4,0},{5,1},{8,4},{9,5},{12,8},{13,9},{14,12},{15,13},... | collective-permute-start | bytes 786440 | tf_op jit(solution)/shard_map/ppermute | solution.py:59
  63.0 47.1 %collective-permute-start.14 = (bf16[256,2048]{1,0:T(8,128)(2,1)S(1)}, bf16[256,2048]{1,0:T(8,128)(2,1)}, u32[]{:S(2)}, u32[]{:S(2)}) collective-permute-start(bf16[256,2048]{1,0:T(8,128)(2,1)S(1)} %collective-permute-done.11.refs_2_.refs_5_), channel_id=1, source_target_pairs={{0,4},{1,5},{4,8},{5,9},{8,12},{9,13},{12,14},{13,15},{14,10},{15,... | collective-permute-start | bytes 3145736 | tf_op jit(solution)/shard_map/ppermute | solution.py:59
  67.1 44.6 %collective-permute-start.13 = (bf16[256,2048]{1,0:T(8,128)(2,1)}, bf16[256,2048]{1,0:T(8,128)(2,1)}, u32[]{:S(2)}, u32[]{:S(2)}) collective-permute-start(bf16[256,2048]{1,0:T(8,128)(2,1)} %collective-permute-done.10.refs_1_.refs_4_), channel_id=1, source_target_pairs={{0,2},{1,3},{4,0},{5,1},{8,4},{9,5},{12,8},{13,9},{14,12},{15,13},... | collective-permute-start | bytes 3145736 | tf_op jit(solution)/shard_map/ppermute | solution.py:59
  72.7 25.2 %collective-permute-start.2 = (bf16[256,512]{1,0:T(8,128)(2,1)S(1)}, bf16[256,512]{1,0:T(8,128)(2,1)S(1)}, u32[]{:S(2)}, u32[]{:S(2)}) collective-permute-start(bf16[256,512]{1,0:T(8,128)(2,1)S(1)} %collective-permute-done.1.refs_5_), channel_id=1, source_target_pairs={{0,2},{1,3},{4,0},{5,1},{8,4},{9,5},{12,8},{13,9},{14,12},{15,13},... | collective-permute-start | bytes 786440 | tf_op jit(solution)/shard_map/ppermute | solution.py:59
  110.1 41.0 %collective-permute-start.17 = (bf16[256,2048]{1,0:T(8,128)(2,1)}, bf16[256,2048]{1,0:T(8,128)(2,1)S(1)}, u32[]{:S(2)}, u32[]{:S(2)}) collective-permute-start(bf16[256,2048]{1,0:T(8,128)(2,1)} %collective-permute-done.14.refs_2_.refs_7_), channel_id=1, source_target_pairs={{0,4},{1,5},{4,8},{5,9},{8,12},{9,13},{12,14},{13,15},{14,10},{15,... | collective-permute-start | bytes 3145736 | tf_op jit(solution)/shard_map/ppermute | solution.py:59
  111.7 42.8 %collective-permute-start.16 = (bf16[256,2048]{1,0:T(8,128)(2,1)}, bf16[256,2048]{1,0:T(8,128)(2,1)}, u32[]{:S(2)}, u32[]{:S(2)}) collective-permute-start(bf16[256,2048]{1,0:T(8,128)(2,1)} %collective-permute-done.13.refs_1_.refs_6_), channel_id=1, source_target_pairs={{0,2},{1,3},{4,0},{5,1},{8,4},{9,5},{12,8},{13,9},{14,12},{15,13},... | collective-permute-start | bytes 3145736 | tf_op jit(solution)/shard_map/ppermute | solution.py:59
  112.8 28.0 %collective-permute-start.9 = (bf16[528,256]{1,0:T(8,128)(2,1)S(1)}, bf16[528,256]{1,0:T(8,128)(2,1)}, u32[]{:S(2)}, u32[]{:S(2)}) collective-permute-start(bf16[528,256]{1,0:T(8,128)(2,1)S(1)} %shard_map.66.refs_3_.refs_8_), channel_id=1, source_target_pairs={{0,4},{1,5},{2,6},{3,7},{4,8},{5,9},{6,10},{7,11},{8,12},{9,13},{1... | collective-permute-start | bytes 811016 | tf_op jit(solution)/shard_map/ppermute | solution.py:37
  158.2 22.5 %collective-permute-start.15 = (bf16[1056,256]{1,0:T(8,128)(2,1)}, bf16[1056,256]{1,0:T(8,128)(2,1)}, u32[]{:S(2)}, u32[]{:S(2)}) collective-permute-start(bf16[1056,256]{1,0:T(8,128)(2,1)} %pad_maximum_fusion), channel_id=1, source_target_pairs={{0,2},{1,3},{2,0},{3,1},{4,6},{5,7},{6,4},{7,5},{8,10},{9,11},{10,... | collective-permute-start | bytes 1622024 | tf_op jit(solution)/shard_map/ppermute | solution.py:32
  169.2 31.8 %collective-permute-start.24 = (bf16[2048,256]{1,0:T(8,128)(2,1)}, bf16[2048,256]{1,0:T(8,128)(2,1)}, u32[]{:S(2)}, u32[]{:S(2)}) collective-permute-start(bf16[2048,256]{1,0:T(8,128)(2,1)} %shard_map.72.refs_10_.refs_7_), channel_id=1, source_target_pairs={{0,2},{1,3},{4,0},{5,1},{8,4},{9,5},{12,8},{13,9},{14,12},{15,13},... | collective-permute-start | bytes 3145736 | tf_op jit(solution)/shard_map/ppermute | solution.py:59
  171.6 31.8 %collective-permute-start.25 = (bf16[2048,256]{1,0:T(8,128)(2,1)}, bf16[2048,256]{1,0:T(8,128)(2,1)}, u32[]{:S(2)}, u32[]{:S(2)}) collective-permute-start(bf16[2048,256]{1,0:T(8,128)(2,1)} %shard_map.72.refs_10_.refs_7_), channel_id=1, source_target_pairs={{0,4},{1,5},{4,8},{5,9},{8,12},{9,13},{12,14},{13,15},{14,10},{15,... | collective-permute-start | bytes 3145736 | tf_op jit(solution)/shard_map/ppermute | solution.py:59
  189.3 16.6 %collective-permute-start.20 = (f32[512,512]{1,0:T(8,128)}, f32[512,512]{1,0:T(8,128)}, u32[]{:S(2)}, u32[]{:S(2)}) collective-permute-start(f32[512,512]{1,0:T(8,128)} %get-tuple-element.39), channel_id=1, source_target_pairs={{0,1},{1,0},{2,3},{3,2},{4,5},{5,4},{6,7},{7,6},{8,9},{9,8},{10,11... | collective-permute-start | bytes 3145736 | tf_op jit(solution)/shard_map/ppermute | solution.py:27
  194.5 33.3 %collective-permute-start.23 = (f32[512,512]{1,0:T(8,128)}, f32[512,512]{1,0:T(8,128)}, u32[]{:S(2)}, u32[]{:S(2)}) collective-permute-start(f32[512,512]{1,0:T(8,128)} %get-tuple-element.44), channel_id=1, source_target_pairs={{0,1},{1,0},{2,3},{3,2},{4,5},{5,4},{6,7},{7,6},{8,9},{9,8},{10,11... | collective-permute-start | bytes 3145736 | tf_op jit(solution)/shard_map/ppermute | solution.py:27
  200.9 44.1 %collective-permute-start.26 = (bf16[2048,256]{1,0:T(8,128)(2,1)}, bf16[2048,256]{1,0:T(8,128)(2,1)}, u32[]{:S(2)}, u32[]{:S(2)}) collective-permute-start(bf16[2048,256]{1,0:T(8,128)(2,1)} %collective-permute-done.24.refs_5_.refs_8_), channel_id=1, source_target_pairs={{0,2},{1,3},{4,0},{5,1},{8,4},{9,5},{12,8},{13,9},{14,12},{15,13},... | collective-permute-start | bytes 3145736 | tf_op jit(solution)/shard_map/ppermute | solution.py:59
  203.4 41.7 %collective-permute-start.27 = (bf16[2048,256]{1,0:T(8,128)(2,1)}, bf16[2048,256]{1,0:T(8,128)(2,1)}, u32[]{:S(2)}, u32[]{:S(2)}) collective-permute-start(bf16[2048,256]{1,0:T(8,128)(2,1)} %collective-permute-done.25.refs_6_.refs_9_), channel_id=1, source_target_pairs={{0,4},{1,5},{4,8},{5,9},{8,12},{9,13},{12,14},{13,15},{14,10},{15,... | collective-permute-start | bytes 3145736 | tf_op jit(solution)/shard_map/ppermute | solution.py:59
  224.4 23.2 %collective-permute-start.21 = (bf16[512,512]{1,0:T(8,128)(2,1)}, bf16[512,512]{1,0:T(8,128)(2,1)}, u32[]{:S(2)}, u32[]{:S(2)}) collective-permute-start(bf16[512,512]{1,0:T(8,128)(2,1)} %shard_map.74.refs_2_), channel_id=1, source_target_pairs={{0,16},{16,0},{1,17},{17,1},{2,18},{18,2},{3,19},{19,3},{4,20},{20... | collective-permute-start | bytes 1572872 | tf_op jit(solution)/shard_map/ppermute | solution.py:42
  227.8 31.9 %collective-permute-start.30 = (bf16[256,2048]{1,0:T(8,128)(2,1)}, bf16[256,2048]{1,0:T(8,128)(2,1)S(1)}, u32[]{:S(2)}, u32[]{:S(2)}) collective-permute-start(bf16[256,2048]{1,0:T(8,128)(2,1)} %get-tuple-element.46), channel_id=1, source_target_pairs={{0,1},{1,0},{2,3},{3,2},{4,5},{5,4},{6,7},{7,6},{8,9},{9,8},{10,11... | collective-permute-start | bytes 3145736 | tf_op jit(solution)/shard_map/ppermute | solution.py:27
  245.6 25.5 %collective-permute-start.31 = (bf16[2048,256]{1,0:T(8,128)(2,1)}, bf16[2048,256]{1,0:T(8,128)(2,1)S(1)}, u32[]{:S(2)}, u32[]{:S(2)}) collective-permute-start(bf16[2048,256]{1,0:T(8,128)(2,1)} %collective-permute-done.26.refs_1_.refs_10_), channel_id=1, source_target_pairs={{0,2},{1,3},{4,0},{5,1},{8,4},{9,5},{12,8},{13,9},{14,12},{15,13},... | collective-permute-start | bytes 3145736 | tf_op jit(solution)/shard_map/ppermute | solution.py:59
  247.6 25.2 %collective-permute-start.32 = (bf16[2048,256]{1,0:T(8,128)(2,1)}, bf16[2048,256]{1,0:T(8,128)(2,1)S(1)}, u32[]{:S(2)}, u32[]{:S(2)}) collective-permute-start(bf16[2048,256]{1,0:T(8,128)(2,1)} %collective-permute-done.27.refs_2_.refs_11_), channel_id=1, source_target_pairs={{0,4},{1,5},{4,8},{5,9},{8,12},{9,13},{12,14},{13,15},{14,10},{15,... | collective-permute-start | bytes 3145736 | tf_op jit(solution)/shard_map/ppermute | solution.py:59
  275.3 18.0 %collective-permute-start.33 = (bf16[256,2048]{1,0:T(8,128)(2,1)S(1)}, bf16[256,2048]{1,0:T(8,128)(2,1)S(1)}, u32[]{:S(2)}, u32[]{:S(2)}) collective-permute-start(bf16[256,2048]{1,0:T(8,128)(2,1)S(1)} %get-tuple-element.50), channel_id=1, source_target_pairs={{0,1},{1,0},{2,3},{3,2},{4,5},{5,4},{6,7},{7,6},{8,9},{9,8},{10,11... | collective-permute-start | bytes 3145736 | tf_op jit(solution)/shard_map/ppermute | solution.py:27
  (45 other events, 374.8 us)
Sparse Core Ops, SparseCore 0:
  9.0 35.7 all-gather.2
  46.4 56.7 all-gather.4

commit v6 on v5

--- a/solution.py
+++ b/solution.py
@@ -27,14 +27,10 @@
     return lax.ppermute(value, "fsdp", [(i, i ^ 1) for i in range(count)])
 
 
-def swap_chips(value):
+def gathered(value):
     count = lax.axis_size("fsdp")
-    return lax.ppermute(value, "fsdp", [(i, i ^ 2) for i in range(count)])
-
-
-def two_chips_on(value):
-    count = lax.axis_size("fsdp")
-    return lax.ppermute(value, "fsdp", [(i, i + 4) for i in range(count - 4)])
+    groups = [list(range(core, count, 2)) for core in range(2)]
+    return lax.all_gather(value, "fsdp", axis=0, tiled=False, axis_index_groups=groups)
 
 
 def to_next_section(value):
@@ -170,32 +166,35 @@
     out_ref[count:, :] = marks.astype(out_ref.dtype)
 
 
-def window_kernel(scal_ref, four_ref, two_ref, own_ref, crossed_ref, kt_ref, v_ref, lo_ref):
-    odd = scal_ref[1]
-    length = own_ref.shape[0]
-    count = length - MARK_ROWS
+def copy_kernel(scal_ref, in_ref, out_ref):
+    out_ref[...] = in_ref[...]
+
+
+def window_kernel(back, scal_ref, parcels_ref, *refs):
+    kt_refs, v_refs, lo_ref = refs[:2], refs[2:4], refs[4]
+    chip = scal_ref[1]
+    count = parcels_ref.shape[1] - MARK_ROWS
     half = count // 2
-    second = pl.multiple_of(odd * length, MARK_ROWS)
-    fourth = pl.multiple_of((1 - odd) * length, MARK_ROWS)
-    places = [(four_ref, 0), (crossed_ref, second), (two_ref, 0), (crossed_ref, fourth), (own_ref, 0)]
     lane = lax.broadcasted_iota(jnp.int32, (count, 128), 1)
     blank = jnp.zeros((HEAD_SIZE, count), jnp.bfloat16)
     marks = []
-    for i, (ref, first) in enumerate(places):
+    for i in range(back + 1):
+        source = chip - back + i
+        ref = parcels_ref.at[jnp.maximum(source, 0)]
         at = slice(i * count, (i + 1) * count)
-        keys = ref[pl.ds(first, count), 0:128].astype(jnp.float32).T.astype(jnp.bfloat16)
-        values = ref[pl.ds(first, count), 128:256].astype(jnp.float32)
+        keys = ref[:count, 0:128].astype(jnp.float32).T.astype(jnp.bfloat16)
+        values = ref[:count, 128:256].astype(jnp.float32)
         turned = pltpu.roll(values, HEAD_SIZE, 1)
         for g in range(2):
             head = keys[g * HEAD_SIZE:(g + 1) * HEAD_SIZE]
-            kt_ref[g, 0, :HEAD_SIZE, at] = head
-            kt_ref[g, 0, HEAD_SIZE:, at] = blank
-            kt_ref[g, 1, :HEAD_SIZE, at] = blank
-            kt_ref[g, 1, HEAD_SIZE:, at] = head
+            kt_refs[g][0, :HEAD_SIZE, at] = head
+            kt_refs[g][0, HEAD_SIZE:, at] = blank
+            kt_refs[g][1, :HEAD_SIZE, at] = blank
+            kt_refs[g][1, HEAD_SIZE:, at] = head
             low, high = (values, turned) if g == 0 else (turned, values)
-            v_ref[g, 0, at, :] = jnp.where(lane < HEAD_SIZE, low, 0.0).astype(jnp.bfloat16)
-            v_ref[g, 1, at, :] = jnp.where(lane < HEAD_SIZE, 0.0, high).astype(jnp.bfloat16)
-        found = ref[pl.ds(first + count, MARK_ROWS), :].astype(jnp.float32)
+            v_refs[g][0, at, :] = jnp.where(lane < HEAD_SIZE, low, 0.0).astype(jnp.bfloat16)
+            v_refs[g][1, at, :] = jnp.where(lane < HEAD_SIZE, 0.0, high).astype(jnp.bfloat16)
+        found = jnp.where(source >= 0, ref[count:, :].astype(jnp.float32), 0.0)
         marks += [found[0:1, :], found[1:2, :]]
     across = lax.broadcasted_iota(jnp.int32, (half, half), 1)
     down = lax.broadcasted_iota(jnp.int32, (half, half), 0)
@@ -355,19 +354,25 @@
     rows, width = hidden.shape
     device = lax.axis_index("fsdp")
     chips = lax.axis_size("fsdp") // 2
-    chip, core = device // 2, device % 2
-    order = jnp.array(ring_order(chips), jnp.int32)
-    place = jnp.argmax(order == chip).astype(jnp.int32)
-    sources = order[(place + jnp.arange(chips, dtype=jnp.int32)) % chips]
-    scalars = jnp.concatenate([jnp.stack([core, chip % 2]).astype(jnp.int32), sources])
+    order = ring_order(chips)
+    table = []
+    for i in range(2 * chips):
+        place = order.index(i // 2)
+        table.append([i % 2, i // 2] + [order[(place + d) % chips] for d in range(chips)])
+    scalars = lax.dynamic_index_in_dim(jnp.array(table, jnp.int32), device, 0, keepdims=False)
 
     keyval_pieces = around(keyval_weight[0], halved=False)
-    query_pieces = around(after(query_weight[0], keyval_pieces[chips // 2][0][1]))
+    out_shard = to_next_section(out_weight[0])
+    kv_steps = [keyval_pieces[d][0][1] for d in (3, chips - 3)]
+    query_shard, = run(
+        copy_kernel, [(query_weight.shape[1:], jnp.bfloat16)], scalars, [query_weight[0]],
+        waits=kv_steps + [out_shard],
+    )
+    query_pieces = around(query_shard)
 
     half = ((rows, width // 2), jnp.bfloat16)
     own_rows, sent_rows = run(functools.partial(split_kernel, True), [half, half], scalars, [hidden])
     other_rows = swap_cores(sent_rows)
-    out_shard = from_section_before(out_weight[0])
 
     kept, sent = run(
         functools.partial(keyval_kernel, list(range(chips))),
@@ -378,16 +383,13 @@
         parcel_kernel, [((2 * rows + MARK_ROWS, 256), jnp.bfloat16)], scalars,
         [segment_ids, kept, swap_cores(sent)],
     )
-    steps = [[query_pieces[d][0][1] for d in (step, chips - step)] for step in range(1, 4)]
-    back_two = after(two_chips_on(parcel), *steps[0])
-    back_four = after(two_chips_on(back_two), *steps[1])
-    even = chip % 2 == 0
-    crossed = swap_chips(jnp.concatenate([jnp.where(even, parcel, back_four), back_two], axis=0))
-    window = 5 * 2 * rows
-    keys_t, values, lowest = run(
-        window_kernel,
-        [((2, 2, 128, window), jnp.bfloat16), ((2, 2, window, 128), jnp.bfloat16), ((2 * rows, 128), jnp.int32)],
-        scalars, [back_four, back_two, parcel, crossed], waits=steps[2],
+    back = -(-LOOKBACK_SPAN // (2 * rows))
+    window = (back + 1) * 2 * rows
+    *heads, lowest = run(
+        functools.partial(window_kernel, back),
+        [((2, 128, window), jnp.bfloat16)] * 2 + [((2, window, 128), jnp.bfloat16)] * 2
+        + [((2 * rows, 128), jnp.int32)],
+        scalars, [gathered(parcel)],
     )
 
     def query_sums(distances, g, waits, before=()):
@@ -402,14 +404,14 @@
     near = [0, 1, chips - 1, 2, chips - 2]
     next_far = [3, chips - 3]
     far = [chips // 2]
-    out_shard = after(out_shard, *[piece for _, piece in query_pieces[chips // 2]])
+    sums = [query_sums(near, g, [parcel]) for g in range(2)]
+    out_shard = after(out_shard, *[piece for _, piece in query_pieces[chips // 2]], sums[0][0], sums[1][0])
     out_pieces = around(out_shard)
-    sums = [query_sums(near, g, [parcel]) for g in range(2)]
-    sums = [query_sums(next_far + far, g, [keys_t, out_shard], sums[g]) for g in range(2)]
+    sums = [query_sums(next_far + far, g, [lowest, out_shard], sums[g]) for g in range(2)]
     attended = []
     for g in range(2):
         waits = [out_pieces[d][0][1] for d in (1, chips - 1)] if g else []
-        attended.append(attention(lowest, sums[g][0], swap_cores(sums[g][1]), keys_t[g], values[g], waits))
+        attended.append(attention(lowest, sums[g][0], swap_cores(sums[g][1]), heads[g], heads[2 + g], waits))
     attended[1] = after(attended[1], *[out_pieces[d][0][1] for d in (2, chips - 2)])
     kept, sent = run(
         functools.partial(split_kernel, False), [half, half], scalars, [from_section_before(hidden)], waits=attended[:1]

time: 303 us -> 300 us (0.990)
  starting transfers between devices: 41.7 us -> 31 us
  waiting for transfers between devices: 150 us -> 159 us
  other arithmetic: 3.24 us -> 0 us
    ppermute x3 -> x0, waiting for transfers between devices: 29.9 us -> none  [the longest x2 28.9 us: two_chips_on(): return lax.ppermute(value, 'fsdp', [(i, i + 4) for i in range(count - 4)])]
    ppermute x2 -> x3, waiting for transfers between devices: 12 us -> 36.1 us  [to_next_section(): lax.ppermute(value, 'section', [(i, (i + 1) % count) for i in range(count)])]
    ppermute x23, waiting for transfers between devices: 105 us -> 118 us  [along_ring(): return lax.ppermute(value, 'fsdp', pairs)]
    ppermute x3 -> x0, starting transfers between devices: 11.1 us -> none  [the longest x2 9.4 us: two_chips_on(): return lax.ppermute(value, 'fsdp', [(i, i + 4) for i in range(count - 4)])]
    unnamed x61 -> x80, local copies, waits for them, and re-layouts: 16.2 us -> 24.3 us
    pallas_call x13 -> x14, Pallas kernels: 34.7 us -> 34 us  [run(): pl.pallas_call(only, in_specs=[pl.BlockSpec(memory_space=pltpu.SMEM)] + [...]
  transfers between devices with their start and end apart: 39 -> 37, of which waited for: 22 -> 17; matrix products, arithmetic and copies ran while one was open for 4% -> 1% of each run, Pallas kernels for 21% -> 20%
where the time goes in v6:
time: 300 us
  waiting for transfers between devices  159 us (53%)
  Pallas kernels  68.4 us (23%)
  starting transfers between devices  31 us (10%)
  local copies, waits for them, and re-layouts  27.1 us (9%)
  between operations  13.8 us (5%)
    ppermute x23, waiting for transfers between devices, along_ring(): return lax.ppermute(value, 'fsdp', pairs)  118 us
    ppermute x3, waiting for transfers between devices, to_next_section(): lax.ppermute(value, 'section', [(i, (i + 1) % count) for i in range(count)])  36.1 us
    pallas_call x2, Pallas kernels, attention(): pl.pallas_call(only, grid=(rows // TILE,), in_specs=[pl.BlockSpec((TILE,...  34.4 us
    pallas_call x14, Pallas kernels, run(): pl.pallas_call(only, in_specs=[pl.BlockSpec(memory_space=pltpu.SMEM)] + [...  34 us
    ppermute x23, starting transfers between devices, along_ring(): return lax.ppermute(value, 'fsdp', pairs)  26.9 us
    unnamed x80, local copies, waits for them, and re-layouts  24.3 us
  transfers between devices with their start and end apart: 37, of which 17 were waited for; matrix products, arithmetic and copies ran while one was open for 1% of the time, Pallas kernels for 20%

profile of v6, /device:TPU:0, one launch (start us, length us, event | category | flops | bytes accessed | tf_op | source)
XLA Modules:
  0.0 299.6 jit_solution(11923184629004835613)
XLA Ops:
  6.5 3.0 %collective-permute-start.4 = (bf16[256,512]{1,0:T(8,128)(2,1)}, bf16[256,512]{1,0:T(8,128)(2,1)S(1)}, u32[]{:S(2)}, u32[]{:S(2)}) collective-permute-start(bf16[256,512]{1,0:T(8,128)(2,1)} %bitcast.13), channel_id=1, source_target_pairs={{0,4},{1,5},{4,8},{5,9},{8,12},{9,13},{12,14},{13,15},{14,10},{15,... | collective-permute-start | bytes 786440 | tf_op jit(solution)/shard_map/ppermute | solution.py:55
  13.3 2.7 collective-permute-done.4.refs_11_
  17.8 4.2 %collective-permute-done.1.refs_5_ = bf16[256,512]{1,0:T(8,128)(2,1)S(1)} collective-permute-done((bf16[256,512]{1,0:T(8,128)(2,1)S(1)}, bf16[256,512]{1,0:T(8,128)(2,1)S(1)}, u32[]{:S(2)}, u32[]{:S(2)}) %collective-permute-start.1) | collective-permute-done | bytes 262176 | tf_op jit(solution)/shard_map/ppermute | solution.py:55
  25.0 4.8 %collective-permute-done.2.refs_6_ = bf16[256,512]{1,0:T(8,128)(2,1)S(1)} collective-permute-done((bf16[256,512]{1,0:T(8,128)(2,1)S(1)}, bf16[256,512]{1,0:T(8,128)(2,1)S(1)}, u32[]{:S(2)}, u32[]{:S(2)}) %collective-permute-start.2) | collective-permute-done | bytes 262176 | tf_op jit(solution)/shard_map/ppermute | solution.py:55
  31.9 4.9 %collective-permute-done.3.refs_7_.refs_2_ = bf16[256,512]{1,0:T(8,128)(2,1)S(1)} collective-permute-done((bf16[256,512]{1,0:T(8,128)(2,1)S(1)}, bf16[256,512]{1,0:T(8,128)(2,1)S(1)}, u32[]{:S(2)}, u32[]{:S(2)}) %collective-permute-start.3) | collective-permute-done | bytes 262176 | tf_op jit(solution)/shard_map/ppermute | solution.py:55
  37.3 1.9 shard_map.65
  43.8 24.2 %collective-permute-done.9.refs_4_.refs_0_ = bf16[2048,256]{1,0:T(8,128)(2,1)S(1)} collective-permute-done((bf16[2048,256]{1,0:T(8,128)(2,1)}, bf16[2048,256]{1,0:T(8,128)(2,1)S(1)}, u32[]{:S(2)}, u32[]{:S(2)}) %collective-permute-start.9) | collective-permute-done | bytes 1048608 | tf_op jit(solution)/shard_map/ppermute | solution.py:38
  74.3 35.9 %collective-permute-done.13.refs_5_ = bf16[256,2048]{1,0:T(8,128)(2,1)} collective-permute-done((bf16[256,2048]{1,0:T(8,128)(2,1)S(1)}, bf16[256,2048]{1,0:T(8,128)(2,1)}, u32[]{:S(2)}, u32[]{:S(2)}) %collective-permute-start.13) | collective-permute-done | bytes 1048608 | tf_op jit(solution)/shard_map/ppermute | solution.py:55
  110.2 2.6 collective-permute-start.14
  114.0 23.3 %collective-permute-done.14.refs_7_ = bf16[256,2048]{1,0:T(8,128)(2,1)} collective-permute-done((bf16[256,2048]{1,0:T(8,128)(2,1)}, bf16[256,2048]{1,0:T(8,128)(2,1)}, u32[]{:S(2)}, u32[]{:S(2)}) %collective-permute-start.14) | collective-permute-done | bytes 1048608 | tf_op jit(solution)/shard_map/ppermute | solution.py:55
  139.4 22.4 %collective-permute-done.15.refs_4_ = bf16[256,2048]{1,0:T(8,128)(2,1)S(1)} collective-permute-done((bf16[256,2048]{1,0:T(8,128)(2,1)}, bf16[256,2048]{1,0:T(8,128)(2,1)S(1)}, u32[]{:S(2)}, u32[]{:S(2)}) %collective-permute-start.15) | collective-permute-done | bytes 1048608 | tf_op jit(solution)/shard_map/ppermute | solution.py:55
  164.1 3.7 %shard_map.70 = (f32[512,512]{1,0:T(8,128)S(1)}, f32[512,512]{1,0:T(8,128)S(1)}) custom-call(s32[10]{0:T(128)S(1)} %dynamic-slice_bitcast_fusion.1.refs_0_, bf16[256,2048]{1,0:T(8,128)(2,1)S(1)} %get-tuple-element.30.refs_2_.refs_1_, bf16[256,2048]{1,0:T(8,128)(2,1)S(1)} %collective-permute-done.refs_3_.refs_2_, bf16[256,2048]{1,0:T(8,128)(2,1)S(1)} %copy-done.3, ...), custom_call_target="tpu_custom_call" | custom-call | flops 1000000 | bytes 100000 | tf_op jit(solution)/shard_map/pallas_call | solution.py:65
  168.9 4.1 %shard_map.69 = (f32[512,512]{1,0:T(8,128)S(1)}, f32[512,512]{1,0:T(8,128)S(1)}) custom-call(s32[10]{0:T(128)S(1)} %dynamic-slice_bitcast_fusion.1.refs_0_, bf16[256,2048]{1,0:T(8,128)(2,1)S(1)} %get-tuple-element.30.refs_2_.refs_1_, bf16[256,2048]{1,0:T(8,128)(2,1)S(1)} %collective-permute-done.refs_3_.refs_2_, bf16[256,2048]{1,0:T(8,128)(2,1)S(1)} %copy-done.3, ...), custom_call_target="tpu_custom_call" | custom-call | flops 1000000 | bytes 100000 | tf_op jit(solution)/shard_map/pallas_call | solution.py:65
  191.5 2.8 shard_map.72
  195.3 2.8 shard_map.74
  201.6 2.0 dynamic-slice_bitcast_fusion.refs_1_
  204.3 17.5 %shard_map.73.refs_2_ = bf16[512,512]{1,0:T(8,128)(2,1)} custom-call(s32[512,128]{1,0:T(8,128)S(1)} %get-tuple-element.34.refs_9_.refs_0_, f32[512,512]{1,0:T(8,128)S(1)} %copy-done.33, f32[512,512]{1,0:T(8,128)} %collective-permute-done.18.refs_2_, bf16[2,128,2560]{2,1,0:T(8,128)(2,1)S(1)} %copy-done.20, bf16[2,2560,128]{2,1,0:T(8,128)(2,1)S(1)} %copy-done.22), custom_call_target="tpu_custom_call" | custom-call | flops 1000000 | bytes 100000 | tf_op jit(solution)/shard_map/pallas_call | solution.py:286
  225.0 16.9 %shard_map.75.refs_0_ = bf16[512,512]{1,0:T(8,128)(2,1)S(1)} custom-call(s32[512,128]{1,0:T(8,128)S(1)} %get-tuple-element.34.refs_9_.refs_0_, f32[512,512]{1,0:T(8,128)S(1)} %copy-done.37, f32[512,512]{1,0:T(8,128)} %collective-permute-done.21.refs_2_, bf16[2,128,2560]{2,1,0:T(8,128)(2,1)S(1)} %copy-done.24, bf16[2,2560,128]{2,1,0:T(8,128)(2,1)S(1)} %copy-done.26, ...), custom_call_target="tpu_custom_call" | custom-call | flops 1000000 | bytes 100000 | tf_op jit(solution)/shard_map/pallas_call | solution.py:286
  245.4 11.9 %collective-permute-done.26.refs_3_ = bf16[512,512]{1,0:T(8,128)(2,1)S(1)} collective-permute-done((bf16[512,512]{1,0:T(8,128)(2,1)}, bf16[512,512]{1,0:T(8,128)(2,1)S(1)}, u32[]{:S(2)}, u32[]{:S(2)}) %collective-permute-start.26) | collective-permute-done | bytes 524320 | tf_op jit(solution)/shard_map/ppermute | solution.py:38
  259.2 5.4 %shard_map.78 = (bf16[256,2048]{1,0:T(8,128)(2,1)S(1)}, bf16[256,2048]{1,0:T(8,128)(2,1)S(1)}) custom-call(s32[10]{0:T(128)S(1)} %dynamic-slice_bitcast_fusion.1.refs_0_, bf16[512,512]{1,0:T(8,128)(2,1)} %collective-permute-done.19.refs_1_, bf16[512,512]{1,0:T(8,128)(2,1)S(1)} %collective-permute-done.20.refs_2_, ...), custom_call_target="tpu_custom_call" | custom-call | flops 1000000 | bytes 100000 | tf_op jit(solution)/shard_map/pallas_call | solution.py:65
  264.6 4.2 %collective-permute-done.30.refs_8_ = bf16[2048,256]{1,0:T(8,128)(2,1)S(1)} collective-permute-done((bf16[2048,256]{1,0:T(8,128)(2,1)}, bf16[2048,256]{1,0:T(8,128)(2,1)S(1)}, u32[]{:S(2)}, u32[]{:S(2)}) %collective-permute-start.30) | collective-permute-done | bytes 1048608 | tf_op jit(solution)/shard_map/ppermute | solution.py:55
  268.8 2.5 shard_map.79
  273.7 12.2 %collective-permute-done.32.refs_7_ = bf16[1024,256]{1,0:T(8,128)(2,1)S(1)} collective-permute-done((bf16[1024,256]{1,0:T(8,128)(2,1)S(1)}, bf16[1024,256]{1,0:T(8,128)(2,1)S(1)}, u32[]{:S(2)}, u32[]{:S(2)}) %collective-permute-start.32) | collective-permute-done | bytes 524320 | tf_op jit(solution)/shard_map/ppermute | solution.py:55
  290.6 2.2 shard_map.81
  (156 shorter events, 67.5 us)
Async XLA Ops:
  6.5 171.5 %all-gather.6.cloned.1.call-start = ((), (), s32[]{:S(2)}) async-start(), calls=%async_computation.1 | async-start | bytes 2433024 | tf_op jit(solution)/shard_map/all_gather | solution.py:33
  13.2 23.6 %collective-permute-start = (bf16[256,2048]{1,0:T(8,128)(2,1)S(1)}, bf16[256,2048]{1,0:T(8,128)(2,1)S(1)}, u32[]{:S(2)}, u32[]{:S(2)}) collective-permute-start(bf16[256,2048]{1,0:T(8,128)(2,1)S(1)} %get-tuple-element.31), channel_id=1, source_target_pairs={{0,1},{1,0},{2,3},{3,2},{4,5},{5,4},{6,7},{7,6},{8,9},{9,8},{10,11... | collective-permute-start | bytes 3145736 | tf_op jit(solution)/shard_map/ppermute | solution.py:27
  42.5 159.1 %all-gather.4.cloned.1.call-start = ((), (), s32[]{:S(2)}) async-start(), calls=%async_computation | async-start | bytes 6291456 | tf_op jit(solution)/shard_map/all_gather | solution.py:44
  42.6 25.5 %collective-permute-start.9 = (bf16[2048,256]{1,0:T(8,128)(2,1)}, bf16[2048,256]{1,0:T(8,128)(2,1)S(1)}, u32[]{:S(2)}, u32[]{:S(2)}) collective-permute-start(bf16[2048,256]{1,0:T(8,128)(2,1)} %bitcast.16), channel_id=1, source_target_pairs={{0,16},{16,0},{1,17},{17,1},{2,18},{18,2},{3,19},{19,3},{4,20},{20... | collective-permute-start | bytes 3145736 | tf_op jit(solution)/shard_map/ppermute | solution.py:38
  71.3 38.9 %collective-permute-start.13 = (bf16[256,2048]{1,0:T(8,128)(2,1)S(1)}, bf16[256,2048]{1,0:T(8,128)(2,1)}, u32[]{:S(2)}, u32[]{:S(2)}) collective-permute-start(bf16[256,2048]{1,0:T(8,128)(2,1)S(1)} %shard_map.68.refs_3_), channel_id=1, source_target_pairs={{0,4},{1,5},{4,8},{5,9},{8,12},{9,13},{12,14},{13,15},{14,10},{15,... | collective-permute-start | bytes 3145736 | tf_op jit(solution)/shard_map/ppermute | solution.py:55
  72.6 40.2 %collective-permute-start.10 = (bf16[256,2048]{1,0:T(8,128)(2,1)S(1)}, bf16[256,2048]{1,0:T(8,128)(2,1)}, u32[]{:S(2)}, u32[]{:S(2)}) collective-permute-start(bf16[256,2048]{1,0:T(8,128)(2,1)S(1)} %shard_map.68.refs_3_), channel_id=1, source_target_pairs={{0,2},{1,3},{4,0},{5,1},{8,4},{9,5},{12,8},{13,9},{14,12},{15,13},... | collective-permute-start | bytes 3145736 | tf_op jit(solution)/shard_map/ppermute | solution.py:55
  110.2 27.2 %collective-permute-start.14 = (bf16[256,2048]{1,0:T(8,128)(2,1)}, bf16[256,2048]{1,0:T(8,128)(2,1)}, u32[]{:S(2)}, u32[]{:S(2)}) collective-permute-start(bf16[256,2048]{1,0:T(8,128)(2,1)} %collective-permute-done.13.refs_5_), channel_id=1, source_target_pairs={{0,4},{1,5},{4,8},{5,9},{8,12},{9,13},{12,14},{13,15},{14,10},{15,... | collective-permute-start | bytes 3145736 | tf_op jit(solution)/shard_map/ppermute | solution.py:55
  112.8 24.9 %collective-permute-start.11 = (bf16[256,2048]{1,0:T(8,128)(2,1)}, bf16[256,2048]{1,0:T(8,128)(2,1)}, u32[]{:S(2)}, u32[]{:S(2)}) collective-permute-start(bf16[256,2048]{1,0:T(8,128)(2,1)} %collective-permute-done.10.refs_4_), channel_id=1, source_target_pairs={{0,2},{1,3},{4,0},{5,1},{8,4},{9,5},{12,8},{13,9},{14,12},{15,13},... | collective-permute-start | bytes 3145736 | tf_op jit(solution)/shard_map/ppermute | solution.py:55
  137.4 24.5 %collective-permute-start.15 = (bf16[256,2048]{1,0:T(8,128)(2,1)}, bf16[256,2048]{1,0:T(8,128)(2,1)S(1)}, u32[]{:S(2)}, u32[]{:S(2)}) collective-permute-start(bf16[256,2048]{1,0:T(8,128)(2,1)} %collective-permute-done.14.refs_7_), channel_id=1, source_target_pairs={{0,4},{1,5},{4,8},{5,9},{8,12},{9,13},{12,14},{13,15},{14,10},{15,... | collective-permute-start | bytes 3145736 | tf_op jit(solution)/shard_map/ppermute | solution.py:55
  137.7 24.5 %collective-permute-start.12 = (bf16[256,2048]{1,0:T(8,128)(2,1)}, bf16[256,2048]{1,0:T(8,128)(2,1)S(1)}, u32[]{:S(2)}, u32[]{:S(2)}) collective-permute-start(bf16[256,2048]{1,0:T(8,128)(2,1)} %collective-permute-done.11.refs_6_), channel_id=1, source_target_pairs={{0,2},{1,3},{4,0},{5,1},{8,4},{9,5},{12,8},{13,9},{14,12},{15,13},... | collective-permute-start | bytes 3145736 | tf_op jit(solution)/shard_map/ppermute | solution.py:55
  161.9 13.1 %collective-permute-start.16 = (bf16[128,2048]{1,0:T(8,128)(2,1)S(1)}, bf16[128,2048]{1,0:T(8,128)(2,1)S(1)}, u32[]{:S(2)}, u32[]{:S(2)}) collective-permute-start(bf16[128,2048]{1,0:T(8,128)(2,1)S(1)} %slice.16), channel_id=1, source_target_pairs={{0,4},{1,5},{4,8},{5,9},{8,12},{9,13},{12,14},{13,15},{14,10},{15,... | collective-permute-start | bytes 1572872 | tf_op jit(solution)/shard_map/ppermute | solution.py:55
  176.0 23.6 %collective-permute-start.22 = (bf16[2048,256]{1,0:T(8,128)(2,1)}, bf16[2048,256]{1,0:T(8,128)(2,1)}, u32[]{:S(2)}, u32[]{:S(2)}) collective-permute-start(bf16[2048,256]{1,0:T(8,128)(2,1)} %shard_map.71.refs_10_.refs_7_), channel_id=1, source_target_pairs={{0,2},{1,3},{4,0},{5,1},{8,4},{9,5},{12,8},{13,9},{14,12},{15,13},... | collective-permute-start | bytes 3145736 | tf_op jit(solution)/shard_map/ppermute | solution.py:55
  177.4 23.6 %collective-permute-start.23 = (bf16[2048,256]{1,0:T(8,128)(2,1)}, bf16[2048,256]{1,0:T(8,128)(2,1)}, u32[]{:S(2)}, u32[]{:S(2)}) collective-permute-start(bf16[2048,256]{1,0:T(8,128)(2,1)} %shard_map.71.refs_10_.refs_7_), channel_id=1, source_target_pairs={{0,4},{1,5},{4,8},{5,9},{8,12},{9,13},{12,14},{13,15},{14,10},{15,... | collective-permute-start | bytes 3145736 | tf_op jit(solution)/shard_map/ppermute | solution.py:55
  199.1 25.9 %collective-permute-start.21 = (f32[512,512]{1,0:T(8,128)}, f32[512,512]{1,0:T(8,128)}, u32[]{:S(2)}, u32[]{:S(2)}) collective-permute-start(f32[512,512]{1,0:T(8,128)} %get-tuple-element.44), channel_id=1, source_target_pairs={{0,1},{1,0},{2,3},{3,2},{4,5},{5,4},{6,7},{7,6},{8,9},{9,8},{10,11... | collective-permute-start | bytes 3145736 | tf_op jit(solution)/shard_map/ppermute | solution.py:27
  199.6 43.2 %collective-permute-start.24 = (bf16[2048,256]{1,0:T(8,128)(2,1)}, bf16[2048,256]{1,0:T(8,128)(2,1)}, u32[]{:S(2)}, u32[]{:S(2)}) collective-permute-start(bf16[2048,256]{1,0:T(8,128)(2,1)} %collective-permute-done.22.refs_5_.refs_8_), channel_id=1, source_target_pairs={{0,2},{1,3},{4,0},{5,1},{8,4},{9,5},{12,8},{13,9},{14,12},{15,13},... | collective-permute-start | bytes 3145736 | tf_op jit(solution)/shard_map/ppermute | solution.py:55
  201.0 41.8 %collective-permute-start.25 = (bf16[2048,256]{1,0:T(8,128)(2,1)}, bf16[2048,256]{1,0:T(8,128)(2,1)}, u32[]{:S(2)}, u32[]{:S(2)}) collective-permute-start(bf16[2048,256]{1,0:T(8,128)(2,1)} %collective-permute-done.23.refs_6_.refs_9_), channel_id=1, source_target_pairs={{0,4},{1,5},{4,8},{5,9},{8,12},{9,13},{12,14},{13,15},{14,10},{15,... | collective-permute-start | bytes 3145736 | tf_op jit(solution)/shard_map/ppermute | solution.py:55
  221.8 23.6 %collective-permute-start.19 = (bf16[512,512]{1,0:T(8,128)(2,1)}, bf16[512,512]{1,0:T(8,128)(2,1)}, u32[]{:S(2)}, u32[]{:S(2)}) collective-permute-start(bf16[512,512]{1,0:T(8,128)(2,1)} %shard_map.73.refs_2_), channel_id=1, source_target_pairs={{0,16},{16,0},{1,17},{17,1},{2,18},{18,2},{3,19},{19,3},{4,20},{20... | collective-permute-start | bytes 1572872 | tf_op jit(solution)/shard_map/ppermute | solution.py:38
  225.0 32.3 %collective-permute-start.28 = (bf16[256,2048]{1,0:T(8,128)(2,1)}, bf16[256,2048]{1,0:T(8,128)(2,1)S(1)}, u32[]{:S(2)}, u32[]{:S(2)}) collective-permute-start(bf16[256,2048]{1,0:T(8,128)(2,1)} %get-tuple-element.48), channel_id=1, source_target_pairs={{0,1},{1,0},{2,3},{3,2},{4,5},{5,4},{6,7},{7,6},{8,9},{9,8},{10,11... | collective-permute-start | bytes 3145736 | tf_op jit(solution)/shard_map/ppermute | solution.py:27
  242.8 14.5 %collective-permute-start.26 = (bf16[512,512]{1,0:T(8,128)(2,1)}, bf16[512,512]{1,0:T(8,128)(2,1)S(1)}, u32[]{:S(2)}, u32[]{:S(2)}) collective-permute-start(bf16[512,512]{1,0:T(8,128)(2,1)} %shard_map.76), channel_id=1, source_target_pairs={{0,16},{16,0},{1,17},{17,1},{2,18},{18,2},{3,19},{19,3},{4,20},{20... | collective-permute-start | bytes 1572872 | tf_op jit(solution)/shard_map/ppermute | solution.py:38
  243.3 25.5 %collective-permute-start.30 = (bf16[2048,256]{1,0:T(8,128)(2,1)}, bf16[2048,256]{1,0:T(8,128)(2,1)S(1)}, u32[]{:S(2)}, u32[]{:S(2)}) collective-permute-start(bf16[2048,256]{1,0:T(8,128)(2,1)} %collective-permute-done.25.refs_2_.refs_11_), channel_id=1, source_target_pairs={{0,4},{1,5},{4,8},{5,9},{8,12},{9,13},{12,14},{13,15},{14,10},{15,... | collective-permute-start | bytes 3145736 | tf_op jit(solution)/shard_map/ppermute | solution.py:55
  243.6 25.2 %collective-permute-start.29 = (bf16[2048,256]{1,0:T(8,128)(2,1)}, bf16[2048,256]{1,0:T(8,128)(2,1)S(1)}, u32[]{:S(2)}, u32[]{:S(2)}) collective-permute-start(bf16[2048,256]{1,0:T(8,128)(2,1)} %collective-permute-done.24.refs_1_.refs_10_), channel_id=1, source_target_pairs={{0,2},{1,3},{4,0},{5,1},{8,4},{9,5},{12,8},{13,9},{14,12},{15,13},... | collective-permute-start | bytes 3145736 | tf_op jit(solution)/shard_map/ppermute | solution.py:55
  271.4 19.2 %collective-permute-start.31 = (bf16[256,2048]{1,0:T(8,128)(2,1)S(1)}, bf16[256,2048]{1,0:T(8,128)(2,1)S(1)}, u32[]{:S(2)}, u32[]{:S(2)}) collective-permute-start(bf16[256,2048]{1,0:T(8,128)(2,1)S(1)} %get-tuple-element.52), channel_id=1, source_target_pairs={{0,1},{1,0},{2,3},{3,2},{4,5},{5,4},{6,7},{7,6},{8,9},{9,8},{10,11... | collective-permute-start | bytes 3145736 | tf_op jit(solution)/shard_map/ppermute | solution.py:27
  271.5 14.4 %collective-permute-start.32 = (bf16[1024,256]{1,0:T(8,128)(2,1)S(1)}, bf16[1024,256]{1,0:T(8,128)(2,1)S(1)}, u32[]{:S(2)}, u32[]{:S(2)}) collective-permute-start(bf16[1024,256]{1,0:T(8,128)(2,1)S(1)} %slice.18), channel_id=1, source_target_pairs={{0,4},{1,5},{4,8},{5,9},{8,12},{9,13},{12,14},{13,15},{14,10},{15,... | collective-permute-start | bytes 1572872 | tf_op jit(solution)/shard_map/ppermute | solution.py:55
  273.3 14.1 %collective-permute-start.33 = (bf16[1024,256]{1,0:T(8,128)(2,1)S(1)}, bf16[1024,256]{1,0:T(8,128)(2,1)S(1)}, u32[]{:S(2)}, u32[]{:S(2)}) collective-permute-start(bf16[1024,256]{1,0:T(8,128)(2,1)S(1)} %slice.19), channel_id=1, source_target_pairs={{0,2},{1,3},{4,0},{5,1},{8,4},{9,5},{12,8},{13,9},{14,12},{15,13},... | collective-permute-start | bytes 1572872 | tf_op jit(solution)/shard_map/ppermute | solution.py:55
  (53 other events, 322.4 us)
Sparse Core Ops, SparseCore 0:
  42.6 64.9 all-gather.5
  114.1 57.2 all-gather.3

commit v7 on v6

--- a/solution.py
+++ b/solution.py
@@ -70,7 +70,7 @@
         out_shape=[jax.ShapeDtypeStruct(shape, dtype) for shape, dtype in outs],
         scratch_shapes=list(scratch),
         input_output_aliases=aliases or {},
-        compiler_params=pltpu.CompilerParams(vmem_limit_bytes=40 * 1024 * 1024),
+        compiler_params=pltpu.CompilerParams(vmem_limit_bytes=8 * 1024 * 1024),
         cost_estimate=pl.CostEstimate(flops=1000000, bytes_accessed=100000, transcendentals=0),
     )(scalars, *arrays, *waits)
 
@@ -298,7 +298,7 @@
         scratch_shapes=[
             pltpu.VMEM((TILE, GROUP_WIDTH), jnp.bfloat16), pltpu.VMEM((2, TILE, span), jnp.float32)
         ],
-        compiler_params=pltpu.CompilerParams(vmem_limit_bytes=40 * 1024 * 1024),
+        compiler_params=pltpu.CompilerParams(vmem_limit_bytes=20 * 1024 * 1024),
         cost_estimate=pl.CostEstimate(flops=1000000, bytes_accessed=100000, transcendentals=0),
     )(lo, kept, received, keys_t, values, *waits)
 
@@ -362,11 +362,11 @@
     scalars = lax.dynamic_index_in_dim(jnp.array(table, jnp.int32), device, 0, keepdims=False)
 
     keyval_pieces = around(keyval_weight[0], halved=False)
-    out_shard = to_next_section(out_weight[0])
+    out_shard = from_section_before(out_weight[0])
     kv_steps = [keyval_pieces[d][0][1] for d in (3, chips - 3)]
     query_shard, = run(
         copy_kernel, [(query_weight.shape[1:], jnp.bfloat16)], scalars, [query_weight[0]],
-        waits=kv_steps + [out_shard],
+        waits=kv_steps,
     )
     query_pieces = around(query_shard)
 
@@ -414,7 +414,7 @@
         attended.append(attention(lowest, sums[g][0], swap_cores(sums[g][1]), heads[g], heads[2 + g], waits))
     attended[1] = after(attended[1], *[out_pieces[d][0][1] for d in (2, chips - 2)])
     kept, sent = run(
-        functools.partial(split_kernel, False), [half, half], scalars, [from_section_before(hidden)], waits=attended[:1]
+        functools.partial(split_kernel, False), [half, half], scalars, [to_next_section(hidden)], waits=attended[:1]
     )
     adds = [kept, swap_cores(sent)]
     arrived = []

time: 300 us -> 282 us (0.940)
  local copies, waits for them, and re-layouts: 27.1 us -> 19.5 us
  waiting for transfers between devices: 159 us -> 153 us
  Pallas kernels: 68.4 us -> 65.3 us
    ppermute x3, waiting for transfers between devices: 36.1 us -> 11.2 us  [to_next_section(): lax.ppermute(value, 'section', [(i, (i + 1) % count) for i in range(count)])]
    ppermute x23, waiting for transfers between devices: 118 us -> 136 us  [along_ring(): return lax.ppermute(value, 'fsdp', pairs)]
    unnamed x80 -> x50, local copies, waits for them, and re-layouts: 24.3 us -> 14.5 us
  transfers between devices with their start and end apart: 37 -> 37, of which waited for: 17 -> 16; matrix products, arithmetic and copies ran while one was open for 1% -> 2% of each run, Pallas kernels for 20% -> 21%
where the time goes in v7:
time: 282 us
  waiting for transfers between devices  153 us (54%)
  Pallas kernels  65.3 us (23%)
  starting transfers between devices  30.7 us (11%)
  local copies, waits for them, and re-layouts  19.5 us (7%)
  between operations  13.7 us (5%)
    ppermute x23, waiting for transfers between devices, along_ring(): return lax.ppermute(value, 'fsdp', pairs)  136 us
    pallas_call x14, Pallas kernels, run(): pl.pallas_call(only, in_specs=[pl.BlockSpec(memory_space=pltpu.SMEM)] + [...  33.3 us
    pallas_call x2, Pallas kernels, attention(): pl.pallas_call(only, grid=(rows // TILE,), in_specs=[pl.BlockSpec((TILE,...  32 us
    ppermute x23, starting transfers between devices, along_ring(): return lax.ppermute(value, 'fsdp', pairs)  26.2 us
    unnamed x50, local copies, waits for them, and re-layouts  14.5 us
    ppermute x3, waiting for transfers between devices, to_next_section(): lax.ppermute(value, 'section', [(i, (i + 1) % count) for i in range(count)])  11.2 us
  transfers between devices with their start and end apart: 37, of which 16 were waited for; matrix products, arithmetic and copies ran while one was open for 2% of the time, Pallas kernels for 21%

profile of v7, /device:TPU:0, one launch (start us, length us, event | category | flops | bytes accessed | tf_op | source)
XLA Modules:
  0.0 281.8 jit_solution(1604703414014857091)
XLA Ops:
  7.3 3.1 %collective-permute-start.4 = (bf16[256,512]{1,0:T(8,128)(2,1)}, bf16[256,512]{1,0:T(8,128)(2,1)S(1)}, u32[]{:S(2)}, u32[]{:S(2)}) collective-permute-start(bf16[256,512]{1,0:T(8,128)(2,1)} %bitcast.13), channel_id=1, source_target_pairs={{0,4},{1,5},{4,8},{5,9},{8,12},{9,13},{12,14},{13,15},{14,10},{15,... | collective-permute-start | bytes 786440 | tf_op jit(solution)/shard_map/ppermute | solution.py:55
  14.1 2.7 collective-permute-done.4.refs_11_
  19.6 4.8 %collective-permute-done.5.refs_10_ = bf16[256,512]{1,0:T(8,128)(2,1)S(1)} collective-permute-done((bf16[256,512]{1,0:T(8,128)(2,1)S(1)}, bf16[256,512]{1,0:T(8,128)(2,1)S(1)}, u32[]{:S(2)}, u32[]{:S(2)}) %collective-permute-start.5) | collective-permute-done | bytes 262176 | tf_op jit(solution)/shard_map/ppermute | solution.py:55
  26.4 4.6 %collective-permute-done.6.refs_9_.refs_3_ = bf16[256,512]{1,0:T(8,128)(2,1)S(1)} collective-permute-done((bf16[256,512]{1,0:T(8,128)(2,1)S(1)}, bf16[256,512]{1,0:T(8,128)(2,1)S(1)}, u32[]{:S(2)}, u32[]{:S(2)}) %collective-permute-start.6) | collective-permute-done | bytes 262176 | tf_op jit(solution)/shard_map/ppermute | solution.py:55
  36.5 24.1 %collective-permute-done.7.refs_8_ = bf16[256,512]{1,0:T(8,128)(2,1)S(1)} collective-permute-done((bf16[256,512]{1,0:T(8,128)(2,1)S(1)}, bf16[256,512]{1,0:T(8,128)(2,1)S(1)}, u32[]{:S(2)}, u32[]{:S(2)}) %collective-permute-start.7) | collective-permute-done | bytes 262176 | tf_op jit(solution)/shard_map/ppermute | solution.py:55
  67.9 31.3 %collective-permute-done.13.refs_7_ = bf16[256,2048]{1,0:T(8,128)(2,1)S(1)} collective-permute-done((bf16[256,2048]{1,0:T(8,128)(2,1)}, bf16[256,2048]{1,0:T(8,128)(2,1)S(1)}, u32[]{:S(2)}, u32[]{:S(2)}) %collective-permute-start.13) | collective-permute-done | bytes 1048608 | tf_op jit(solution)/shard_map/ppermute | solution.py:55
  99.2 2.4 collective-permute-start.14
  102.6 37.5 %collective-permute-done.14.refs_4_ = bf16[256,2048]{1,0:T(8,128)(2,1)S(1)} collective-permute-done((bf16[256,2048]{1,0:T(8,128)(2,1)S(1)}, bf16[256,2048]{1,0:T(8,128)(2,1)S(1)}, u32[]{:S(2)}, u32[]{:S(2)}) %collective-permute-start.14) | collective-permute-done | bytes 1048608 | tf_op jit(solution)/shard_map/ppermute | solution.py:55
  142.0 2.5 collective-permute-start.15
  148.0 2.5 dynamic-slice_bitcast_fusion.refs_0_
  150.5 3.1 %shard_map.70 = (f32[512,512]{1,0:T(8,128)S(1)}, f32[512,512]{1,0:T(8,128)S(1)}) custom-call(s32[10]{0:T(128)S(1)} %dynamic-slice_bitcast_fusion.1.refs_0_, bf16[256,2048]{1,0:T(8,128)(2,1)S(1)} %get-tuple-element.30.refs_2_.refs_1_, bf16[256,2048]{1,0:T(8,128)(2,1)S(1)} %collective-permute-done.refs_3_.refs_2_, bf16[256,2048]{1,0:T(8,128)(2,1)S(1)} %shard_map.68.refs_3_, ...), custom_call_target="tpu_custom_call" | custom-call | flops 1000000 | bytes 100000 | tf_op jit(solution)/shard_map/pallas_call | solution.py:65
  154.6 3.5 %shard_map.69 = (f32[512,512]{1,0:T(8,128)S(1)}, f32[512,512]{1,0:T(8,128)S(1)}) custom-call(s32[10]{0:T(128)S(1)} %dynamic-slice_bitcast_fusion.1.refs_0_, bf16[256,2048]{1,0:T(8,128)(2,1)S(1)} %get-tuple-element.30.refs_2_.refs_1_, bf16[256,2048]{1,0:T(8,128)(2,1)S(1)} %collective-permute-done.refs_3_.refs_2_, bf16[256,2048]{1,0:T(8,128)(2,1)S(1)} %shard_map.68.refs_3_, ...), custom_call_target="tpu_custom_call" | custom-call | flops 1000000 | bytes 100000 | tf_op jit(solution)/shard_map/pallas_call | solution.py:65
  169.4 2.6 shard_map.72
  172.1 2.5 shard_map.74
  175.2 9.2 %collective-permute-done.21.refs_5_.refs_8_ = bf16[2048,256]{1,0:T(8,128)(2,1)} collective-permute-done((bf16[2048,256]{1,0:T(8,128)(2,1)}, bf16[2048,256]{1,0:T(8,128)(2,1)}, u32[]{:S(2)}, u32[]{:S(2)}) %collective-permute-start.21) | collective-permute-done | bytes 1048608 | tf_op jit(solution)/shard_map/ppermute | solution.py:55
  186.5 16.4 %shard_map.73.refs_2_ = bf16[512,512]{1,0:T(8,128)(2,1)} custom-call(s32[512,128]{1,0:T(8,128)S(1)} %get-tuple-element.34.refs_9_.refs_0_, f32[512,512]{1,0:T(8,128)S(1)} %get-tuple-element.38.refs_1_, f32[512,512]{1,0:T(8,128)S(1)} %collective-permute-done.17.refs_2_, bf16[2,128,2560]{2,1,0:T(8,128)(2,1)S(1)} %get-tuple-element.40.refs_3_, ...), custom_call_target="tpu_custom_call" | custom-call | flops 1000000 | bytes 100000 | tf_op jit(solution)/shard_map/pallas_call | solution.py:286
  203.5 2.8 %shard_map.77 = (bf16[256,2048]{1,0:T(8,128)(2,1)S(1)}, bf16[256,2048]{1,0:T(8,128)(2,1)}) custom-call(s32[10]{0:T(128)S(1)} %dynamic-slice_bitcast_fusion.1.refs_0_, bf16[256,4096]{1,0:T(8,128)(2,1)} %collective-permute-done.27.refs_1_, bf16[512,512]{1,0:T(8,128)(2,1)} %shard_map.73.refs_2_), custom_call_target="tpu_custom_call" | custom-call | flops 1000000 | bytes 100000 | tf_op jit(solution)/shard_map/pallas_call | solution.py:65
  206.4 15.6 %shard_map.75.refs_0_ = bf16[512,512]{1,0:T(8,128)(2,1)S(1)} custom-call(s32[512,128]{1,0:T(8,128)S(1)} %get-tuple-element.34.refs_9_.refs_0_, f32[512,512]{1,0:T(8,128)S(1)} %get-tuple-element.43.refs_1_, f32[512,512]{1,0:T(8,128)S(1)} %collective-permute-done.20.refs_2_, bf16[2,128,2560]{2,1,0:T(8,128)(2,1)S(1)} %get-tuple-element.45.refs_3_, ...), custom_call_target="tpu_custom_call" | custom-call | flops 1000000 | bytes 100000 | tf_op jit(solution)/shard_map/pallas_call | solution.py:286
  226.2 11.2 %collective-permute-done.25.refs_3_ = bf16[512,512]{1,0:T(8,128)(2,1)S(1)} collective-permute-done((bf16[512,512]{1,0:T(8,128)(2,1)}, bf16[512,512]{1,0:T(8,128)(2,1)S(1)}, u32[]{:S(2)}, u32[]{:S(2)}) %collective-permute-start.25) | collective-permute-done | bytes 524320 | tf_op jit(solution)/shard_map/ppermute | solution.py:38
  239.3 5.3 %shard_map.78 = (bf16[256,2048]{1,0:T(8,128)(2,1)S(1)}, bf16[256,2048]{1,0:T(8,128)(2,1)S(1)}) custom-call(s32[10]{0:T(128)S(1)} %dynamic-slice_bitcast_fusion.1.refs_0_, bf16[512,512]{1,0:T(8,128)(2,1)} %collective-permute-done.18.refs_1_, bf16[512,512]{1,0:T(8,128)(2,1)S(1)} %collective-permute-done.19.refs_2_, ...), custom_call_target="tpu_custom_call" | custom-call | flops 1000000 | bytes 100000 | tf_op jit(solution)/shard_map/pallas_call | solution.py:65
  244.7 5.0 %collective-permute-done.30.refs_8_ = bf16[2048,256]{1,0:T(8,128)(2,1)S(1)} collective-permute-done((bf16[2048,256]{1,0:T(8,128)(2,1)}, bf16[2048,256]{1,0:T(8,128)(2,1)S(1)}, u32[]{:S(2)}, u32[]{:S(2)}) %collective-permute-start.30) | collective-permute-done | bytes 1048608 | tf_op jit(solution)/shard_map/ppermute | solution.py:55
  251.1 2.5 shard_map.79
  255.9 12.2 %collective-permute-done.32.refs_7_ = bf16[1024,256]{1,0:T(8,128)(2,1)S(1)} collective-permute-done((bf16[1024,256]{1,0:T(8,128)(2,1)S(1)}, bf16[1024,256]{1,0:T(8,128)(2,1)S(1)}, u32[]{:S(2)}, u32[]{:S(2)}) %collective-permute-start.32) | collective-permute-done | bytes 524320 | tf_op jit(solution)/shard_map/ppermute | solution.py:55
  272.8 2.2 shard_map.81
  (126 shorter events, 58.5 us)
Async XLA Ops:
  6.5 141.5 %all-gather.4.cloned.1.call-start = ((), (), s32[]{:S(2)}) async-start(), calls=%async_computation | async-start | bytes 3145728 | tf_op jit(solution)/shard_map/all_gather | solution.py:44
  7.3 155.0 %all-gather.6.cloned.1.call-start = ((), (), s32[]{:S(2)}) async-start(), calls=%async_computation.1 | async-start | bytes 2433024 | tf_op jit(solution)/shard_map/all_gather | solution.py:33
  14.0 22.5 %collective-permute-start = (bf16[256,2048]{1,0:T(8,128)(2,1)S(1)}, bf16[256,2048]{1,0:T(8,128)(2,1)S(1)}, u32[]{:S(2)}, u32[]{:S(2)}) collective-permute-start(bf16[256,2048]{1,0:T(8,128)(2,1)S(1)} %get-tuple-element.31), channel_id=1, source_target_pairs={{0,1},{1,0},{2,3},{3,2},{4,5},{5,4},{6,7},{7,6},{8,9},{9,8},{10,11... | collective-permute-start | bytes 3145736 | tf_op jit(solution)/shard_map/ppermute | solution.py:27
  32.8 33.0 %collective-permute-start.12 = (bf16[256,2048]{1,0:T(8,128)(2,1)S(1)}, bf16[256,2048]{1,0:T(8,128)(2,1)}, u32[]{:S(2)}, u32[]{:S(2)}) collective-permute-start(bf16[256,2048]{1,0:T(8,128)(2,1)S(1)} %shard_map.68.refs_3_), channel_id=1, source_target_pairs={{0,4},{1,5},{4,8},{5,9},{8,12},{9,13},{12,14},{13,15},{14,10},{15,... | collective-permute-start | bytes 3145736 | tf_op jit(solution)/shard_map/ppermute | solution.py:55
  34.4 33.1 %collective-permute-start.9 = (bf16[256,2048]{1,0:T(8,128)(2,1)S(1)}, bf16[256,2048]{1,0:T(8,128)(2,1)}, u32[]{:S(2)}, u32[]{:S(2)}) collective-permute-start(bf16[256,2048]{1,0:T(8,128)(2,1)S(1)} %shard_map.68.refs_3_), channel_id=1, source_target_pairs={{0,2},{1,3},{4,0},{5,1},{8,4},{9,5},{12,8},{13,9},{14,12},{15,13},... | collective-permute-start | bytes 3145736 | tf_op jit(solution)/shard_map/ppermute | solution.py:55
  34.9 25.7 %collective-permute-start.7 = (bf16[256,512]{1,0:T(8,128)(2,1)S(1)}, bf16[256,512]{1,0:T(8,128)(2,1)S(1)}, u32[]{:S(2)}, u32[]{:S(2)}) collective-permute-start(bf16[256,512]{1,0:T(8,128)(2,1)S(1)} %collective-permute-done.6.refs_9_.refs_3_), channel_id=1, source_target_pairs={{0,4},{1,5},{4,8},{5,9},{8,12},{9,13},{12,14},{13,15},{14,10},{15,... | collective-permute-start | bytes 786440 | tf_op jit(solution)/shard_map/ppermute | solution.py:55
  65.9 33.3 %collective-permute-start.13 = (bf16[256,2048]{1,0:T(8,128)(2,1)}, bf16[256,2048]{1,0:T(8,128)(2,1)S(1)}, u32[]{:S(2)}, u32[]{:S(2)}) collective-permute-start(bf16[256,2048]{1,0:T(8,128)(2,1)} %collective-permute-done.12.refs_5_), channel_id=1, source_target_pairs={{0,4},{1,5},{4,8},{5,9},{8,12},{9,13},{12,14},{13,15},{14,10},{15,... | collective-permute-start | bytes 3145736 | tf_op jit(solution)/shard_map/ppermute | solution.py:55
  67.5 35.1 %collective-permute-start.10 = (bf16[256,2048]{1,0:T(8,128)(2,1)}, bf16[256,2048]{1,0:T(8,128)(2,1)S(1)}, u32[]{:S(2)}, u32[]{:S(2)}) collective-permute-start(bf16[256,2048]{1,0:T(8,128)(2,1)} %collective-permute-done.9.refs_4_), channel_id=1, source_target_pairs={{0,2},{1,3},{4,0},{5,1},{8,4},{9,5},{12,8},{13,9},{14,12},{15,13},... | collective-permute-start | bytes 3145736 | tf_op jit(solution)/shard_map/ppermute | solution.py:55
  99.2 40.9 %collective-permute-start.14 = (bf16[256,2048]{1,0:T(8,128)(2,1)S(1)}, bf16[256,2048]{1,0:T(8,128)(2,1)S(1)}, u32[]{:S(2)}, u32[]{:S(2)}) collective-permute-start(bf16[256,2048]{1,0:T(8,128)(2,1)S(1)} %collective-permute-done.13.refs_7_), channel_id=1, source_target_pairs={{0,4},{1,5},{4,8},{5,9},{8,12},{9,13},{12,14},{13,15},{14,10},{15,... | collective-permute-start | bytes 3145736 | tf_op jit(solution)/shard_map/ppermute | solution.py:55
  102.6 41.9 %collective-permute-start.11 = (bf16[256,2048]{1,0:T(8,128)(2,1)S(1)}, bf16[256,2048]{1,0:T(8,128)(2,1)S(1)}, u32[]{:S(2)}, u32[]{:S(2)}) collective-permute-start(bf16[256,2048]{1,0:T(8,128)(2,1)S(1)} %collective-permute-done.10.refs_6_), channel_id=1, source_target_pairs={{0,2},{1,3},{4,0},{5,1},{8,4},{9,5},{12,8},{13,9},{14,12},{15,13},... | collective-permute-start | bytes 3145736 | tf_op jit(solution)/shard_map/ppermute | solution.py:55
  142.0 18.1 %collective-permute-start.15 = (bf16[128,2048]{1,0:T(8,128)(2,1)}, bf16[128,2048]{1,0:T(8,128)(2,1)}, u32[]{:S(2)}, u32[]{:S(2)}) collective-permute-start(bf16[128,2048]{1,0:T(8,128)(2,1)} %slice.16), channel_id=1, source_target_pairs={{0,4},{1,5},{4,8},{5,9},{8,12},{9,13},{12,14},{13,15},{14,10},{15,... | collective-permute-start | bytes 1572872 | tf_op jit(solution)/shard_map/ppermute | solution.py:55
  146.5 57.1 %collective-permute-start.27 = (bf16[256,4096]{1,0:T(8,128)(2,1)}, bf16[256,4096]{1,0:T(8,128)(2,1)}, u32[]{:S(2)}, u32[]{:S(2)}) collective-permute-start(bf16[256,4096]{1,0:T(8,128)(2,1)} %bitcast.10), channel_id=1, source_target_pairs={{0,16},{16,0},{1,17},{17,1},{2,18},{18,2},{3,19},{19,3},{4,20},{20... | collective-permute-start | bytes 6291464 | tf_op jit(solution)/shard_map/ppermute | solution.py:38
  160.1 24.3 %collective-permute-start.21 = (bf16[2048,256]{1,0:T(8,128)(2,1)}, bf16[2048,256]{1,0:T(8,128)(2,1)}, u32[]{:S(2)}, u32[]{:S(2)}) collective-permute-start(bf16[2048,256]{1,0:T(8,128)(2,1)} %shard_map.71.refs_10_.refs_7_), channel_id=1, source_target_pairs={{0,2},{1,3},{4,0},{5,1},{8,4},{9,5},{12,8},{13,9},{14,12},{15,13},... | collective-permute-start | bytes 3145736 | tf_op jit(solution)/shard_map/ppermute | solution.py:55
  161.7 23.2 %collective-permute-start.22 = (bf16[2048,256]{1,0:T(8,128)(2,1)}, bf16[2048,256]{1,0:T(8,128)(2,1)}, u32[]{:S(2)}, u32[]{:S(2)}) collective-permute-start(bf16[2048,256]{1,0:T(8,128)(2,1)} %shard_map.71.refs_10_.refs_7_), channel_id=1, source_target_pairs={{0,4},{1,5},{4,8},{5,9},{8,12},{9,13},{12,14},{13,15},{14,10},{15,... | collective-permute-start | bytes 3145736 | tf_op jit(solution)/shard_map/ppermute | solution.py:55
  172.0 14.4 %collective-permute-start.17 = (f32[512,512]{1,0:T(8,128)S(1)}, f32[512,512]{1,0:T(8,128)S(1)}, u32[]{:S(2)}, u32[]{:S(2)}) collective-permute-start(f32[512,512]{1,0:T(8,128)S(1)} %get-tuple-element.39), channel_id=1, source_target_pairs={{0,1},{1,0},{2,3},{3,2},{4,5},{5,4},{6,7},{7,6},{8,9},{9,8},{10,11... | collective-permute-start | bytes 3145736 | tf_op jit(solution)/shard_map/ppermute | solution.py:27
  174.7 31.7 %collective-permute-start.20 = (f32[512,512]{1,0:T(8,128)S(1)}, f32[512,512]{1,0:T(8,128)S(1)}, u32[]{:S(2)}, u32[]{:S(2)}) collective-permute-start(f32[512,512]{1,0:T(8,128)S(1)} %get-tuple-element.44), channel_id=1, source_target_pairs={{0,1},{1,0},{2,3},{3,2},{4,5},{5,4},{6,7},{7,6},{8,9},{9,8},{10,11... | collective-permute-start | bytes 3145736 | tf_op jit(solution)/shard_map/ppermute | solution.py:27
  184.4 38.4 %collective-permute-start.23 = (bf16[2048,256]{1,0:T(8,128)(2,1)}, bf16[2048,256]{1,0:T(8,128)(2,1)}, u32[]{:S(2)}, u32[]{:S(2)}) collective-permute-start(bf16[2048,256]{1,0:T(8,128)(2,1)} %collective-permute-done.21.refs_5_.refs_8_), channel_id=1, source_target_pairs={{0,2},{1,3},{4,0},{5,1},{8,4},{9,5},{12,8},{13,9},{14,12},{15,13},... | collective-permute-start | bytes 3145736 | tf_op jit(solution)/shard_map/ppermute | solution.py:55
  184.9 38.0 %collective-permute-start.24 = (bf16[2048,256]{1,0:T(8,128)(2,1)}, bf16[2048,256]{1,0:T(8,128)(2,1)}, u32[]{:S(2)}, u32[]{:S(2)}) collective-permute-start(bf16[2048,256]{1,0:T(8,128)(2,1)} %collective-permute-done.22.refs_6_.refs_9_), channel_id=1, source_target_pairs={{0,4},{1,5},{4,8},{5,9},{8,12},{9,13},{12,14},{13,15},{14,10},{15,... | collective-permute-start | bytes 3145736 | tf_op jit(solution)/shard_map/ppermute | solution.py:55
  202.8 23.4 %collective-permute-start.18 = (bf16[512,512]{1,0:T(8,128)(2,1)}, bf16[512,512]{1,0:T(8,128)(2,1)}, u32[]{:S(2)}, u32[]{:S(2)}) collective-permute-start(bf16[512,512]{1,0:T(8,128)(2,1)} %shard_map.73.refs_2_), channel_id=1, source_target_pairs={{0,16},{16,0},{1,17},{17,1},{2,18},{18,2},{3,19},{19,3},{4,20},{20... | collective-permute-start | bytes 1572872 | tf_op jit(solution)/shard_map/ppermute | solution.py:38
  206.4 31.0 %collective-permute-start.28 = (bf16[256,2048]{1,0:T(8,128)(2,1)}, bf16[256,2048]{1,0:T(8,128)(2,1)S(1)}, u32[]{:S(2)}, u32[]{:S(2)}) collective-permute-start(bf16[256,2048]{1,0:T(8,128)(2,1)} %get-tuple-element.48), channel_id=1, source_target_pairs={{0,1},{1,0},{2,3},{3,2},{4,5},{5,4},{6,7},{7,6},{8,9},{9,8},{10,11... | collective-permute-start | bytes 3145736 | tf_op jit(solution)/shard_map/ppermute | solution.py:27
  222.9 14.5 %collective-permute-start.25 = (bf16[512,512]{1,0:T(8,128)(2,1)}, bf16[512,512]{1,0:T(8,128)(2,1)S(1)}, u32[]{:S(2)}, u32[]{:S(2)}) collective-permute-start(bf16[512,512]{1,0:T(8,128)(2,1)} %shard_map.76), channel_id=1, source_target_pairs={{0,16},{16,0},{1,17},{17,1},{2,18},{18,2},{3,19},{19,3},{4,20},{20... | collective-permute-start | bytes 1572872 | tf_op jit(solution)/shard_map/ppermute | solution.py:38
  224.2 25.5 %collective-permute-start.30 = (bf16[2048,256]{1,0:T(8,128)(2,1)}, bf16[2048,256]{1,0:T(8,128)(2,1)S(1)}, u32[]{:S(2)}, u32[]{:S(2)}) collective-permute-start(bf16[2048,256]{1,0:T(8,128)(2,1)} %collective-permute-done.24.refs_2_.refs_11_), channel_id=1, source_target_pairs={{0,4},{1,5},{4,8},{5,9},{8,12},{9,13},{12,14},{13,15},{14,10},{15,... | collective-permute-start | bytes 3145736 | tf_op jit(solution)/shard_map/ppermute | solution.py:55
  225.9 25.2 %collective-permute-start.29 = (bf16[2048,256]{1,0:T(8,128)(2,1)}, bf16[2048,256]{1,0:T(8,128)(2,1)S(1)}, u32[]{:S(2)}, u32[]{:S(2)}) collective-permute-start(bf16[2048,256]{1,0:T(8,128)(2,1)} %collective-permute-done.23.refs_1_.refs_10_), channel_id=1, source_target_pairs={{0,2},{1,3},{4,0},{5,1},{8,4},{9,5},{12,8},{13,9},{14,12},{15,13},... | collective-permute-start | bytes 3145736 | tf_op jit(solution)/shard_map/ppermute | solution.py:55
  253.6 19.2 %collective-permute-start.31 = (bf16[256,2048]{1,0:T(8,128)(2,1)S(1)}, bf16[256,2048]{1,0:T(8,128)(2,1)S(1)}, u32[]{:S(2)}, u32[]{:S(2)}) collective-permute-start(bf16[256,2048]{1,0:T(8,128)(2,1)S(1)} %get-tuple-element.52), channel_id=1, source_target_pairs={{0,1},{1,0},{2,3},{3,2},{4,5},{5,4},{6,7},{7,6},{8,9},{9,8},{10,11... | collective-permute-start | bytes 3145736 | tf_op jit(solution)/shard_map/ppermute | solution.py:27
  (38 other events, 336.0 us)
Sparse Core Ops, SparseCore 0:
  8.9 35.8 all-gather.3
  66.0 72.3 all-gather.5

commit v8 on v7

--- a/solution.py
+++ b/solution.py
@@ -27,10 +27,14 @@
     return lax.ppermute(value, "fsdp", [(i, i ^ 1) for i in range(count)])
 
 
-def gathered(value):
+def swap_chips(value):
     count = lax.axis_size("fsdp")
-    groups = [list(range(core, count, 2)) for core in range(2)]
-    return lax.all_gather(value, "fsdp", axis=0, tiled=False, axis_index_groups=groups)
+    return lax.ppermute(value, "fsdp", [(i, i ^ 2) for i in range(count)])
+
+
+def two_chips_on(value):
+    count = lax.axis_size("fsdp")
+    return lax.ppermute(value, "fsdp", [(i, i + 4) for i in range(count - 4)])
 
 
 def to_next_section(value):
@@ -170,20 +174,22 @@
     out_ref[...] = in_ref[...]
 
 
-def window_kernel(back, scal_ref, parcels_ref, *refs):
+def window_kernel(scal_ref, four_ref, two_ref, own_ref, crossed_ref, *refs):
     kt_refs, v_refs, lo_ref = refs[:2], refs[2:4], refs[4]
-    chip = scal_ref[1]
-    count = parcels_ref.shape[1] - MARK_ROWS
+    odd = scal_ref[1]
+    length = own_ref.shape[0]
+    count = length - MARK_ROWS
     half = count // 2
+    second = pl.multiple_of(odd * length, MARK_ROWS)
+    fourth = pl.multiple_of((1 - odd) * length, MARK_ROWS)
+    places = [(four_ref, 0), (crossed_ref, second), (two_ref, 0), (crossed_ref, fourth), (own_ref, 0)]
     lane = lax.broadcasted_iota(jnp.int32, (count, 128), 1)
     blank = jnp.zeros((HEAD_SIZE, count), jnp.bfloat16)
     marks = []
-    for i in range(back + 1):
-        source = chip - back + i
-        ref = parcels_ref.at[jnp.maximum(source, 0)]
+    for i, (ref, first) in enumerate(places):
         at = slice(i * count, (i + 1) * count)
-        keys = ref[:count, 0:128].astype(jnp.float32).T.astype(jnp.bfloat16)
-        values = ref[:count, 128:256].astype(jnp.float32)
+        keys = ref[pl.ds(first, count), 0:128].astype(jnp.float32).T.astype(jnp.bfloat16)
+        values = ref[pl.ds(first, count), 128:256].astype(jnp.float32)
         turned = pltpu.roll(values, HEAD_SIZE, 1)
         for g in range(2):
             head = keys[g * HEAD_SIZE:(g + 1) * HEAD_SIZE]
@@ -194,7 +200,7 @@
             low, high = (values, turned) if g == 0 else (turned, values)
             v_refs[g][0, at, :] = jnp.where(lane < HEAD_SIZE, low, 0.0).astype(jnp.bfloat16)
             v_refs[g][1, at, :] = jnp.where(lane < HEAD_SIZE, 0.0, high).astype(jnp.bfloat16)
-        found = jnp.where(source >= 0, ref[count:, :].astype(jnp.float32), 0.0)
+        found = ref[pl.ds(first + count, MARK_ROWS), :].astype(jnp.float32)
         marks += [found[0:1, :], found[1:2, :]]
     across = lax.broadcasted_iota(jnp.int32, (half, half), 1)
     down = lax.broadcasted_iota(jnp.int32, (half, half), 0)
@@ -358,12 +364,12 @@
     table = []
     for i in range(2 * chips):
         place = order.index(i // 2)
-        table.append([i % 2, i // 2] + [order[(place + d) % chips] for d in range(chips)])
+        table.append([i % 2, i // 2 % 2] + [order[(place + d) % chips] for d in range(chips)])
     scalars = lax.dynamic_index_in_dim(jnp.array(table, jnp.int32), device, 0, keepdims=False)
 
     keyval_pieces = around(keyval_weight[0], halved=False)
     out_shard = from_section_before(out_weight[0])
-    kv_steps = [keyval_pieces[d][0][1] for d in (3, chips - 3)]
+    kv_steps = [keyval_pieces[d][0][1] for d in (3, chips - 3, chips // 2)]
     query_shard, = run(
         copy_kernel, [(query_weight.shape[1:], jnp.bfloat16)], scalars, [query_weight[0]],
         waits=kv_steps,
@@ -383,13 +389,17 @@
         parcel_kernel, [((2 * rows + MARK_ROWS, 256), jnp.bfloat16)], scalars,
         [segment_ids, kept, swap_cores(sent)],
     )
-    back = -(-LOOKBACK_SPAN // (2 * rows))
-    window = (back + 1) * 2 * rows
+    steps = [[query_pieces[d][0][1] for d in (step, chips - step)] for step in range(1, 4)]
+    back_two = after(two_chips_on(parcel), *steps[0])
+    back_four = after(two_chips_on(back_two), *steps[1])
+    even = device // 2 % 2 == 0
+    crossed = swap_chips(jnp.concatenate([jnp.where(even, parcel, back_four), back_two], axis=0))
+    window = 5 * 2 * rows
     *heads, lowest = run(
-        functools.partial(window_kernel, back),
+        window_kernel,
         [((2, 128, window), jnp.bfloat16)] * 2 + [((2, window, 128), jnp.bfloat16)] * 2
         + [((2 * rows, 128), jnp.int32)],
-        scalars, [gathered(parcel)],
+        scalars, [back_four, back_two, parcel, crossed], waits=steps[2],
     )
 
     def query_sums(distances, g, waits, before=()):

time: 282 us -> 267 us (0.947)
  waiting for transfers between devices: 153 us -> 126 us
  starting transfers between devices: 30.7 us -> 40.9 us
    ppermute x23, waiting for transfers between devices: 136 us -> 90.9 us  [along_ring(): return lax.ppermute(value, 'fsdp', pairs)]
    ppermute x0 -> x3, waiting for transfers between devices: none -> 18.6 us  [the longest x1 18.6 us: swap_chips(): return lax.ppermute(value, 'fsdp', [(i, i ^ 2) for i in range(count)])]
    ppermute x0 -> x3, starting transfers between devices: none -> 10.9 us  [the longest x2 9.12 us: two_chips_on(): return lax.ppermute(value, 'fsdp', [(i, i + 4) for i in range(count - 4)])]
    unnamed x50 -> x66, local copies, waits for them, and re-layouts: 14.5 us -> 13.4 us
  transfers between devices with their start and end apart: 37 -> 39, of which waited for: 16 -> 15; matrix products, arithmetic and copies ran while one was open for 2% -> 2% of each run, Pallas kernels for 21% -> 23%
where the time goes in v8:
time: 267 us; the launch traced here: 266 us
  waiting for transfers between devices  126 us (47%)
  Pallas kernels  66.5 us (25%)
  starting transfers between devices  40.9 us (15%)
  local copies, waits for them, and re-layouts  18.2 us (7%)
  between operations  13.8 us (5%)
    ppermute x23, waiting for transfers between devices, along_ring(): return lax.ppermute(value, 'fsdp', pairs)  90.9 us
    pallas_call x14, Pallas kernels, run(): pl.pallas_call(only, in_specs=[pl.BlockSpec(memory_space=pltpu.SMEM)] + [...  34.5 us
    pallas_call x2, Pallas kernels, attention(): pl.pallas_call(only, grid=(rows // TILE,), in_specs=[pl.BlockSpec((TILE,...  32 us
    ppermute x23, starting transfers between devices, along_ring(): return lax.ppermute(value, 'fsdp', pairs)  25.5 us
    ppermute x1, waiting for transfers between devices, swap_chips(): return lax.ppermute(value, 'fsdp', [(i, i ^ 2) for i in range(count)])  18.6 us
    unnamed x66, local copies, waits for them, and re-layouts  13.4 us
    ppermute x3, waiting for transfers between devices, to_next_section(): lax.ppermute(value, 'section', [(i, (i + 1) % count) for i in range(count)])  11 us
    ppermute x2, starting transfers between devices, two_chips_on(): return lax.ppermute(value, 'fsdp', [(i, i + 4) for i in range(count - 4)])  9.12 us
  transfers between devices with their start and end apart: 39, of which 15 were waited for; matrix products, arithmetic and copies ran while one was open for 2% of the time, Pallas kernels for 23%

profile of v8, /device:TPU:0, one launch (start us, length us, event | category | flops | bytes accessed | tf_op | source)
XLA Modules:
  0.0 266.2 jit_solution(410298121997787426)
XLA Ops:
  6.5 3.0 %collective-permute-start.4 = (bf16[256,512]{1,0:T(8,128)(2,1)}, bf16[256,512]{1,0:T(8,128)(2,1)S(1)}, u32[]{:S(2)}, u32[]{:S(2)}) collective-permute-start(bf16[256,512]{1,0:T(8,128)(2,1)} %bitcast.11), channel_id=1, source_target_pairs={{0,4},{1,5},{4,8},{5,9},{8,12},{9,13},{12,14},{13,15},{14,10},{15,... | collective-permute-start | bytes 786440 | tf_op jit(solution)/shard_map/ppermute | solution.py:59
  9.6 6.5 %collective-permute-done.4.refs_11_ = bf16[256,512]{1,0:T(8,128)(2,1)S(1)} collective-permute-done((bf16[256,512]{1,0:T(8,128)(2,1)}, bf16[256,512]{1,0:T(8,128)(2,1)S(1)}, u32[]{:S(2)}, u32[]{:S(2)}) %collective-permute-start.4) | collective-permute-done | bytes 262176 | tf_op jit(solution)/shard_map/ppermute | solution.py:59
  19.5 4.0 %collective-permute-done.5.refs_10_ = bf16[256,512]{1,0:T(8,128)(2,1)S(1)} collective-permute-done((bf16[256,512]{1,0:T(8,128)(2,1)S(1)}, bf16[256,512]{1,0:T(8,128)(2,1)S(1)}, u32[]{:S(2)}, u32[]{:S(2)}) %collective-permute-start.5) | collective-permute-done | bytes 262176 | tf_op jit(solution)/shard_map/ppermute | solution.py:59
  26.2 3.8 %collective-permute-done.6.refs_9_.refs_3_ = bf16[256,512]{1,0:T(8,128)(2,1)S(1)} collective-permute-done((bf16[256,512]{1,0:T(8,128)(2,1)S(1)}, bf16[256,512]{1,0:T(8,128)(2,1)S(1)}, u32[]{:S(2)}, u32[]{:S(2)}) %collective-permute-start.6) | collective-permute-done | bytes 262176 | tf_op jit(solution)/shard_map/ppermute | solution.py:59
  32.5 3.9 %collective-permute-done.7.refs_8_.refs_4_ = bf16[256,512]{1,0:T(8,128)(2,1)S(1)} collective-permute-done((bf16[256,512]{1,0:T(8,128)(2,1)S(1)}, bf16[256,512]{1,0:T(8,128)(2,1)S(1)}, u32[]{:S(2)}, u32[]{:S(2)}) %collective-permute-start.7) | collective-permute-done | bytes 262176 | tf_op jit(solution)/shard_map/ppermute | solution.py:59
  40.5 21.1 %collective-permute-done.11.refs_2_.refs_5_ = bf16[256,2048]{1,0:T(8,128)(2,1)} collective-permute-done((bf16[256,2048]{1,0:T(8,128)(2,1)S(1)}, bf16[256,2048]{1,0:T(8,128)(2,1)}, u32[]{:S(2)}, u32[]{:S(2)}) %collective-permute-start.11) | collective-permute-done | bytes 1048608 | tf_op jit(solution)/shard_map/ppermute | solution.py:59
  66.7 18.2 %collective-permute-done.14.refs_2_.refs_7_ = bf16[256,2048]{1,0:T(8,128)(2,1)} collective-permute-done((bf16[256,2048]{1,0:T(8,128)(2,1)}, bf16[256,2048]{1,0:T(8,128)(2,1)}, u32[]{:S(2)}, u32[]{:S(2)}) %collective-permute-start.14) | collective-permute-done | bytes 1048608 | tf_op jit(solution)/shard_map/ppermute | solution.py:59
  91.6 4.3 %collective-permute-start.9 = (bf16[528,256]{1,0:T(8,128)(2,1)S(1)}, bf16[528,256]{1,0:T(8,128)(2,1)}, u32[]{:S(2)}, u32[]{:S(2)}) collective-permute-start(bf16[528,256]{1,0:T(8,128)(2,1)S(1)} %shard_map.66.refs_3_.refs_8_), channel_id=1, source_target_pairs={{0,4},{1,5},{2,6},{3,7},{4,8},{5,9},{6,10},{7,11},{8,12},{9,13},{1... | collective-permute-start | bytes 811016 | tf_op jit(solution)/shard_map/ppermute | solution.py:37
  95.9 14.7 %collective-permute-done.17.refs_6_.refs_4_ = bf16[256,2048]{1,0:T(8,128)(2,1)S(1)} collective-permute-done((bf16[256,2048]{1,0:T(8,128)(2,1)}, bf16[256,2048]{1,0:T(8,128)(2,1)S(1)}, u32[]{:S(2)}, u32[]{:S(2)}) %collective-permute-start.17) | collective-permute-done | bytes 1048608 | tf_op jit(solution)/shard_map/ppermute | solution.py:59
  116.7 4.8 %collective-permute-start.12 = (bf16[528,256]{1,0:T(8,128)(2,1)}, bf16[528,256]{1,0:T(8,128)(2,1)}, u32[]{:S(2)}, u32[]{:S(2)}) collective-permute-start(bf16[528,256]{1,0:T(8,128)(2,1)} %shard_map.68.refs_2_), channel_id=1, source_target_pairs={{0,4},{1,5},{2,6},{3,7},{4,8},{5,9},{6,10},{7,11},{8,12},{9,13},{1... | collective-permute-start | bytes 811016 | tf_op jit(solution)/shard_map/ppermute | solution.py:37
  125.3 3.7 %shard_map.72 = (f32[512,512]{1,0:T(8,128)S(1)}, f32[512,512]{1,0:T(8,128)S(1)}) custom-call(s32[10]{0:T(128)S(1)} %dynamic-slice_bitcast_fusion.1.refs_0_, bf16[256,2048]{1,0:T(8,128)(2,1)S(1)} %get-tuple-element.30.refs_2_.refs_1_, bf16[256,2048]{1,0:T(8,128)(2,1)S(1)} %collective-permute-done.refs_3_.refs_2_, bf16[256,2048]{1,0:T(8,128)(2,1)S(1)} %shard_map.67.refs_3_, ...), custom_call_target="tpu_custom_call" | custom-call | flops 1000000 | bytes 100000 | tf_op jit(solution)/shard_map/pallas_call | solution.py:69
  130.0 4.1 %shard_map.71 = (f32[512,512]{1,0:T(8,128)S(1)}, f32[512,512]{1,0:T(8,128)S(1)}) custom-call(s32[10]{0:T(128)S(1)} %dynamic-slice_bitcast_fusion.1.refs_0_, bf16[256,2048]{1,0:T(8,128)(2,1)S(1)} %get-tuple-element.30.refs_2_.refs_1_, bf16[256,2048]{1,0:T(8,128)(2,1)S(1)} %collective-permute-done.refs_3_.refs_2_, bf16[256,2048]{1,0:T(8,128)(2,1)S(1)} %shard_map.67.refs_3_, ...), custom_call_target="tpu_custom_call" | custom-call | flops 1000000 | bytes 100000 | tf_op jit(solution)/shard_map/pallas_call | solution.py:69
  141.1 18.6 %collective-permute-done.15.refs_4_ = bf16[1056,256]{1,0:T(8,128)(2,1)S(1)} collective-permute-done((bf16[1056,256]{1,0:T(8,128)(2,1)S(1)}, bf16[1056,256]{1,0:T(8,128)(2,1)S(1)}, u32[]{:S(2)}, u32[]{:S(2)}) %collective-permute-start.15) | collective-permute-done | bytes 540704 | tf_op jit(solution)/shard_map/ppermute | solution.py:32
  161.0 2.4 shard_map.70
  164.6 2.6 shard_map.74
  167.4 2.5 shard_map.76
  172.4 16.3 %shard_map.75.refs_2_ = bf16[512,512]{1,0:T(8,128)(2,1)} custom-call(s32[512,128]{1,0:T(8,128)S(1)} %get-tuple-element.34.refs_9_.refs_0_, f32[512,512]{1,0:T(8,128)S(1)} %get-tuple-element.38.refs_1_, f32[512,512]{1,0:T(8,128)S(1)} %collective-permute-done.20.refs_2_, bf16[2,128,2560]{2,1,0:T(8,128)(2,1)S(1)} %get-tuple-element.40.refs_3_, ...), custom_call_target="tpu_custom_call" | custom-call | flops 1000000 | bytes 100000 | tf_op jit(solution)/shard_map/pallas_call | solution.py:292
  189.3 2.8 %shard_map.79 = (bf16[256,2048]{1,0:T(8,128)(2,1)S(1)}, bf16[256,2048]{1,0:T(8,128)(2,1)}) custom-call(s32[10]{0:T(128)S(1)} %dynamic-slice_bitcast_fusion.1.refs_0_, bf16[256,4096]{1,0:T(8,128)(2,1)} %collective-permute-done.30.refs_1_, bf16[512,512]{1,0:T(8,128)(2,1)} %shard_map.75.refs_2_), custom_call_target="tpu_custom_call" | custom-call | flops 1000000 | bytes 100000 | tf_op jit(solution)/shard_map/pallas_call | solution.py:69
  192.2 15.6 %shard_map.77.refs_0_ = bf16[512,512]{1,0:T(8,128)(2,1)S(1)} custom-call(s32[512,128]{1,0:T(8,128)S(1)} %get-tuple-element.34.refs_9_.refs_0_, f32[512,512]{1,0:T(8,128)S(1)} %get-tuple-element.43.refs_1_, f32[512,512]{1,0:T(8,128)S(1)} %collective-permute-done.23.refs_2_, bf16[2,128,2560]{2,1,0:T(8,128)(2,1)S(1)} %get-tuple-element.45.refs_3_, ...), custom_call_target="tpu_custom_call" | custom-call | flops 1000000 | bytes 100000 | tf_op jit(solution)/shard_map/pallas_call | solution.py:292
  212.2 11.0 %collective-permute-done.28.refs_3_ = bf16[512,512]{1,0:T(8,128)(2,1)S(1)} collective-permute-done((bf16[512,512]{1,0:T(8,128)(2,1)}, bf16[512,512]{1,0:T(8,128)(2,1)S(1)}, u32[]{:S(2)}, u32[]{:S(2)}) %collective-permute-start.28) | collective-permute-done | bytes 524320 | tf_op jit(solution)/shard_map/ppermute | solution.py:42
  225.1 5.4 %shard_map.80 = (bf16[256,2048]{1,0:T(8,128)(2,1)S(1)}, bf16[256,2048]{1,0:T(8,128)(2,1)S(1)}) custom-call(s32[10]{0:T(128)S(1)} %dynamic-slice_bitcast_fusion.1.refs_0_, bf16[512,512]{1,0:T(8,128)(2,1)} %collective-permute-done.21.refs_1_, bf16[512,512]{1,0:T(8,128)(2,1)S(1)} %collective-permute-done.22.refs_2_, ...), custom_call_target="tpu_custom_call" | custom-call | flops 1000000 | bytes 100000 | tf_op jit(solution)/shard_map/pallas_call | solution.py:69
  230.5 5.2 %collective-permute-done.33.refs_8_ = bf16[2048,256]{1,0:T(8,128)(2,1)S(1)} collective-permute-done((bf16[2048,256]{1,0:T(8,128)(2,1)}, bf16[2048,256]{1,0:T(8,128)(2,1)S(1)}, u32[]{:S(2)}, u32[]{:S(2)}) %collective-permute-start.33) | collective-permute-done | bytes 1048608 | tf_op jit(solution)/shard_map/ppermute | solution.py:59
  235.6 2.5 shard_map.81
  240.4 12.2 %collective-permute-done.35.refs_7_ = bf16[1024,256]{1,0:T(8,128)(2,1)S(1)} collective-permute-done((bf16[1024,256]{1,0:T(8,128)(2,1)S(1)}, bf16[1024,256]{1,0:T(8,128)(2,1)S(1)}, u32[]{:S(2)}, u32[]{:S(2)}) %collective-permute-start.35) | collective-permute-done | bytes 524320 | tf_op jit(solution)/shard_map/ppermute | solution.py:59
  (149 shorter events, 63.0 us)
Async XLA Ops:
  6.5 116.4 %all-gather.2.cloned.1.call-start = ((), (), s32[]{:S(2)}) async-start(), calls=%async_computation | async-start | bytes 3145728 | tf_op jit(solution)/shard_map/all_gather | solution.py:48
  38.4 23.2 %collective-permute-start.11 = (bf16[256,2048]{1,0:T(8,128)(2,1)S(1)}, bf16[256,2048]{1,0:T(8,128)(2,1)}, u32[]{:S(2)}, u32[]{:S(2)}) collective-permute-start(bf16[256,2048]{1,0:T(8,128)(2,1)S(1)} %shard_map.67.refs_3_), channel_id=1, source_target_pairs={{0,4},{1,5},{4,8},{5,9},{8,12},{9,13},{12,14},{13,15},{14,10},{15,... | collective-permute-start | bytes 3145736 | tf_op jit(solution)/shard_map/ppermute | solution.py:59
  40.2 23.1 %collective-permute-start.10 = (bf16[256,2048]{1,0:T(8,128)(2,1)S(1)}, bf16[256,2048]{1,0:T(8,128)(2,1)}, u32[]{:S(2)}, u32[]{:S(2)}) collective-permute-start(bf16[256,2048]{1,0:T(8,128)(2,1)S(1)} %shard_map.67.refs_3_), channel_id=1, source_target_pairs={{0,2},{1,3},{4,0},{5,1},{8,4},{9,5},{12,8},{13,9},{14,12},{15,13},... | collective-permute-start | bytes 3145736 | tf_op jit(solution)/shard_map/ppermute | solution.py:59
  61.6 23.3 %collective-permute-start.14 = (bf16[256,2048]{1,0:T(8,128)(2,1)}, bf16[256,2048]{1,0:T(8,128)(2,1)}, u32[]{:S(2)}, u32[]{:S(2)}) collective-permute-start(bf16[256,2048]{1,0:T(8,128)(2,1)} %collective-permute-done.11.refs_2_.refs_5_), channel_id=1, source_target_pairs={{0,4},{1,5},{4,8},{5,9},{8,12},{9,13},{12,14},{13,15},{14,10},{15,... | collective-permute-start | bytes 3145736 | tf_op jit(solution)/shard_map/ppermute | solution.py:59
  63.3 23.3 %collective-permute-start.13 = (bf16[256,2048]{1,0:T(8,128)(2,1)}, bf16[256,2048]{1,0:T(8,128)(2,1)}, u32[]{:S(2)}, u32[]{:S(2)}) collective-permute-start(bf16[256,2048]{1,0:T(8,128)(2,1)} %collective-permute-done.10.refs_1_.refs_4_), channel_id=1, source_target_pairs={{0,2},{1,3},{4,0},{5,1},{8,4},{9,5},{12,8},{13,9},{14,12},{15,13},... | collective-permute-start | bytes 3145736 | tf_op jit(solution)/shard_map/ppermute | solution.py:59
  66.7 20.3 %collective-permute-start = (bf16[256,2048]{1,0:T(8,128)(2,1)S(1)}, bf16[256,2048]{1,0:T(8,128)(2,1)S(1)}, u32[]{:S(2)}, u32[]{:S(2)}) collective-permute-start(bf16[256,2048]{1,0:T(8,128)(2,1)S(1)} %get-tuple-element.31), channel_id=1, source_target_pairs={{0,1},{1,0},{2,3},{3,2},{4,5},{5,4},{6,7},{7,6},{8,9},{9,8},{10,11... | collective-permute-start | bytes 3145736 | tf_op jit(solution)/shard_map/ppermute | solution.py:27
  84.9 25.7 %collective-permute-start.17 = (bf16[256,2048]{1,0:T(8,128)(2,1)}, bf16[256,2048]{1,0:T(8,128)(2,1)S(1)}, u32[]{:S(2)}, u32[]{:S(2)}) collective-permute-start(bf16[256,2048]{1,0:T(8,128)(2,1)} %collective-permute-done.14.refs_2_.refs_7_), channel_id=1, source_target_pairs={{0,4},{1,5},{4,8},{5,9},{8,12},{9,13},{12,14},{13,15},{14,10},{15,... | collective-permute-start | bytes 3145736 | tf_op jit(solution)/shard_map/ppermute | solution.py:59
  86.7 28.2 %collective-permute-start.16 = (bf16[256,2048]{1,0:T(8,128)(2,1)}, bf16[256,2048]{1,0:T(8,128)(2,1)S(1)}, u32[]{:S(2)}, u32[]{:S(2)}) collective-permute-start(bf16[256,2048]{1,0:T(8,128)(2,1)} %collective-permute-done.13.refs_1_.refs_6_), channel_id=1, source_target_pairs={{0,2},{1,3},{4,0},{5,1},{8,4},{9,5},{12,8},{13,9},{14,12},{15,13},... | collective-permute-start | bytes 3145736 | tf_op jit(solution)/shard_map/ppermute | solution.py:59
  91.6 25.1 %collective-permute-start.9 = (bf16[528,256]{1,0:T(8,128)(2,1)S(1)}, bf16[528,256]{1,0:T(8,128)(2,1)}, u32[]{:S(2)}, u32[]{:S(2)}) collective-permute-start(bf16[528,256]{1,0:T(8,128)(2,1)S(1)} %shard_map.66.refs_3_.refs_8_), channel_id=1, source_target_pairs={{0,4},{1,5},{2,6},{3,7},{4,8},{5,9},{6,10},{7,11},{8,12},{9,13},{1... | collective-permute-start | bytes 811016 | tf_op jit(solution)/shard_map/ppermute | solution.py:37
  112.5 23.7 %collective-permute-start.18 = (bf16[128,2048]{1,0:T(8,128)(2,1)}, bf16[128,2048]{1,0:T(8,128)(2,1)}, u32[]{:S(2)}, u32[]{:S(2)}) collective-permute-start(bf16[128,2048]{1,0:T(8,128)(2,1)} %slice.16), channel_id=1, source_target_pairs={{0,4},{1,5},{4,8},{5,9},{8,12},{9,13},{12,14},{13,15},{14,10},{15,... | collective-permute-start | bytes 1572872 | tf_op jit(solution)/shard_map/ppermute | solution.py:59
  116.7 19.5 %collective-permute-start.19 = (bf16[128,2048]{1,0:T(8,128)(2,1)}, bf16[128,2048]{1,0:T(8,128)(2,1)}, u32[]{:S(2)}, u32[]{:S(2)}) collective-permute-start(bf16[128,2048]{1,0:T(8,128)(2,1)} %slice.17), channel_id=1, source_target_pairs={{0,2},{1,3},{4,0},{5,1},{8,4},{9,5},{12,8},{13,9},{14,12},{15,13},... | collective-permute-start | bytes 1572872 | tf_op jit(solution)/shard_map/ppermute | solution.py:59
  116.7 21.5 %collective-permute-start.12 = (bf16[528,256]{1,0:T(8,128)(2,1)}, bf16[528,256]{1,0:T(8,128)(2,1)}, u32[]{:S(2)}, u32[]{:S(2)}) collective-permute-start(bf16[528,256]{1,0:T(8,128)(2,1)} %shard_map.68.refs_2_), channel_id=1, source_target_pairs={{0,4},{1,5},{2,6},{3,7},{4,8},{5,9},{6,10},{7,11},{8,12},{9,13},{1... | collective-permute-start | bytes 811016 | tf_op jit(solution)/shard_map/ppermute | solution.py:37
  121.5 67.9 %collective-permute-start.30 = (bf16[256,4096]{1,0:T(8,128)(2,1)}, bf16[256,4096]{1,0:T(8,128)(2,1)}, u32[]{:S(2)}, u32[]{:S(2)}) collective-permute-start(bf16[256,4096]{1,0:T(8,128)(2,1)} %bitcast.8), channel_id=1, source_target_pairs={{0,16},{16,0},{1,17},{17,1},{2,18},{18,2},{3,19},{19,3},{4,20},{20... | collective-permute-start | bytes 6291464 | tf_op jit(solution)/shard_map/ppermute | solution.py:42
  136.2 34.3 %collective-permute-start.24 = (bf16[2048,256]{1,0:T(8,128)(2,1)}, bf16[2048,256]{1,0:T(8,128)(2,1)}, u32[]{:S(2)}, u32[]{:S(2)}) collective-permute-start(bf16[2048,256]{1,0:T(8,128)(2,1)} %shard_map.73.refs_10_.refs_7_), channel_id=1, source_target_pairs={{0,2},{1,3},{4,0},{5,1},{8,4},{9,5},{12,8},{13,9},{14,12},{15,13},... | collective-permute-start | bytes 3145736 | tf_op jit(solution)/shard_map/ppermute | solution.py:59
  137.0 33.8 %collective-permute-start.25 = (bf16[2048,256]{1,0:T(8,128)(2,1)}, bf16[2048,256]{1,0:T(8,128)(2,1)}, u32[]{:S(2)}, u32[]{:S(2)}) collective-permute-start(bf16[2048,256]{1,0:T(8,128)(2,1)} %shard_map.73.refs_10_.refs_7_), channel_id=1, source_target_pairs={{0,4},{1,5},{4,8},{5,9},{8,12},{9,13},{12,14},{13,15},{14,10},{15,... | collective-permute-start | bytes 3145736 | tf_op jit(solution)/shard_map/ppermute | solution.py:59
  139.3 20.4 %collective-permute-start.15 = (bf16[1056,256]{1,0:T(8,128)(2,1)S(1)}, bf16[1056,256]{1,0:T(8,128)(2,1)S(1)}, u32[]{:S(2)}, u32[]{:S(2)}) collective-permute-start(bf16[1056,256]{1,0:T(8,128)(2,1)S(1)} %pad_maximum_fusion), channel_id=1, source_target_pairs={{0,2},{1,3},{2,0},{3,1},{4,6},{5,7},{6,4},{7,5},{8,10},{9,11},{10,... | collective-permute-start | bytes 1622024 | tf_op jit(solution)/shard_map/ppermute | solution.py:32
  169.9 22.3 %collective-permute-start.23 = (f32[512,512]{1,0:T(8,128)S(1)}, f32[512,512]{1,0:T(8,128)S(1)}, u32[]{:S(2)}, u32[]{:S(2)}) collective-permute-start(f32[512,512]{1,0:T(8,128)S(1)} %get-tuple-element.44), channel_id=1, source_target_pairs={{0,1},{1,0},{2,3},{3,2},{4,5},{5,4},{6,7},{7,6},{8,9},{9,8},{10,11... | collective-permute-start | bytes 3145736 | tf_op jit(solution)/shard_map/ppermute | solution.py:27
  170.4 38.2 %collective-permute-start.26 = (bf16[2048,256]{1,0:T(8,128)(2,1)}, bf16[2048,256]{1,0:T(8,128)(2,1)}, u32[]{:S(2)}, u32[]{:S(2)}) collective-permute-start(bf16[2048,256]{1,0:T(8,128)(2,1)} %collective-permute-done.24.refs_5_.refs_8_), channel_id=1, source_target_pairs={{0,2},{1,3},{4,0},{5,1},{8,4},{9,5},{12,8},{13,9},{14,12},{15,13},... | collective-permute-start | bytes 3145736 | tf_op jit(solution)/shard_map/ppermute | solution.py:59
  170.8 37.9 %collective-permute-start.27 = (bf16[2048,256]{1,0:T(8,128)(2,1)}, bf16[2048,256]{1,0:T(8,128)(2,1)}, u32[]{:S(2)}, u32[]{:S(2)}) collective-permute-start(bf16[2048,256]{1,0:T(8,128)(2,1)} %collective-permute-done.25.refs_6_.refs_9_), channel_id=1, source_target_pairs={{0,4},{1,5},{4,8},{5,9},{8,12},{9,13},{12,14},{13,15},{14,10},{15,... | collective-permute-start | bytes 3145736 | tf_op jit(solution)/shard_map/ppermute | solution.py:59
  188.8 23.4 %collective-permute-start.21 = (bf16[512,512]{1,0:T(8,128)(2,1)}, bf16[512,512]{1,0:T(8,128)(2,1)}, u32[]{:S(2)}, u32[]{:S(2)}) collective-permute-start(bf16[512,512]{1,0:T(8,128)(2,1)} %shard_map.75.refs_2_), channel_id=1, source_target_pairs={{0,16},{16,0},{1,17},{17,1},{2,18},{18,2},{3,19},{19,3},{4,20},{20... | collective-permute-start | bytes 1572872 | tf_op jit(solution)/shard_map/ppermute | solution.py:42
  192.2 31.0 %collective-permute-start.31 = (bf16[256,2048]{1,0:T(8,128)(2,1)}, bf16[256,2048]{1,0:T(8,128)(2,1)S(1)}, u32[]{:S(2)}, u32[]{:S(2)}) collective-permute-start(bf16[256,2048]{1,0:T(8,128)(2,1)} %get-tuple-element.48), channel_id=1, source_target_pairs={{0,1},{1,0},{2,3},{3,2},{4,5},{5,4},{6,7},{7,6},{8,9},{9,8},{10,11... | collective-permute-start | bytes 3145736 | tf_op jit(solution)/shard_map/ppermute | solution.py:27
  210.1 25.5 %collective-permute-start.33 = (bf16[2048,256]{1,0:T(8,128)(2,1)}, bf16[2048,256]{1,0:T(8,128)(2,1)S(1)}, u32[]{:S(2)}, u32[]{:S(2)}) collective-permute-start(bf16[2048,256]{1,0:T(8,128)(2,1)} %collective-permute-done.27.refs_2_.refs_11_), channel_id=1, source_target_pairs={{0,4},{1,5},{4,8},{5,9},{8,12},{9,13},{12,14},{13,15},{14,10},{15,... | collective-permute-start | bytes 3145736 | tf_op jit(solution)/shard_map/ppermute | solution.py:59
  210.2 25.4 %collective-permute-start.32 = (bf16[2048,256]{1,0:T(8,128)(2,1)}, bf16[2048,256]{1,0:T(8,128)(2,1)S(1)}, u32[]{:S(2)}, u32[]{:S(2)}) collective-permute-start(bf16[2048,256]{1,0:T(8,128)(2,1)} %collective-permute-done.26.refs_1_.refs_10_), channel_id=1, source_target_pairs={{0,2},{1,3},{4,0},{5,1},{8,4},{9,5},{12,8},{13,9},{14,12},{15,13},... | collective-permute-start | bytes 3145736 | tf_op jit(solution)/shard_map/ppermute | solution.py:59
  238.1 19.0 %collective-permute-start.34 = (bf16[256,2048]{1,0:T(8,128)(2,1)S(1)}, bf16[256,2048]{1,0:T(8,128)(2,1)S(1)}, u32[]{:S(2)}, u32[]{:S(2)}) collective-permute-start(bf16[256,2048]{1,0:T(8,128)(2,1)S(1)} %get-tuple-element.52), channel_id=1, source_target_pairs={{0,1},{1,0},{2,3},{3,2},{4,5},{5,4},{6,7},{7,6},{8,9},{9,8},{10,11... | collective-permute-start | bytes 3145736 | tf_op jit(solution)/shard_map/ppermute | solution.py:27
  (48 other events, 416.7 us)
Sparse Core Ops, SparseCore 0:
  63.8 34.5 all-gather.1
